TPU v7x, 32 devices: a whole 2x2x4 slice. The times are simulated.
32 devices in a mesh: dp: 2 (over x), ctx: 16 (over z, y, core).
Axes of the slice: x: 2, y: 2, z: 4, core: 2. Of those that a mesh axis runs over, the one named last changes fastest.
Arguments:
- tokens: bfloat16 [2, 2, 1024, 1536], P(None, 'dp', 'ctx'), may hold values from -6 to 6
- lengths: int32 [2, 2], P(None, 'dp'), may hold values from 256 to 1024, as said below
- routes: int32 [2, 2, 1024, 2], P(None, 'dp', 'ctx'), may hold values from 0 to 3, all different within a row
- cotangent: bfloat16 [2, 2, 1024, 1536], P(None, 'dp', 'ctx'), may hold values from -6 to 6
- attn_gain: bfloat16 [1536], P(('dp', 'ctx')), may hold values from 0.5 to 1.5
- qkv_weight: bfloat16 [1536, 2560], P(('dp', 'ctx')), may hold values from -0.15625 to 0.15625
- out_weight: bfloat16 [1536, 1536], P(None, ('dp', 'ctx')), may hold values from -1.75 to 1.75
- moe_gain: bfloat16 [1536], P(('dp', 'ctx')), may hold values from 0.5 to 1.5
- router: bfloat16 [1536, 4], P(('dp', 'ctx')), may hold values from -0.109375 to 0.109375
- gateup_weight: bfloat16 [4, 1536, 2048], P(None, ('dp', 'ctx')), may hold values from -0.15625 to 0.15625
- down_weight: bfloat16 [4, 1024, 1536], P(None, None, ('dp', 'ctx')), may hold values from -0.1875 to 0.1875
Outputs:
- output: bfloat16 [2, 2, 1024, 1536], P(None, 'dp', 'ctx')
- grad_tokens: bfloat16 [2, 2, 1024, 1536], P(None, 'dp', 'ctx')
- grad_attn_gain: float32 [1536], P(('dp', 'ctx'))
- grad_qkv_weight: float32 [1536, 2560], P(('dp', 'ctx'))
- grad_out_weight: float32 [1536, 1536], P(None, ('dp', 'ctx'))
- grad_moe_gain: float32 [1536], P(('dp', 'ctx'))
- grad_router: float32 [1536, 4], P(('dp', 'ctx'))
- grad_gateup_weight: float32 [4, 1536, 2048], P(None, ('dp', 'ctx'))
- grad_down_weight: float32 [4, 1024, 1536], P(None, None, ('dp', 'ctx'))
Inputs may be any that keep to these rules, and one draw needn't show every extreme that they name: `lengths`: in every draw some sequence fills all 1024 slots. `routes`: each slot names 2 different experts.
All inputs are finite; a program needn't handle non-finite values.
Results may differ from a plain program's by a relative error of at most 0.014.
Values may be sent and summed in bfloat16 or wider, within the bound.
No kernel may reach another device: no remote copies, remote signals or barrier semaphores. Data moves between devices by JAX's collectives and lax.ppermute only.
A program may use at most 448 MiB of HBM per device.

v0:
```python
import jax
import jax.numpy as jnp
from jax import lax
from jax.sharding import PartitionSpec as P

D = 1536
H = 24
KVH = 8
HD = 64
FF = 1024
E = 4
MB = 2
QW = 1536
KW = 512


def rms_scale(values, gain):
    return values * lax.rsqrt(jnp.mean(values * values, axis=-1, keepdims=True) + 1e-05) * gain


def gate_mix(logits, chosen):
    picked = jnp.sum(chosen * logits[:, None, :], axis=-1)
    shares = jax.nn.softmax(picked, axis=-1)
    return jnp.sum(shares[:, :, None] * chosen, axis=1)


def swiglu(gate_up):
    half_cols = gate_up.shape[1] // 2
    return jax.nn.silu(gate_up[:, :half_cols]) * gate_up[:, half_cols:]


def fetch_attention(attn_gain, qkv_weight, out_weight):
    return (
        lax.all_gather(attn_gain, ("dp", "ctx"), axis=0, tiled=True),
        lax.all_gather(qkv_weight, ("dp", "ctx"), axis=0, tiled=True),
        lax.all_gather(out_weight, ("dp", "ctx"), axis=1, tiled=True),
    )


def fetch_experts(moe_gain, router, gateup_weight, down_weight):
    return (
        lax.all_gather(moe_gain, ("dp", "ctx"), axis=0, tiled=True),
        lax.all_gather(router, ("dp", "ctx"), axis=0, tiled=True),
        lax.all_gather(gateup_weight, ("dp", "ctx"), axis=1, tiled=True),
        lax.all_gather(down_weight, ("dp", "ctx"), axis=2, tiled=True),
    )


def pair_probs(query_block, keyval, allowed):
    scores = (
        jnp.einsum(
            "hgsd,htd->hgst", query_block, keyval[..., :HD], preferred_element_type=jnp.float32
        )
        * 0.125
    )
    return jnp.where(allowed, scores, -1e30)


def attend_forward(queries, kv_pairs, allowed):

    def one_pair(operands):
        query_block, keyval = operands
        scores = pair_probs(query_block, keyval, allowed)
        row_max = jnp.max(scores, axis=-1, keepdims=True)
        expo = jnp.exp(scores - row_max)
        summed = jnp.sum(expo, axis=-1, keepdims=True)
        attn_probs = (expo / summed).astype(jnp.bfloat16)
        attended = jnp.einsum(
            "hgst,htd->hgsd", attn_probs, keyval[..., HD:], preferred_element_type=jnp.float32
        )
        return (attended, row_max, summed)

    return lax.map(one_pair, (queries, kv_pairs))


def attend_backward(queries, kv_pairs, allowed, row_maxes, row_sums, grad_pairs):

    def one_pair(operands):
        query_block, keyval, row_max, summed, grad_block = operands
        scores = pair_probs(query_block, keyval, allowed)
        attn_probs = jnp.exp(scores - row_max) / summed
        probs_low = attn_probs.astype(jnp.bfloat16)
        grad_probs = jnp.einsum(
            "hgsd,htd->hgst", grad_block, keyval[..., HD:], preferred_element_type=jnp.float32
        )
        inner = jnp.sum(attn_probs * grad_probs, axis=-1, keepdims=True)
        grad_scores = (attn_probs * (grad_probs - inner)).astype(jnp.bfloat16)
        grad_query = (
            jnp.einsum(
                "hgst,htd->hgsd", grad_scores, keyval[..., :HD], preferred_element_type=jnp.float32
            )
            * 0.125
        )
        grad_keys = (
            jnp.einsum(
                "hgst,hgsd->htd", grad_scores, query_block, preferred_element_type=jnp.float32
            )
            * 0.125
        )
        grad_values = jnp.einsum(
            "hgst,hgsd->htd", probs_low, grad_block, preferred_element_type=jnp.float32
        )
        return (grad_query, jnp.concatenate([grad_keys, grad_values], axis=-1))

    return lax.map(one_pair, (queries, kv_pairs, row_maxes, row_sums, grad_pairs))


def to_pairs(rows, slot_count, groups):
    return (
        rows.reshape(slot_count, KVH, groups, HD)
        .transpose(1, 2, 0, 3)
        .reshape(KVH, 1, groups, slot_count, HD)
    )


def from_pairs(pairs, slot_count, groups):
    return pairs.reshape(KVH, groups, slot_count, HD).transpose(2, 0, 1, 3).reshape(slot_count, QW)


def body(
    tokens,
    lengths,
    routes,
    cotangent,
    attn_gain,
    qkv_weight,
    out_weight,
    moe_gain,
    router,
    gateup_weight,
    down_weight,
):
    slot_count = tokens.shape[2]
    groups = H // KVH
    key_count = slot_count * lax.axis_size("ctx")
    positions = lax.axis_index("ctx") * slot_count + jnp.arange(slot_count, dtype=jnp.int32)
    key_pos = jnp.arange(key_count, dtype=jnp.int32)
    expert_ids = jnp.arange(E, dtype=jnp.int32)
    acc_attn_gain = jnp.zeros((D,), jnp.float32)
    acc_qkv = jnp.zeros((D, QW + 2 * KW), jnp.float32)
    acc_out = jnp.zeros((D, QW), jnp.float32)
    acc_moe_gain = jnp.zeros((D,), jnp.float32)
    acc_router = jnp.zeros((D, E), jnp.float32)
    acc_gateup = [jnp.zeros((D, 2 * FF), jnp.float32) for expert in range(E)]
    acc_down = [jnp.zeros((D, FF), jnp.float32) for expert in range(E)]
    outputs = []
    input_grads = []
    for current in range(MB):
        attn_set = fetch_attention(attn_gain, qkv_weight, out_weight)
        moe_set = fetch_experts(moe_gain, router, gateup_weight, down_weight)
        gain_first = attn_set[0].astype(jnp.float32)
        qkv_full = attn_set[1]
        out_full = attn_set[2]
        gain_second = moe_set[0].astype(jnp.float32)
        router_full = moe_set[1]
        gateup_full = moe_set[2]
        down_full = moe_set[3]
        rows_in = tokens[current, 0].astype(jnp.float32)
        length = lengths[current, 0]
        valid_rows = (positions < length).astype(jnp.float32)[:, None]
        packed = rms_scale(rows_in, gain_first).astype(jnp.bfloat16)
        qkv = jnp.dot(packed, qkv_full, preferred_element_type=jnp.float32).astype(jnp.bfloat16)
        queries = to_pairs(qkv[:, :QW], slot_count, groups)
        local_kv = jnp.concatenate(
            [
                qkv[:, QW : QW + KW].reshape(slot_count, KVH, HD),
                qkv[:, QW + KW :].reshape(slot_count, KVH, HD),
            ],
            axis=-1,
        ).transpose(1, 0, 2)
        kv_full = lax.all_gather(local_kv, "ctx", axis=1, tiled=True)
        kv_pairs = kv_full.reshape(KVH, 1, key_count, 2 * HD)
        allowed = (key_pos[None, :] <= positions[:, None]) & (key_pos[None, :] < length)
        attended, row_maxes, row_sums = attend_forward(queries, kv_pairs, allowed)
        attended_low = from_pairs(attended, slot_count, groups).astype(jnp.bfloat16)
        branch = jnp.dot(attended_low, out_full, preferred_element_type=jnp.float32)
        mixed = rows_in + valid_rows * branch
        normed = rms_scale(mixed, gain_second).astype(jnp.bfloat16)
        logits = jnp.dot(normed, router_full, preferred_element_type=jnp.float32)
        chosen = (routes[current, 0][:, :, None] == expert_ids[None, None, :]).astype(jnp.float32)
        combine = gate_mix(logits, chosen)
        mixture = jnp.zeros((slot_count, D), jnp.float32)
        gate_ups = []
        activations = []
        expert_outs = []
        for expert in range(E):
            gate_up = jnp.dot(normed, gateup_full[expert], preferred_element_type=jnp.float32)
            activated = swiglu(gate_up).astype(jnp.bfloat16)
            expert_out = jnp.dot(activated, down_full[expert], preferred_element_type=jnp.float32)
            mixture = mixture + combine[:, expert : expert + 1] * expert_out
            gate_ups.append(gate_up)
            activations.append(activated)
            expert_outs.append(expert_out)
        outputs.append((mixed + valid_rows * mixture).astype(jnp.bfloat16))
        attn_set = fetch_attention(attn_gain, qkv_weight, out_weight)
        moe_set = fetch_experts(moe_gain, router, gateup_weight, down_weight)
        qkv_full = attn_set[1]
        out_full = attn_set[2]
        router_full = moe_set[1]
        gateup_full = moe_set[2]
        down_full = moe_set[3]
        grad_rows = cotangent[current, 0].astype(jnp.float32)
        grad_mixture = valid_rows * grad_rows
        grad_normed = jnp.zeros((slot_count, D), jnp.float32)
        grad_combine_cols = []
        for expert in range(E):
            grad_expert = (combine[:, expert : expert + 1] * grad_mixture).astype(jnp.bfloat16)
            grad_combine_cols.append(jnp.sum(expert_outs[expert] * grad_mixture, axis=-1))
            grad_act = jnp.dot(grad_expert, down_full[expert].T, preferred_element_type=jnp.float32)
            unused, pull_back = jax.vjp(swiglu, gate_ups[expert])
            grad_gate_up = pull_back(grad_act)[0].astype(jnp.bfloat16)
            grad_normed = grad_normed + jnp.dot(
                grad_gate_up, gateup_full[expert].T, preferred_element_type=jnp.float32
            )
            acc_gateup[expert] = acc_gateup[expert] + jnp.dot(
                normed.T, grad_gate_up, preferred_element_type=jnp.float32
            )
            acc_down[expert] = acc_down[expert] + jnp.dot(
                grad_expert.T, activations[expert], preferred_element_type=jnp.float32
            )
        grad_combine = jnp.stack(grad_combine_cols, axis=1)
        unused, pull_back = jax.vjp(lambda logit_rows: gate_mix(logit_rows, chosen), logits)
        grad_logits = pull_back(grad_combine)[0].astype(jnp.bfloat16)
        grad_normed = grad_normed + jnp.dot(
            grad_logits, router_full.T, preferred_element_type=jnp.float32
        )
        acc_router = acc_router + jnp.dot(normed.T, grad_logits, preferred_element_type=jnp.float32)
        unused, pull_back = jax.vjp(rms_scale, mixed, gain_second)
        grad_mixed_norm, grad_gain_second = pull_back(grad_normed)
        acc_moe_gain = acc_moe_gain + grad_gain_second
        grad_mixed = grad_rows + grad_mixed_norm
        grad_branch = (valid_rows * grad_mixed).astype(jnp.bfloat16)
        acc_out = acc_out + jnp.dot(grad_branch.T, attended_low, preferred_element_type=jnp.float32)
        grad_attended = jnp.dot(grad_branch, out_full.T, preferred_element_type=jnp.float32).astype(
            jnp.bfloat16
        )
        kv_back = lax.all_gather(local_kv, "ctx", axis=1, tiled=True).reshape(
            KVH, 1, key_count, 2 * HD
        )
        grad_query, grad_kv = attend_backward(
            queries,
            kv_back,
            allowed,
            row_maxes,
            row_sums,
            to_pairs(grad_attended, slot_count, groups),
        )
        grad_kv_own = lax.psum_scatter(
            grad_kv.reshape(KVH, key_count, 2 * HD), "ctx", scatter_dimension=1, tiled=True
        )
        grad_qkv = jnp.concatenate(
            [
                from_pairs(grad_query, slot_count, groups),
                grad_kv_own[..., :HD].transpose(1, 0, 2).reshape(slot_count, KW),
                grad_kv_own[..., HD:].transpose(1, 0, 2).reshape(slot_count, KW),
            ],
            axis=1,
        ).astype(jnp.bfloat16)
        acc_qkv = acc_qkv + jnp.dot(packed.T, grad_qkv, preferred_element_type=jnp.float32)
        grad_normed_in = jnp.dot(grad_qkv, qkv_full.T, preferred_element_type=jnp.float32)
        unused, pull_back = jax.vjp(rms_scale, rows_in, gain_first)
        grad_rows_norm, grad_gain_first = pull_back(grad_normed_in)
        acc_attn_gain = acc_attn_gain + grad_gain_first
        input_grads.append((grad_mixed + grad_rows_norm).astype(jnp.bfloat16))
    summed_grads = (
        lax.psum_scatter(acc_attn_gain, ("dp", "ctx"), scatter_dimension=0, tiled=True),
        lax.psum_scatter(acc_qkv, ("dp", "ctx"), scatter_dimension=0, tiled=True),
        lax.psum_scatter(acc_out, ("dp", "ctx"), scatter_dimension=0, tiled=True),
        lax.psum_scatter(acc_moe_gain, ("dp", "ctx"), scatter_dimension=0, tiled=True),
        lax.psum_scatter(acc_router, ("dp", "ctx"), scatter_dimension=0, tiled=True),
        lax.psum_scatter(
            jnp.stack(acc_gateup, axis=1), ("dp", "ctx"), scatter_dimension=0, tiled=True
        ),
        lax.psum_scatter(
            jnp.stack(acc_down, axis=1), ("dp", "ctx"), scatter_dimension=0, tiled=True
        ),
    )
    result = jnp.stack(outputs, axis=0)[:, None]
    grad_tokens = jnp.stack(input_grads, axis=0)[:, None]
    return (
        result,
        grad_tokens,
        summed_grads[0],
        summed_grads[1],
        summed_grads[2].T,
        summed_grads[3],
        summed_grads[4],
        summed_grads[5].transpose(1, 0, 2),
        summed_grads[6].transpose(1, 2, 0),
    )


def solution(mesh):
    in_specs = (
        P(None, "dp", "ctx", None),
        P(None, "dp"),
        P(None, "dp", "ctx", None),
        P(None, "dp", "ctx", None),
        P(("dp", "ctx")),
        P(("dp", "ctx"), None),
        P(None, ("dp", "ctx")),
        P(("dp", "ctx")),
        P(("dp", "ctx"), None),
        P(None, ("dp", "ctx"), None),
        P(None, None, ("dp", "ctx")),
    )
    out_specs = (
        P(None, "dp", "ctx", None),
        P(None, "dp", "ctx", None),
        P(("dp", "ctx")),
        P(("dp", "ctx"), None),
        P(None, ("dp", "ctx")),
        P(("dp", "ctx")),
        P(("dp", "ctx"), None),
        P(None, ("dp", "ctx"), None),
        P(None, None, ("dp", "ctx")),
    )
    return jax.shard_map(body, mesh=mesh, in_specs=in_specs, out_specs=out_specs, check_vma=False)
```

profile of v0, /device:TPU:0, one launch (start us, length us, event | category | flops | bytes accessed | tf_op | source)
XLA Modules:
  0.0 2127.7 jit_solution(15032596763810968730)
XLA Ops:
  9.7 42.6 %all-reduce.21 = (bf16[1536]{0:T(1024)(128)(2,1)S(1)}, bf16[1536]{0:T(1024)(128)(2,1)S(1)}) all-reduce(bf16[1536]{0:T(1024)(128)(2,1)S(1)} %dynamic-update-slice, bf16[1536]{0:T(1024)(128)(2,1)S(1)} %dynamic-update-slice.1), channel_id=1, replica_groups=mesh['dp'=2,'ctx'=16] {'dp','ctx'}, use_global_device_ids=true, to_apply=%add.16 | all-reduce | flops 3072 | bytes 12288
  53.5 36.1 %all-gather.8.cloned.1.call-done = bf16[1536,2560]{1,0:T(8,128)(2,1)} async-done(((bf16[48,2560]{1,0:T(8,128)(2,1)}), bf16[1536,2560]{1,0:T(8,128)(2,1)}) %all-gather.8.cloned.1.call-update) | async-done | bytes 7864336 | tf_op jit(solution)/shard_map/all_gather | solution.py:35
  107.7 39.2 %all-gather = bf16[32,48,4]{1,2,0:T(4,128)(2,1)S(1)} all-gather(bf16[1,48,4]{1,2,0:T(4,128)(2,1)S(1)} %bitcast.655), channel_id=1, replica_groups=mesh['dp'=2,'ctx'=16] {'dp','ctx'}, dimensions={0}, use_global_device_ids=true | all-gather | bytes 12672 | tf_op jit(solution)/shard_map/all_gather | solution.py:43
  153.9 24.8 %all-gather.10.cloned.1.call-done = bf16[8,1024,128]{2,0,1:T(8,128)(2,1)} async-done(((bf16[8,64,128]{2,0,1:T(8,128)(2,1)}), bf16[8,1024,128]{2,0,1:T(8,128)(2,1)}) %all-gather.10.cloned.1.call-update) | async-done | bytes 2097168 | tf_op jit(solution)/shard_map/all_gather | solution.py:171
  184.1 33.1 %while.57 = (s32[]{:T(128)}, bf16[8,1,3,64,64]{4,3,2,1,0:T(8,128)(2,1)S(1)}, f32[8,1,3,64,1]{3,2,4,1,0:T(4,128)}, f32[8,1,3,64,1]{3,2,4,1,0:T(4,128)}, bf16[8,1,...) while((s32[]{:T(128)}, ...), condition=%wide.region_14.15_spmd.clone, body=%wide.region_11.14_spmd.clone.sunk | while | flops 52035200 | bytes 3437685 | solution.py:73
  219.4 28.2 %while.56 = (s32[]{:T(128)}, bf16[8,1,3,64,64]{4,3,2,1,0:T(8,128)(2,1)S(1)}, f32[8,1,3,64,1]{3,2,4,1,0:T(4,128)}, f32[8,1,3,64,1]{3,2,4,1,0:T(4,128)}, bf16[8,1,...) while((s32[]{:T(128)}, ...), condition=%wide.region_4.5_spmd.clone, body=%wide.region_1.4_spmd.clone.sunk | while | flops 52035200 | bytes 3437685 | solution.py:73
  258.7 141.6 %all-gather.14.cloned.1.call-done = bf16[4,1536,2048]{2,1,0:T(8,128)(2,1)} async-done(((bf16[4,48,2048]{2,1,0:T(8,128)(2,1)}), bf16[4,1536,2048]{2,1,0:T(8,128)(2,1)}) %all-gather.14.cloned.1.call-update) | async-done | bytes 25165840 | tf_op jit(solution)/shard_map/all_gather | solution.py:44
  428.4 69.0 %all-gather.16.cloned.1.call-done = bf16[4,1024,1536]{1,2,0:T(8,128)(2,1)} async-done(((bf16[4,1024,48]{1,2,0:T(8,128)(2,1)}), bf16[4,1024,1536]{1,2,0:T(8,128)(2,1)}) %all-gather.16.cloned.1.call-update) | async-done | bytes 12582928 | tf_op jit(solution)/shard_map/all_gather | solution.py:45
  586.7 184.7 %while.59 = (s32[]{:T(128)}, bf16[8,1,3,64,64]{4,3,2,1,0:T(8,128)(2,1)}, f32[8,1,1024,128]{3,0,2,1:T(8,128)}, bf16[8,1,3,64,64]{4,3,2,1,0:T(8,128)(2,1)}, bf16[8...) while((s32[]{:T(128)}, ...), condition=%wide.region_43.44_spmd.clone, body=%wide.region_41.43_spmd.clone.sunk | while | flops 128134976 | bytes 10921885 | solution.py:105
  595.0 14.8 dynamic_update_slice.66
  618.1 14.8 dynamic_update_slice.66
  641.2 14.8 dynamic_update_slice.66
  664.3 14.8 dynamic_update_slice.66
  687.3 14.8 dynamic_update_slice.66
  710.4 14.8 dynamic_update_slice.66
  733.5 14.8 dynamic_update_slice.66
  756.6 14.8 dynamic_update_slice.66
  774.7 166.4 %while.58 = (s32[]{:T(128)}, bf16[8,1,3,64,64]{4,3,2,1,0:T(8,128)(2,1)}, f32[8,1,1024,128]{3,0,2,1:T(8,128)}, bf16[8,1,3,64,64]{4,3,2,1,0:T(8,128)(2,1)}, bf16[8...) while((s32[]{:T(128)}, ...), condition=%wide.region_30.31_spmd.clone, body=%wide.region_28.30_spmd.clone.sunk | while | flops 128134976 | bytes 10921885 | solution.py:105
  780.6 14.9 dynamic_update_slice.64
  801.5 14.8 dynamic_update_slice.64
  822.3 14.8 dynamic_update_slice.64
  843.1 14.8 dynamic_update_slice.64
  863.9 14.8 dynamic_update_slice.64
  884.7 14.8 dynamic_update_slice.64
  905.5 14.8 dynamic_update_slice.64
  964.7 47.2 %reduce-scatter.10.cloned.1.call-done = f32[8,64,128]{2,0,1:T(8,128)} async-done(((f32[8,1024,128]{2,0,1:T(8,128)}), f32[8,64,128]{2,0,1:T(8,128)}) %reduce-scatter.10.cloned.1.call-update) | async-done | bytes 262160 | tf_op jit(solution)/shard_map/reduce_scatter | solution.py:248
  1094.2 34.7 %pad_maximum_fusion = f32[1536,4,2048]{2,0,1:T(8,128)} fusion(f32[1536,1,2048]{2,0,1:T(8,128)} %add_bitcast_fusion, f32[1536,1,2048]{2,0,1:T(8,128)} %add_bitcast_fusion.1, f32[1536,1,2048]{2,0,1:T(8,128)} %add_bitcast_fusion.2, f32[1536,1,2048]{2,0,1:T(8,128)} %add_bitcast_fusion.3), kind=kLoop, calls=%fused_computation.114 | loop fusion | flops 37748736 | bytes 100663296 | tf_op jit(solution)/shard_map/stack | solution.py:272
  1144.5 40.9 %all-reduce.20 = (f32[1536]{0:T(1024)S(1)}, f32[1536]{0:T(1024)S(1)}) all-reduce(f32[1536]{0:T(1024)S(1)} %add.297, f32[1536]{0:T(1024)S(1)} %add.300), channel_id=4, replica_groups=mesh['dp'=2,'ctx'=16] {'dp','ctx'}, use_global_device_ids=true, to_apply=%region_48.49.clone | all-reduce | flops 3072 | bytes 24576
  1187.7 65.3 %reduce-scatter.16.cloned.1.call-done = f32[48,1536]{1,0:T(8,128)} async-done(((f32[1536,1536]{1,0:T(8,128)}), f32[48,1536]{1,0:T(8,128)}) %reduce-scatter.16.cloned.1.call-update) | async-done | bytes 294928 | tf_op jit(solution)/shard_map/reduce_scatter | solution.py:268
  1253.0 177.2 %reduce-scatter.14.cloned.1.call-done = f32[48,2560]{1,0:T(8,128)} async-done(((f32[1536,2560]{1,0:T(8,128)}), f32[48,2560]{1,0:T(8,128)}) %reduce-scatter.14.cloned.1.call-update) | async-done | bytes 491536 | tf_op jit(solution)/shard_map/reduce_scatter | solution.py:267
  1430.2 252.6 %reduce-scatter.20.cloned.1.call-done = f32[48,4,1024]{2,0,1:T(8,128)} async-done(((f32[1536,4,1024]{2,0,1:T(8,128)}), f32[48,4,1024]{2,0,1:T(8,128)}) %reduce-scatter.20.cloned.1.call-update) | async-done | bytes 786448 | tf_op jit(solution)/shard_map/reduce_scatter | solution.py:274
  1682.8 438.2 %reduce-scatter.18.cloned.1.call-done = f32[48,4,2048]{2,0,1:T(8,128)} async-done(((f32[1536,4,2048]{2,0,1:T(8,128)}), f32[48,4,2048]{2,0,1:T(8,128)}) %reduce-scatter.18.cloned.1.call-update) | async-done | bytes 1572880 | tf_op jit(solution)/shard_map/reduce_scatter | solution.py:271
  (776 shorter events, 477.5 us)
Async XLA Ops:
  7.2 82.4 %all-gather.8.cloned.1.call-start = ((), (), s32[]{:S(2)}) async-start(), calls=%async_computation.7 | async-start | bytes 8110080 | tf_op jit(solution)/shard_map/all_gather | solution.py:35
  7.9 141.9 %all-gather.18.cloned.1.call-start = ((), (), s32[]{:S(2)}) async-start(), calls=%async_computation.12 | async-start | bytes 2228224 | tf_op jit(solution)/shard_map/all_gather | solution.py:171
  95.5 83.2 %all-gather.10.cloned.1.call-start = ((), (), s32[]{:S(2)}) async-start(), calls=%async_computation.8 | async-start | bytes 2228224 | tf_op jit(solution)/shard_map/all_gather | solution.py:171
  101.5 146.9 %all-gather.12.cloned.1.call-start = ((), (), s32[]{:S(2)}) async-start(), calls=%async_computation.9 | async-start | bytes 4866048 | tf_op jit(solution)/shard_map/all_gather | solution.py:36
  102.1 298.2 %all-gather.14.cloned.1.call-start = ((), (), s32[]{:S(2)}) async-start(), calls=%async_computation.10 | async-start | bytes 25952256 | tf_op jit(solution)/shard_map/all_gather | solution.py:44
  102.7 394.7 %all-gather.16.cloned.1.call-start = ((), (), s32[]{:S(2)}) async-start(), calls=%async_computation.11 | async-start | bytes 12976128 | tf_op jit(solution)/shard_map/all_gather | solution.py:45
  103.3 860.1 %reduce-scatter.12.cloned.1.call-start = ((), (), s32[]{:S(2)}) async-start(), calls=%async_computation.14 | async-start | bytes 4456448 | tf_op jit(solution)/shard_map/reduce_scatter | solution.py:248
  104.6 147.9 %copy-start.90 = (f32[64]{0:T(128)}, f32[64]{0:T(128)S(1)}, u32[]{:S(2)}) copy-start(f32[64]{0:T(128)S(1)} %compare_convert_fusion) | copy-start | bytes 772
  106.5 141.9 %copy-start.86 = (f32[64]{0:T(128)}, f32[64]{0:T(128)S(1)}, u32[]{:S(2)}) copy-start(f32[64]{0:T(128)S(1)} %compare_convert_fusion.1) | copy-start | bytes 772
  107.7 149.3 %copy-start.84 = (f32[1536]{0:T(1024)}, f32[1536]{0:T(1024)S(1)}, u32[]{:S(2)}) copy-start(f32[1536]{0:T(1024)S(1)} %convert_element_type.280) | copy-start | bytes 18436
  147.0 110.9 %copy-start.50 = (bf16[1536,4]{0,1:T(4,128)(2,1)}, bf16[1536,4]{0,1:T(4,128)(2,1)S(1)}, u32[]{:S(2)}) copy-start(bf16[1536,4]{0,1:T(4,128)(2,1)S(1)} %reshape.653) | copy-start | bytes 36868
  405.2 92.2 %copy-start.23 = (bf16[64,1024]{1,0:T(8,128)(2,1)}, bf16[64,1024]{1,0:T(8,128)(2,1)S(1)}, u32[]{:S(2)}) copy-start(bf16[64,1024]{1,0:T(8,128)(2,1)S(1)} %multiply_convert_fusion.10) | copy-start | bytes 393220
  410.9 89.6 %copy-start.27 = (bf16[64,1024]{1,0:T(8,128)(2,1)}, bf16[64,1024]{1,0:T(8,128)(2,1)S(1)}, u32[]{:S(2)}) copy-start(bf16[64,1024]{1,0:T(8,128)(2,1)S(1)} %multiply_convert_fusion.11) | copy-start | bytes 393220
  415.8 88.5 %copy-start.30 = (bf16[64,1024]{1,0:T(8,128)(2,1)}, bf16[64,1024]{1,0:T(8,128)(2,1)S(1)}, u32[]{:S(2)}) copy-start(bf16[64,1024]{1,0:T(8,128)(2,1)S(1)} %multiply_convert_fusion.12) | copy-start | bytes 393220
  421.4 86.0 %copy-start.25 = (bf16[64,1024]{1,0:T(8,128)(2,1)}, bf16[64,1024]{1,0:T(8,128)(2,1)S(1)}, u32[]{:S(2)}) copy-start(bf16[64,1024]{1,0:T(8,128)(2,1)S(1)} %multiply_convert_fusion.6) | copy-start | bytes 393220
  427.6 69.8 %copy-start.49 = (f32[64,2048]{1,0:T(8,128)}, f32[64,2048]{1,0:T(8,128)S(1)}, u32[]{:S(2)}) copy-start(f32[64,2048]{1,0:T(8,128)S(1)} %fusion.74) | copy-start | bytes 1572868
  517.3 57.6 %copy-start.101 = (bf16[64,4]{0,1:T(4,128)(2,1)}, bf16[64,4]{0,1:T(4,128)(2,1)S(1)}, u32[]{:S(2)}) copy-start(bf16[64,4]{0,1:T(4,128)(2,1)S(1)} %get-tuple-element.449) | copy-start | bytes 1540
  517.3 57.8 %copy-start.105 = (f32[64]{0:T(128)}, f32[64]{0:T(128)S(1)}, u32[]{:S(2)}) copy-start(f32[64]{0:T(128)S(1)} %get-tuple-element.582) | copy-start | bytes 772
  517.3 57.8 %copy-start.107 = (f32[64]{0:T(128)}, f32[64]{0:T(128)S(1)}, u32[]{:S(2)}) copy-start(f32[64]{0:T(128)S(1)} %get-tuple-element.583) | copy-start | bytes 772
  517.4 57.8 %copy-start.109 = (f32[64]{0:T(128)}, f32[64]{0:T(128)S(1)}, u32[]{:S(2)}) copy-start(f32[64]{0:T(128)S(1)} %get-tuple-element.584) | copy-start | bytes 772
  517.4 57.8 %copy-start.111 = (f32[64]{0:T(128)}, f32[64]{0:T(128)S(1)}, u32[]{:S(2)}) copy-start(f32[64]{0:T(128)S(1)} %get-tuple-element.581) | copy-start | bytes 772
  577.1 366.9 %copy-start.2 = (f32[64,1536]{1,0:T(8,128)}, f32[64,1536]{1,0:T(8,128)S(1)}, u32[]{:S(2)}) copy-start(f32[64,1536]{1,0:T(8,128)S(1)} %get-tuple-element.567) | copy-start | bytes 1179652
  577.1 373.2 %copy-start.4 = (f32[64,1536]{1,0:T(8,128)}, f32[64,1536]{1,0:T(8,128)S(1)}, u32[]{:S(2)}) copy-start(f32[64,1536]{1,0:T(8,128)S(1)} %get-tuple-element.568) | copy-start | bytes 1179652
  771.5 240.4 %reduce-scatter.10.cloned.1.call-start = ((), (), s32[]{:S(2)}) async-start(), calls=%async_computation.13 | async-start | bytes 4456448 | tf_op jit(solution)/shard_map/reduce_scatter | solution.py:248
  941.1 189.6 %reduce-scatter.22.cloned.1.call-start = ((), (), s32[]{:S(2)}) async-start(), calls=%async_computation.19 | async-start | bytes 811008
  950.2 302.7 %reduce-scatter.16.cloned.1.call-start = ((), (), s32[]{:S(2)}) async-start(), calls=%async_computation.16 | async-start | bytes 9732096 | tf_op jit(solution)/shard_map/reduce_scatter | solution.py:268
  959.6 470.6 %reduce-scatter.14.cloned.1.call-start = ((), (), s32[]{:S(2)}) async-start(), calls=%async_computation.15 | async-start | bytes 16220160 | tf_op jit(solution)/shard_map/reduce_scatter | solution.py:267
  1023.5 659.3 %reduce-scatter.20.cloned.1.call-start = ((), (), s32[]{:S(2)}) async-start(), calls=%async_computation.18 | async-start | bytes 25952256 | tf_op jit(solution)/shard_map/reduce_scatter | solution.py:274
  1041.9 1079.1 %reduce-scatter.18.cloned.1.call-start = ((), (), s32[]{:S(2)}) async-start(), calls=%async_computation.17 | async-start | bytes 51904512 | tf_op jit(solution)/shard_map/reduce_scatter | solution.py:271
  1132.1 54.5 %copy-start.131 = (f32[64]{0:T(128)S(1)}, f32[64]{0:T(128)}, u32[]{:S(2)}) copy-start(f32[64]{0:T(128)} %copy-done.130) | copy-start | bytes 772
  1132.1 54.5 %copy-start.3 = (f32[64,1536]{1,0:T(8,128)S(1)}, f32[64,1536]{1,0:T(8,128)}, u32[]{:S(2)}) copy-start(f32[64,1536]{1,0:T(8,128)} %copy-done.2) | copy-start | bytes 1179652
  1132.1 54.5 %copy-start.5 = (f32[64,1536]{1,0:T(8,128)S(1)}, f32[64,1536]{1,0:T(8,128)}, u32[]{:S(2)}) copy-start(f32[64,1536]{1,0:T(8,128)} %copy-done.4) | copy-start | bytes 1179652
  (125 other events, 1223.7 us)
Sparse Core Ops, SparseCore 0:
  10.9 78.6 all-gather.7
  95.7 40.0 all-gather.17
  138.4 40.2 all-gather.9
  181.5 62.4 all-gather.11
  246.7 153.5 all-gather.13
  403.1 94.2 all-gather.15
  771.6 70.8 reduce-scatter.11
  941.2 70.6 reduce-scatter.9
  1017.0 94.6 reduce-scatter.21
  1118.1 134.8 reduce-scatter.15
  1260.6 169.5 reduce-scatter.13
  1438.2 244.5 reduce-scatter.19
  1689.8 431.1 reduce-scatter.17
where the time goes:
time: 2150 us; the launch traced here: 2130 us
  waiting for transfers between devices  1250 us (58%)
  local copies, waits for them, and re-layouts  334 us (16%)
  matrix products  316 us (15%)
  blocking collectives  123 us (6%)
  other arithmetic  81.2 us (4%)
    reduce_scatter x1, waiting for transfers between devices, body(): lax.psum_scatter(jnp.stack(acc_gateup, axis=1), ('dp', 'ctx'), scatter_di...  438 us
    reduce_scatter x1, waiting for transfers between devices, body(): lax.psum_scatter(jnp.stack(acc_down, axis=1), ('dp', 'ctx'), scatter_dime...  253 us
    dynamic_update_slice x32, local copies, waits for them, and re-layouts, attend_backward(): lax.map(one_pair, (queries, kv_pairs, row_maxes, row_sums, grad_pairs))  243 us
    reduce_scatter x1, waiting for transfers between devices, body(): lax.psum_scatter(acc_qkv, ('dp', 'ctx'), scatter_dimension=0, tiled=True)  177 us
    all_gather x1, waiting for transfers between devices, fetch_experts(): lax.all_gather(gateup_weight, ('dp', 'ctx'), axis=1, tiled=True)  142 us
    unnamed x2, blocking collectives  83.5 us
    all_gather x1, waiting for transfers between devices, fetch_experts(): lax.all_gather(down_weight, ('dp', 'ctx'), axis=2, tiled=True)  69 us
    reduce_scatter x1, waiting for transfers between devices, body(): lax.psum_scatter(acc_out, ('dp', 'ctx'), scatter_dimension=0, tiled=True)  65.3 us
  transfers between devices with their start and end apart: 13, of which 9 were waited for; matrix products, arithmetic and copies ran while one was open for 21% of the time, Pallas kernels for 0%

commit v1 on v0

v1 whole, which is shorter than its diff:
```python
import functools

import jax
import jax.numpy as jnp
from jax import lax
from jax.experimental import pallas as pl
from jax.experimental.pallas import tpu as pltpu
from jax.sharding import PartitionSpec as P

D = 1536
H = 24
KVH = 8
HD = 64
FF = 1024
E = 4
MB = 2
QW = 1536
KW = 512
CUBE = 8
GROUP = H // KVH
HALF = FF // 2
QH = GROUP * HD
SHARD = QH + 2 * HD
EXTRA = 128
WIDE = D + EXTRA
ORDER = (0, 4, 2, 6, 1, 5, 3, 7)
LOG2E = 1.4426950408889634
F32 = jnp.float32
BF16 = jnp.bfloat16
NN = (((1,), (0,)), ((), ()))
NT = (((1,), (1,)), ((), ()))
TN = (((0,), (0,)), ((), ()))
AXES = ("dp", "ctx")


def dot(left, right, dims=NN):
    return lax.dot_general(left, right, dims, preferred_element_type=F32)


def kernel_call(kernel, outs, ins, scratch=(), flops=0, scalars=True):
    vmem = pl.BlockSpec(memory_space=pltpu.VMEM)
    smem = pl.BlockSpec(memory_space=pltpu.SMEM)
    specs = [vmem] * len(ins)
    if scalars:
        specs[0] = smem
    moved = sum(a.size * a.dtype.itemsize for a in list(ins) + list(outs))
    return pl.pallas_call(
        kernel,
        out_shape=list(outs),
        in_specs=specs,
        out_specs=[vmem] * len(outs),
        scratch_shapes=list(scratch),
        compiler_params=pltpu.CompilerParams(vmem_limit_bytes=56 * 1024 * 1024),
        cost_estimate=pl.CostEstimate(flops=flops, bytes_accessed=moved, transcendentals=0),
    )(*ins)


def shape(dims, dtype=BF16):
    return jax.ShapeDtypeStruct(dims, dtype)


class Links:
    def __init__(self, nx, nc):
        self.nx, self.nc, self.ng = nx, nc, nc // CUBE

    def _pairs(self, move):
        pairs = []
        for x in range(self.nx):
            for g in range(self.ng):
                for t in range(CUBE):
                    goal = move(x, g, t)
                    if goal is not None:
                        gx, gg, gt = goal
                        pairs.append((x * self.nc + g * CUBE + t, gx * self.nc + gg * CUBE + gt))
        return pairs

    def cube(self, value, bits):
        return lax.ppermute(value, AXES, self._pairs(lambda x, g, t: (x, g, t ^ bits)))

    def outer(self, value, dx, dg):
        return lax.ppermute(value, AXES, self._pairs(lambda x, g, t: (x ^ dx, g ^ dg, t)))

    def climb(self, value, step):
        def move(x, g, t):
            return (x, g + step, t) if 0 <= g + step < self.ng else None

        return lax.ppermute(value, AXES, self._pairs(move))

    def cubes(self):
        return [
            [x * self.nc + g * CUBE + t for t in range(CUBE)]
            for x in range(self.nx)
            for g in range(self.ng)
        ]

    def swap(self, value):
        return lax.all_to_all(
            value, AXES, split_axis=0, concat_axis=0, tiled=True, axis_index_groups=self.cubes()
        )

    def cube_gather(self, rows):
        half = rows.shape[0] // 2
        far = self.cube(rows, 4)
        side = self.cube(rows, 2)
        low = self.cube(far[:half], 2)
        high = self.cube(side[half:], 4)
        near = [rows, far, side, low, high]
        return near + [self.cube(block, 1) for block in near]

    def outer_gather(self, rows):
        own = [rows] + [self.outer(rows, 0, dg) for dg in range(1, self.ng)]
        for dx in range(1, self.nx):
            own = own + [self.outer(block, dx, 0) for block in own[: self.ng]]
        return own

    def outer_scatter(self, parts, x, g):
        total = parts[0].astype(F32)
        for dx in range(1, self.nx):
            total = total + self.outer(parts[dx], dx, 0).astype(F32)
        rows = total.shape[0] // self.ng
        total = total.reshape(self.ng, rows, total.shape[1])
        own = lax.dynamic_index_in_dim(total, g, 0, keepdims=False)
        low = total.astype(BF16)
        for dg in range(1, self.ng):
            part = lax.dynamic_index_in_dim(low, g ^ dg, 0, keepdims=False)
            own = own + self.outer(part, 0, dg).astype(F32)
        return own


def cube_rows(refs, out, width=None):
    rows = refs[0].shape[0]
    half = rows // 2
    spots = (0, rows, 2 * rows, 3 * rows, 3 * rows + half)
    for base, group in ((0, refs[:5]), (4 * rows, refs[5:])):
        for spot, ref in zip(spots, group):
            out[base + spot : base + spot + ref.shape[0], :] = ref[...]


def outer_rows(refs, out, x, g, ng):
    rows = refs[0].shape[0]
    for j, ref in enumerate(refs):
        place = (x ^ (j // ng)) * ng + (g ^ (j % ng))
        out[pl.ds(pl.multiple_of(place * rows, 16), rows), :] = ref[...]


def qkv_kernel(ng, n_outer, scal, *refs):
    x, g = scal[0], scal[1]
    blocks, refs = refs[:10], refs[10:]
    weights, refs = refs[:n_outer], refs[n_outer:]
    xg, q_out, kv_out, w_full = refs
    cube_rows(blocks, xg)
    outer_rows(weights, w_full, x, g, ng)
    rows = blocks[0].shape[0]
    slots = rows // MB
    blank = jnp.zeros((slots, HD), BF16)
    for p, k in enumerate(ORDER):
        y = dot(xg[p * rows : (p + 1) * rows, :], w_full[...]).astype(BF16)
        for m in range(MB):
            part = y[m * slots : (m + 1) * slots]
            spot = slice(k * slots, (k + 1) * slots)
            for h in range(GROUP):
                q_out[m, h, spot, :] = jnp.concatenate(
                    [part[:, h * HD : (h + 1) * HD], blank], axis=1
                )
            kv_out[m, spot, :] = part[:, QH:]


def key_bias(block, slots, extent, g, t, step, length):
    local = lax.broadcasted_iota(jnp.int32, (extent, 1), 0) ^ (t * slots)
    seen = ((g - step) * extent + local < length) & (g >= step)
    return jnp.where(seen, 0.0, -1e30).astype(F32)


def causal_bias(slots, extent, t):
    keys = lax.broadcasted_iota(jnp.int32, (extent, extent), 0) ^ (t * slots)
    rows = lax.broadcasted_iota(jnp.int32, (extent, extent), 1) ^ (t * slots)
    return jnp.where(keys <= rows, 0.0, -1e30).astype(F32)


def attend_kernel(slots, scal, *refs):
    g, t = scal[1], scal[2]
    n_keys = len(refs) - 1 - CUBE - 2
    q_ref, kv_refs, refs = refs[0], refs[1 : 1 + n_keys], refs[1 + n_keys :]
    att_refs, (ot_ref, lse_ref) = refs[:CUBE], refs[CUBE:]
    extent = q_ref.shape[2]
    causal = causal_bias(slots, extent, t)
    for m in range(MB):
        length = scal[3 + m]
        biases = [key_bias(s, slots, extent, g, t, s, length) for s in range(n_keys)]
        for h in range(GROUP):
            q = q_ref[m, h]
            top = total = acc = None
            for s in range(n_keys):
                kv = kv_refs[s][m]
                st = dot(kv, q, NT) * (0.125 * LOG2E) + biases[s]
                if s == 0:
                    st = st + causal
                peak = jnp.max(st, axis=0, keepdims=True)
                if s == 0:
                    pt = jnp.exp2(st - peak)
                    top, total = peak, jnp.sum(pt, axis=0, keepdims=True)
                    acc = dot(kv, pt.astype(BF16), TN)
                else:
                    fresh = jnp.maximum(top, peak)
                    scale = jnp.exp2(top - fresh)
                    pt = jnp.exp2(st - fresh)
                    total = total * scale + jnp.sum(pt, axis=0, keepdims=True)
                    acc = acc * scale + dot(kv, pt.astype(BF16), TN)
                    top = fresh
            ot = acc[HD:, :] / total
            ot_ref[m, h] = ot
            lse_ref[m, h : h + 1, :] = top + jnp.log2(total)
            o = ot.T.astype(BF16)
            for k in range(CUBE):
                att_refs[k][m * slots : (m + 1) * slots, h * HD : (h + 1) * HD] = o[
                    k * slots : (k + 1) * slots
                ]


def row_valid(scal, rows):
    slots = rows // MB
    spot = lax.broadcasted_iota(jnp.int32, (rows, 1), 0)
    place = (scal[1] * CUBE + scal[2]) * slots
    length = jnp.where(spot < slots, scal[3], scal[4])
    inner = jnp.where(spot < slots, spot, spot - slots)
    return jnp.where(place + inner < length, 1.0, 0.0).astype(F32)


def mix_kernel(scal, x_ref, routes_ref, wo_ref, rt_ref, *refs):
    t = scal[2]
    att_refs, (mixed_ref, wide_ref, comb_ref) = refs[:CUBE], refs[CUBE:]
    rows = x_ref.shape[0]
    branch = jnp.zeros((rows, D), F32)
    for k in range(CUBE):
        spot = pl.ds(pl.multiple_of((t ^ k) * QH, 64), QH)
        branch = branch + dot(att_refs[k][...], wo_ref[spot, :])
    valid = row_valid(scal, rows)
    mixed = x_ref[...].astype(F32) + valid * branch
    mixed_ref[...] = mixed
    scale = lax.rsqrt(jnp.mean(mixed * mixed, axis=-1, keepdims=True) + 1e-05)
    low = (mixed * scale).astype(BF16)
    logits = dot(low, rt_ref[...])
    lane = lax.broadcasted_iota(jnp.int32, (rows, EXTRA), 1)
    expert = lane & (E - 1)
    chosen = ((expert == routes_ref[:, 0:1]) | (expert == routes_ref[:, 1:2])) & (lane < 2 * E)
    peak = jnp.max(jnp.where(chosen, logits, -3e38), axis=-1, keepdims=True)
    expo = jnp.where(chosen, jnp.exp(logits - peak), 0.0)
    comb = expo / (0.5 * jnp.sum(expo, axis=-1, keepdims=True))
    comb_ref[...] = jnp.where(lane < E, comb, 0.0)
    comb = comb * valid
    high = comb.astype(BF16)
    rest = (comb - high.astype(F32)).astype(BF16)
    wide_ref[:, :D] = low
    wide_ref[:, D:] = jnp.where(lane < E, high, rest)


def cot_kernel(ng, n_outer, scal, *refs):
    x, g = scal[0], scal[1]
    blocks, refs = refs[:10], refs[10:]
    weights, (dyg, q_ref, w_full) = refs[:n_outer], refs[n_outer:]
    cube_rows(blocks, dyg)
    outer_rows(weights, w_full, x, g, ng)
    step = dyg.shape[0] // 4

    @pl.loop(0, 4)
    def _(i):
        spot = pl.ds(pl.multiple_of(i * step, 128), step)
        q_ref[spot, :] = dot(dyg[spot, :], w_full[...])


def own_share(wide, scal):
    lane = lax.broadcasted_iota(jnp.int32, wide.shape, 1)
    expert = scal[2] // 2
    mine = (lane == expert) | (lane == expert + E)
    return jnp.sum(jnp.where(mine, wide.astype(F32), 0.0), axis=-1, keepdims=True)


def expert_kernel(ng, n_outer, scal, *refs):
    x, g = scal[0], scal[1]
    blocks, refs = refs[:10], refs[10:]
    weights, refs = refs[:n_outer], refs[n_outer:]
    q_ref, ngw, act_ref, ggu_ref, even_ref, odd_ref, w_full = refs
    cube_rows(blocks, ngw)
    outer_rows(weights, w_full, x, g, ng)
    half_rows = ngw.shape[0] // 2
    step = half_rows // 2
    expert = scal[2] // 2
    for part, out_ref in enumerate((even_ref, odd_ref)):

        @pl.loop(0, 2)
        def _(i):
            local = pl.ds(pl.multiple_of(i * step, 128), step)
            spot = pl.ds(pl.multiple_of(part * half_rows + i * step, 128), step)
            share = own_share(ngw[spot, D:], scal)
            gu = dot(ngw[spot, :D], w_full[...])
            gate, up = gu[:, :HALF], gu[:, HALF:]
            sig = 1.0 / (1.0 + jnp.exp(-gate))
            soft = gate * sig
            act = (soft * up).astype(BF16)
            act_ref[spot, :] = act
            back = q_ref[spot, :]
            dots = jnp.sum(act.astype(F32) * back, axis=-1, keepdims=True)
            back = back * share
            ggu_ref[spot, :HALF] = (back * up * (sig * (1.0 + gate * (1.0 - sig)))).astype(BF16)
            ggu_ref[spot, HALF:] = (back * soft).astype(BF16)
            out_ref[local, :D] = dot(ggu_ref[spot, :], w_full[...], NT).astype(BF16)
            high = dots.astype(BF16)
            rest = (dots - high.astype(F32)).astype(BF16)
            lane = lax.broadcasted_iota(jnp.int32, (step, EXTRA), 1)
            out_ref[local, D:] = jnp.where(
                lane == expert, high, jnp.where(lane == expert + E, rest, jnp.zeros_like(rest))
            )


def spread_kernel(ng, n_outer, scal, ngw, dyg, act_ref, ggu_ref, *refs):
    x, g = scal[0], scal[1]
    weights, (other_ref, mine_ref, even_ref, odd_ref, w_full, ca_ref) = refs[:n_outer], refs[n_outer:]
    outer_rows(weights, w_full, x, g, ng)
    rows = ngw.shape[0]
    step = rows // 4

    @pl.loop(0, 4)
    def _(i):
        spot = pl.ds(pl.multiple_of(i * step, 128), step)
        share = own_share(ngw[spot, D:], scal)
        ca_ref[spot, :] = (act_ref[spot, :].astype(F32) * share).astype(BF16)

    cut = D // 6
    for flip, out_ref in ((1, other_ref), (0, mine_ref)):

        @pl.loop(0, 3)
        def _(i):
            cols = pl.ds(pl.multiple_of((x ^ flip) * (D // 2) + i * cut, 128), cut)
            spot = pl.ds(pl.multiple_of(i * cut, 128), cut)
            out_ref[spot, : 2 * HALF] = dot(ngw[:, cols], ggu_ref[...], TN).astype(BF16)
            out_ref[spot, 2 * HALF :] = dot(dyg[:, cols], ca_ref[...], TN).astype(BF16)

    for part, out_ref in enumerate((even_ref, odd_ref)):

        @pl.loop(0, 2)
        def _(i):
            local = pl.ds(pl.multiple_of(i * step, 128), step)
            spot = pl.ds(pl.multiple_of(part * 2 * step + i * step, 128), step)
            share = own_share(ngw[spot, D:], scal)
            out_ref[local, :] = (dot(act_ref[spot, :], w_full[...], NT) * share).astype(BF16)


def pair_kernel(even_ref, odd_ref, *outs):
    rows = outs[0].shape[0]
    for p, out in enumerate(outs):
        spot = slice(p * rows, (p + 1) * rows)
        out[...] = (even_ref[spot, :].astype(F32) + odd_ref[spot, :].astype(F32)).astype(BF16)


def norm_back(grad, values, scale):
    unit = values * scale
    return scale * (grad - unit * jnp.mean(grad * unit, axis=-1, keepdims=True))


def turn_kernel(scal, a0, a1, a2, a3, mixed_ref, cot_ref, comb_ref, wo_ref, rt_ref, *refs):
    t = scal[2]
    (grad_ref, wide_ref), ga_refs = refs[:2], refs[2:]
    rows = mixed_ref.shape[0]
    total = (
        a0[...].astype(F32) + a1[...].astype(F32) + a2[...].astype(F32) + a3[...].astype(F32)
    )
    valid = row_valid(scal, rows)
    lane = lax.broadcasted_iota(jnp.int32, (rows, EXTRA), 1)
    dots = total[:, D:]
    dots = (dots + pltpu.roll(dots, EXTRA - E, 1)) * valid
    comb = comb_ref[...]
    inner = jnp.sum(comb * dots, axis=-1, keepdims=True)
    grad_logits = jnp.where(lane < E, comb * (dots - inner), 0.0).astype(BF16)
    grad_normed = total[:, :D] + dot(grad_logits, rt_ref[...], NT)
    mixed = mixed_ref[...]
    scale = lax.rsqrt(jnp.mean(mixed * mixed, axis=-1, keepdims=True) + 1e-05)
    grad_mixed = cot_ref[...].astype(F32) + norm_back(grad_normed, mixed, scale)
    grad_ref[...] = grad_mixed
    branch = (valid * grad_mixed).astype(BF16)
    wide_ref[:, :D] = branch
    wide_ref[:, D:] = grad_logits
    for k in range(CUBE):
        spot = pl.ds(pl.multiple_of((t ^ k) * QH, 64), QH)
        ga_refs[k][...] = dot(branch, wo_ref[spot, :], NT).astype(BF16)


def attend_back_kernel(slots, n_keys, scal, *refs):
    g, t = scal[1], scal[2]
    q_ref, kv_refs, refs = refs[0], refs[1 : 1 + n_keys], refs[1 + n_keys :]
    ot_ref, lse_ref, refs = refs[0], refs[1], refs[2:]
    ga_refs, refs = refs[:CUBE], refs[CUBE:]
    gq_ref, gkv_refs, (do_ref,) = refs[0], refs[1 : 1 + n_keys], refs[1 + n_keys :]
    extent = q_ref.shape[2]
    causal = causal_bias(slots, extent, t)
    blank = jnp.zeros((slots, HD), BF16)
    place = {k: p for p, k in enumerate(ORDER)}
    for m in range(MB):
        length = scal[3 + m]
        biases = [key_bias(s, slots, extent, g, t, s, length) for s in range(n_keys)]
        sums = [None] * n_keys
        for h in range(GROUP):
            for k in range(CUBE):
                part = ga_refs[k][m * slots : (m + 1) * slots, h * HD : (h + 1) * HD]
                do_ref[k * slots : (k + 1) * slots, :] = jnp.concatenate([blank, part], axis=1)
            q = q_ref[m, h]
            do = do_ref[...]
            dot_t = do.astype(F32).T[HD:, :]
            delta = jnp.sum(dot_t * ot_ref[m, h], axis=0, keepdims=True)
            lse = lse_ref[m, h : h + 1, :]
            grad_q = None
            for s in range(n_keys):
                kv = kv_refs[s][m]
                st = dot(kv, q, NT) * (0.125 * LOG2E) + biases[s]
                if s == 0:
                    st = st + causal
                pt = jnp.exp2(st - lse)
                dpt = dot(kv, do, NT)
                dst = (pt * (dpt - delta) * 0.125).astype(BF16)
                part = dot(dst, q) + dot(pt.astype(BF16), do)
                sums[s] = part if sums[s] is None else sums[s] + part
                part = dot(kv, dst, TN)
                grad_q = part if grad_q is None else grad_q + part
            gq = grad_q[:HD, :].T.astype(BF16)
            for k in range(CUBE):
                base = place[k] * MB * slots + m * slots
                gq_ref[base : base + slots, h * HD : (h + 1) * HD] = gq[k * slots : (k + 1) * slots]
        for s in range(n_keys):
            gkv_refs[s][m] = sums[s].astype(gkv_refs[s].dtype)


def close_kernel(ng, n_outer, n_keys, scal, gq_ref, own_ref, *refs):
    x, g = scal[0], scal[1]
    others, refs = refs[: n_keys - 1], refs[n_keys - 1 :]
    weights, refs = refs[:n_outer], refs[n_outer:]
    xg, even_ref, odd_ref, other_ref, mine_ref, w_full, gqkv = refs
    outer_rows(weights, w_full, x, g, ng)
    rows = xg.shape[0] // CUBE
    slots = rows // MB
    gqkv[:, :QH] = gq_ref[...]
    for p, k in enumerate(ORDER):
        for m in range(MB):
            spot = slice(k * slots, (k + 1) * slots)
            total = own_ref[m, spot, :]
            for other in others:
                total = total + other[m, spot, :].astype(F32)
            base = p * rows + m * slots
            gqkv[base : base + slots, QH:] = total.astype(BF16)
    step = 2 * rows
    for part, out_ref in enumerate((even_ref, odd_ref)):

        @pl.loop(0, 2)
        def _(i):
            local = pl.ds(pl.multiple_of(i * step, 128), step)
            spot = pl.ds(pl.multiple_of(part * 2 * step + i * step, 128), step)
            out_ref[local, :] = dot(gqkv[spot, :], w_full[...], NT).astype(BF16)

    cut = D // 6
    for flip, out_ref in ((1, other_ref), (0, mine_ref)):

        @pl.loop(0, 3)
        def _(i):
            cols = pl.ds(pl.multiple_of((x ^ flip) * (D // 2) + i * cut, 128), cut)
            spot = pl.ds(pl.multiple_of(i * cut, 128), cut)
            out_ref[spot, :] = dot(xg[:, cols], gqkv[...], TN).astype(BF16)


def out_grad_kernel(scal, *refs):
    x = scal[0]
    blocks, refs = refs[:10], refs[10:]
    att_refs, (ngw, other_ref, mine_ref, wide, att) = refs[:CUBE], refs[CUBE:]
    cube_rows(blocks, wide)
    rows = att_refs[0].shape[0]
    for p, k in enumerate(ORDER):
        att[p * rows : (p + 1) * rows, :] = att_refs[k][...]
    cut = D // 6
    for flip, out_ref in ((1, other_ref), (0, mine_ref)):

        @pl.loop(0, 3)
        def _(i):
            cols = pl.ds(pl.multiple_of((x ^ flip) * (D // 2) + i * cut, 128), cut)
            spot = pl.ds(pl.multiple_of(i * cut, 128), cut)
            out_ref[spot, :QH] = dot(wide[:, cols], att[...], TN).astype(BF16)
            out_ref[spot, QH:] = dot(ngw[:, cols], wide[:, D:], TN)[:, : 256 - QH].astype(BF16)


def output_kernel(a0, a1, a2, a3, mixed_ref, out_ref):
    total = (
        a0[...].astype(F32) + a1[...].astype(F32) + a2[...].astype(F32) + a3[...].astype(F32)
    )
    out_ref[...] = (mixed_ref[...] + total).astype(BF16)


def tokens_kernel(a0, a1, a2, a3, x_ref, grad_ref, out_ref):
    total = (
        a0[...].astype(F32) + a1[...].astype(F32) + a2[...].astype(F32) + a3[...].astype(F32)
    )
    x = x_ref[...].astype(F32)
    scale = lax.rsqrt(jnp.mean(x * x, axis=-1, keepdims=True) + 1e-05)
    out_ref[...] = (grad_ref[...] + norm_back(total, x, scale)).astype(BF16)


def pair_sums(links, even, odd):
    rows = even.shape[0] // 4
    outs = [shape((rows, even.shape[1]))] * 4
    sums = kernel_call(pair_kernel, outs, [even, links.cube(odd, 1)], scalars=False)
    return [sums[0]] + [links.cube(part, bits) for part, bits in zip(sums[1:], ORDER[1:4])]


def body(
    tokens,
    lengths,
    routes,
    cotangent,
    attn_gain,
    qkv_weight,
    out_weight,
    moe_gain,
    router,
    gateup_weight,
    down_weight,
):
    nx, nc = lax.axis_size("dp"), lax.axis_size("ctx")
    links = Links(nx, nc)
    ng = links.ng
    n_outer = nx * ng
    x = lax.axis_index("dp")
    ctx = lax.axis_index("ctx")
    g, t = ctx // CUBE, ctx % CUBE
    slots = tokens.shape[2]
    rows = MB * slots
    extent = CUBE * slots
    scal = jnp.stack([x, g, t, lengths[0, 0], lengths[1, 0]]).astype(jnp.int32)
    wr = attn_gain.shape[0]
    out_rows = CUBE * rows

    tok = tokens.reshape(rows, D)
    cot = cotangent.reshape(rows, D)
    tok_f = tok.astype(F32)
    first = lax.rsqrt(jnp.mean(tok_f * tok_f, axis=-1, keepdims=True) + 1e-05)
    unit = (tok_f * first).astype(BF16)

    gain1 = attn_gain.astype(F32)[:, None]
    gain2 = moe_gain.astype(F32)[:, None]
    wq = (qkv_weight.astype(F32) * gain1).astype(BF16)
    wq_parts = jnp.concatenate(
        [
            wq[:, :QW].reshape(wr, CUBE, QH),
            wq[:, QW : QW + KW].reshape(wr, CUBE, HD),
            wq[:, QW + KW :].reshape(wr, CUBE, HD),
        ],
        axis=2,
    ).transpose(1, 0, 2)
    wq_blocks = links.outer_gather(links.swap(wq_parts).reshape(CUBE * wr, SHARD))
    unit_blocks = links.cube_gather(unit)

    gu = (gateup_weight.astype(F32) * gain2[None]).astype(BF16)
    gu_parts = (
        gu.reshape(E, wr, 2, 2, HALF).transpose(0, 3, 1, 2, 4).reshape(CUBE, wr, 2 * HALF)
    )
    dn_parts = down_weight.reshape(CUBE, HALF, wr).transpose(0, 2, 1)
    gu_blocks = links.outer_gather(links.swap(gu_parts).reshape(CUBE * wr, 2 * HALF))
    dn_blocks = links.outer_gather(links.swap(dn_parts).reshape(CUBE * wr, HALF))

    rt_low = (router.astype(F32) * gain2).astype(BF16)
    wo_t = jnp.concatenate(
        [out_weight.T, rt_low, rt_low, jnp.zeros((wr, EXTRA - 2 * E), BF16)], axis=1
    )
    wo_all = lax.all_gather(wo_t, AXES, axis=0, tiled=True)
    wo = wo_all[:, :QW].T
    rt = wo_all[:, QW:]

    xg, q, kv = kernel_call(
        functools.partial(qkv_kernel, ng, n_outer),
        [
            shape((out_rows, D)),
            shape((MB, GROUP, extent, 2 * HD)),
            shape((MB, extent, 2 * HD)),
        ],
        [scal] + unit_blocks + wq_blocks,
        [pltpu.VMEM((D, SHARD), BF16)],
        flops=2 * out_rows * D * SHARD,
    )
    kvs = [kv] + [links.climb(kv, step) for step in range(1, ng)]
    attended = kernel_call(
        functools.partial(attend_kernel, slots),
        [shape((rows, QH))] * CUBE
        + [shape((MB, GROUP, HD, extent), F32), shape((MB, GROUP, extent), F32)],
        [scal, q] + kvs,
        flops=8 * MB * GROUP * extent * extent * 2 * HD * ng,
    )
    att_blocks, (ot, lse) = attended[:CUBE], attended[CUBE:]
    att_own = [att_blocks[0]] + [links.cube(att_blocks[k], k) for k in range(1, CUBE)]
    mixed, wide, comb = kernel_call(
        mix_kernel,
        [shape((rows, D), F32), shape((rows, WIDE)), shape((rows, EXTRA), F32)],
        [scal, tok, routes.reshape(rows, 2), wo, rt] + att_own,
        flops=2 * rows * D * QW,
    )
    cot_blocks = links.cube_gather(cot)
    dyg, back = kernel_call(
        functools.partial(cot_kernel, ng, n_outer),
        [shape((out_rows, D)), shape((out_rows, HALF), F32)],
        [scal] + cot_blocks + dn_blocks,
        [pltpu.VMEM((D, HALF), BF16)],
        flops=2 * out_rows * D * HALF,
    )
    ngw, act, ggu, even, odd = kernel_call(
        functools.partial(expert_kernel, ng, n_outer),
        [
            shape((out_rows, WIDE)),
            shape((out_rows, HALF)),
            shape((out_rows, 2 * HALF)),
            shape((out_rows // 2, WIDE)),
            shape((out_rows // 2, WIDE)),
        ],
        [scal] + links.cube_gather(wide) + gu_blocks + [back],
        [pltpu.VMEM((D, 2 * HALF), BF16)],
        flops=8 * out_rows * D * HALF,
    )
    grad_sums = pair_sums(links, even, odd)
    turned = kernel_call(
        turn_kernel,
        [shape((rows, D), F32), shape((rows, WIDE))] + [shape((rows, QH))] * CUBE,
        [scal] + grad_sums + [mixed, cot, comb, wo, rt],
        flops=2 * rows * D * QW,
    )
    grad_mixed, grad_wide, ga_blocks = turned[0], turned[1], turned[2:]
    ga_heads = [ga_blocks[0]] + [links.cube(ga_blocks[k], k) for k in range(1, CUBE)]

    moe_other, moe_mine, out_even, out_odd = kernel_call(
        functools.partial(spread_kernel, ng, n_outer),
        [
            shape((D // 2, 3 * HALF)),
            shape((D // 2, 3 * HALF)),
            shape((out_rows // 2, D)),
            shape((out_rows // 2, D)),
        ],
        [scal, ngw, dyg, act, ggu] + dn_blocks,
        [pltpu.VMEM((D, HALF), BF16), pltpu.VMEM((out_rows, HALF), BF16)],
        flops=8 * out_rows * D * HALF,
    )
    moe_sum = links.outer_scatter([moe_mine, moe_other], x, g)
    moe_grad = links.swap(moe_sum.astype(BF16).reshape(CUBE, wr, 3 * HALF))

    grads = kernel_call(
        functools.partial(attend_back_kernel, slots, ng),
        [shape((out_rows, QH)), shape((MB, extent, 2 * HD), F32)]
        + [shape((MB, extent, 2 * HD))] * (ng - 1),
        [scal, q] + kvs + [ot, lse] + ga_heads,
        [pltpu.VMEM((extent, 2 * HD), BF16)],
        flops=20 * MB * GROUP * extent * extent * 2 * HD * ng,
    )
    gkv_others = [links.climb(grads[1 + step], -step) for step in range(1, ng)]
    even, odd, qkv_other, qkv_mine = kernel_call(
        functools.partial(close_kernel, ng, n_outer, ng),
        [
            shape((out_rows // 2, D)),
            shape((out_rows // 2, D)),
            shape((D // 2, SHARD)),
            shape((D // 2, SHARD)),
        ],
        [scal, grads[0], grads[1]] + gkv_others + wq_blocks + [xg],
        [pltpu.VMEM((D, SHARD), BF16), pltpu.VMEM((out_rows, SHARD), BF16)],
        flops=4 * out_rows * D * SHARD,
    )
    qkv_sum = links.outer_scatter([qkv_mine, qkv_other], x, g)
    qkv_grad = links.swap(qkv_sum.astype(BF16).reshape(CUBE, wr, SHARD)).astype(F32)
    token_sums = pair_sums(links, even, odd)
    grad_tokens = kernel_call(
        tokens_kernel, [shape((rows, D))], token_sums + [tok, grad_mixed], scalars=False
    )[0]

    wo_other, wo_mine = kernel_call(
        out_grad_kernel,
        [shape((D // 2, 256)), shape((D // 2, 256))],
        [scal] + links.cube_gather(grad_wide) + list(att_blocks) + [ngw],
        [pltpu.VMEM((out_rows, WIDE), BF16), pltpu.VMEM((out_rows, QH), BF16)],
        flops=2 * out_rows * D * 256,
    )
    wo_sum = links.outer_scatter([wo_mine, wo_other], x, g)
    wo_grad = links.swap(wo_sum.astype(BF16).reshape(CUBE, wr, 256)).astype(F32)

    output = kernel_call(
        output_kernel,
        [shape((rows, D))],
        pair_sums(links, out_even, out_odd) + [mixed],
        scalars=False,
    )[0]

    qkv_unit = jnp.concatenate(
        [
            qkv_grad[:, :, :QH].transpose(1, 0, 2).reshape(wr, QW),
            qkv_grad[:, :, QH : QH + HD].transpose(1, 0, 2).reshape(wr, KW),
            qkv_grad[:, :, QH + HD :].transpose(1, 0, 2).reshape(wr, KW),
        ],
        axis=1,
    )
    grad_attn_gain = jnp.sum(qkv_unit * qkv_weight.astype(F32), axis=1)
    grad_out = wo_grad[:, :, :QH].transpose(0, 2, 1).reshape(QW, wr)
    router_unit = wo_grad[0, :, QH : QH + E]
    moe_f = moe_grad.astype(F32)
    gu_unit = (
        moe_f[:, :, : 2 * HALF]
        .reshape(E, 2, wr, 2, HALF)
        .transpose(0, 2, 3, 1, 4)
        .reshape(E, wr, 2 * FF)
    )
    grad_down = moe_f[:, :, 2 * HALF :].transpose(0, 2, 1).reshape(E, FF, wr)
    grad_moe_gain = jnp.sum(gu_unit * gateup_weight.astype(F32), axis=(0, 2)) + jnp.sum(
        router_unit * router.astype(F32), axis=1
    )
    return (
        output.reshape(MB, 1, slots, D),
        grad_tokens.reshape(MB, 1, slots, D),
        grad_attn_gain,
        qkv_unit * gain1,
        grad_out,
        grad_moe_gain,
        router_unit * gain2,
        gu_unit * gain2[None],
        grad_down,
    )


def solution(mesh):
    in_specs = (
        P(None, "dp", "ctx", None),
        P(None, "dp"),
        P(None, "dp", "ctx", None),
        P(None, "dp", "ctx", None),
        P(("dp", "ctx")),
        P(("dp", "ctx"), None),
        P(None, ("dp", "ctx")),
        P(("dp", "ctx")),
        P(("dp", "ctx"), None),
        P(None, ("dp", "ctx"), None),
        P(None, None, ("dp", "ctx")),
    )
    out_specs = (
        P(None, "dp", "ctx", None),
        P(None, "dp", "ctx", None),
        P(("dp", "ctx")),
        P(("dp", "ctx"), None),
        P(None, ("dp", "ctx")),
        P(("dp", "ctx")),
        P(("dp", "ctx"), None),
        P(None, ("dp", "ctx"), None),
        P(None, None, ("dp", "ctx")),
    )
    return jax.shard_map(body, mesh=mesh, in_specs=in_specs, out_specs=out_specs, check_vma=False)
```

time: 2150 us -> 522 us (0.24)
  waiting for transfers between devices: 1250 us -> 210 us
  matrix products: 316 us -> 0 us
  local copies, waits for them, and re-layouts: 334 us -> 60.6 us
  blocking collectives: 123 us -> 0 us
  starting transfers between devices: 1.14 us -> 107 us
  Pallas kernels: 0 us -> 105 us
  other arithmetic: 81.2 us -> 17.7 us
    reduce_scatter x6 -> x0, waiting for transfers between devices: 981 us -> none  [the longest x1 438 us: body(): lax.psum_scatter(jnp.stack(acc_gateup, axis=1), ('dp', 'ctx'), scatter_di...]
    dot_general x178 -> x0, matrix products: 316 us -> none  [the longest x8 51.1 us: body(): jnp.dot(normed.T, grad_gate_up, preferred_element_type=jnp.float32)]
    all_gather x6 -> x1, waiting for transfers between devices: 271 us -> 0.01 us  [body(): wo_all = lax.all_gather(wo_t, AXES, axis=0, tiled=True)]
    dynamic_update_slice x48 -> x0, local copies, waits for them, and re-layouts: 252 us -> none  [the longest x32 243 us: attend_backward(): lax.map(one_pair, (queries, kv_pairs, row_maxes, row_sums, grad_pairs))]
    ppermute x0 -> x79, waiting for transfers between devices: none -> 193 us  [the longest x15 112 us: outer(): lax.ppermute(value, AXES, self._pairs(lambda x, g, t: (x ^ dx, g ^ dg, t)))]
    pallas_call x0 -> x15, Pallas kernels: none -> 105 us  [kernel_call(): pl.pallas_call(kernel, out_shape=list(outs), in_specs=specs, out_specs=[v...]
    ppermute x0 -> x79, starting transfers between devices: none -> 84.8 us  [the longest x62 52 us: cube(): lax.ppermute(value, AXES, self._pairs(lambda x, g, t: (x, g, t ^ bits)))]
    unnamed x2 -> x0, blocking collectives: 83.5 us -> none
  transfers between devices with their start and end apart: 13 -> 86, of which waited for: 9 -> 24; matrix products, arithmetic and copies ran while one was open for 21% -> 10% of each run, Pallas kernels for 0% -> 18%
where the time goes in v1:
time: 522 us; the launch traced here: 516 us
  waiting for transfers between devices  210 us (40%)
  starting transfers between devices  107 us (20%)
  Pallas kernels  105 us (20%)
  local copies, waits for them, and re-layouts  60.6 us (12%)
  other arithmetic  17.7 us (3%)
  between operations  15.2 us (3%)
    ppermute x15, waiting for transfers between devices, outer(): lax.ppermute(value, AXES, self._pairs(lambda x, g, t: (x ^ dx, g ^ dg, t)))  112 us
    pallas_call x15, Pallas kernels, kernel_call(): pl.pallas_call(kernel, out_shape=list(outs), in_specs=specs, out_specs=[v...  105 us
    ppermute x62, waiting for transfers between devices, cube(): lax.ppermute(value, AXES, self._pairs(lambda x, g, t: (x, g, t ^ bits)))  66.5 us
    ppermute x62, starting transfers between devices, cube(): lax.ppermute(value, AXES, self._pairs(lambda x, g, t: (x, g, t ^ bits)))  52 us
    ppermute x15, starting transfers between devices, outer(): lax.ppermute(value, AXES, self._pairs(lambda x, g, t: (x ^ dx, g ^ dg, t)))  25.5 us
    all_to_all x6, starting transfers between devices, swap(): lax.all_to_all(value, AXES, split_axis=0, concat_axis=0, tiled=True, axis...  22 us
    all_to_all x6, waiting for transfers between devices, swap(): lax.all_to_all(value, AXES, split_axis=0, concat_axis=0, tiled=True, axis...  16.8 us
    ppermute x2, waiting for transfers between devices, climb(): return lax.ppermute(value, AXES, self._pairs(move))  15.3 us
  transfers between devices with their start and end apart: 86, of which 24 were waited for; matrix products, arithmetic and copies ran while one was open for 10% of the time, Pallas kernels for 18%

profile of v1, /device:TPU:0, one launch (start us, length us, event | category | flops | bytes accessed | tf_op | source)
XLA Modules:
  0.0 515.6 jit_solution(5935361056329252303)
XLA Ops:
  25.3 5.5 %all-to-all-done = bf16[8,48,320]{2,1,0:T(8,128)(2,1)S(1)} async-done(((bf16[8,48,320]{2,1,0:T(8,128)(2,1)}), bf16[8,48,320]{2,1,0:T(8,128)(2,1)S(1)}, u32[]{:S(2)}, u32[]{:S(2)}) %all-to-all-start) | async-done | bytes 245792 | tf_op jit(solution)/shard_map/all_to_all | solution.py:97
  44.5 6.4 %collective-permute-done.2.refs_3_ = bf16[64,1536]{1,0:T(8,128)(2,1)S(1)} collective-permute-done((bf16[64,1536]{1,0:T(8,128)(2,1)S(1)}, bf16[64,1536]{1,0:T(8,128)(2,1)S(1)}, u32[]{:S(2)}, u32[]{:S(2)}) %collective-permute-start.2) | collective-permute-done | bytes 196640 | tf_op jit(solution)/shard_map/ppermute | solution.py:78
  50.9 12.6 %collective-permute-done.3.refs_4_ = bf16[64,1536]{1,0:T(8,128)(2,1)S(1)} collective-permute-done((bf16[64,1536]{1,0:T(8,128)(2,1)S(1)}, bf16[64,1536]{1,0:T(8,128)(2,1)S(1)}, u32[]{:S(2)}, u32[]{:S(2)}) %collective-permute-start.3) | collective-permute-done | bytes 196640 | tf_op jit(solution)/shard_map/ppermute | solution.py:78
  71.0 7.6 %collective-permute-done.11.refs_13_.refs_4_ = bf16[384,320]{1,0:T(8,128)(2,1)} collective-permute-done((bf16[384,320]{1,0:T(8,128)(2,1)S(1)}, bf16[384,320]{1,0:T(8,128)(2,1)}, u32[]{:S(2)}, u32[]{:S(2)}) %collective-permute-start.11) | collective-permute-done | bytes 245792 | tf_op jit(solution)/shard_map/ppermute | solution.py:81
  78.6 5.9 %shard_map.178 = (bf16[1024,1536]{1,0:T(8,128)(2,1)}, bf16[2,3,512,128]{3,2,1,0:T(8,128)(2,1)}, bf16[2,512,128]{2,1,0:T(8,128)(2,1)}) custom-call(s32[5]{0:T(128)} %stack.15.scal, bf16[128,1536]{1,0:T(8,128)(2,1)} %copy-done.4, bf16[128,1536]{1,0:T(8,128)(2,1)} %collective-permute-done.refs_1_, bf16[128,1536]{1,0:T(8,128)(2,1)} %collective-permute-done.1.refs_2_, ...), custom_call_target="tpu_custom_call" | custom-call | flops 1006632960 | bytes 8323092 | tf_op jit(solution)/shard_map/pallas_call | solution.py:47
  84.5 6.0 %collective-permute-start.12 = (bf16[2,512,128]{2,1,0:T(8,128)(2,1)}, bf16[2,512,128]{2,1,0:T(8,128)(2,1)S(1)}, u32[]{:S(2)}, u32[]{:S(2)}) collective-permute-start(bf16[2,512,128]{2,1,0:T(8,128)(2,1)} %get-tuple-element.68.refs_1_), channel_id=1, source_target_pairs={{0,8},{1,9},{2,10},{3,11},{4,12},{5,13},{6,14},{7,15},{16,24},{17,... | collective-permute-start | bytes 786440 | tf_op jit(solution)/shard_map/ppermute | solution.py:87
  98.3 8.4 %shard_map.179 = (bf16[128,192]{1,0:T(8,128)(2,1)}, bf16[128,192]{1,0:T(8,128)(2,1)}, bf16[128,192]{1,0:T(8,128)(2,1)}, bf16[128,192]{1,0:T(8,128)(2,1)}, bf16[1...) custom-call(s32[5]{0:T(128)} %stack.15.scal, ...), custom_call_target="tpu_custom_call" | custom-call | flops 3221225472 | bytes 2502676 | tf_op jit(solution)/shard_map/pallas_call | solution.py:47
  109.2 5.4 %collective-permute-start.16 = (bf16[128,192]{1,0:T(8,128)(2,1)}, bf16[128,192]{1,0:T(8,128)(2,1)S(1)}, u32[]{:S(2)}, u32[]{:S(2)}) collective-permute-start(bf16[128,192]{1,0:T(8,128)(2,1)} %get-tuple-element.73.refs_14_), channel_id=1, source_target_pairs={{0,4},{1,5},{2,6},{3,7},{4,0},{5,1},{6,2},{7,3},{8,12},{9,13},{10,... | collective-permute-start | bytes 147464 | tf_op jit(solution)/shard_map/ppermute | solution.py:78
  127.8 4.7 slice_bitcast_fusion
  132.6 6.6 %copy.83.wo_ref = bf16[1536,1536]{1,0:T(8,128)(2,1)} copy(bf16[1536,1536]{0,1:T(8,128)(2,1)} %slice_bitcast_fusion) | data formatting | bytes 9437184 | tf_op jit(solution)/shard_map/transpose | solution.py:569
  141.0 5.0 shard_map.180
  152.6 19.0 %collective-permute-done.29.refs_11_ = bf16[384,1024]{1,0:T(8,128)(2,1)} collective-permute-done((bf16[384,1024]{1,0:T(8,128)(2,1)S(1)}, bf16[384,1024]{1,0:T(8,128)(2,1)}, u32[]{:S(2)}, u32[]{:S(2)}) %collective-permute-start.29) | collective-permute-done | bytes 786464 | tf_op jit(solution)/shard_map/ppermute | solution.py:81
  174.2 5.3 %collective-permute-done.41.refs_11_.refs_1_ = bf16[384,512]{1,0:T(8,128)(2,1)S(1)} collective-permute-done((bf16[384,512]{1,0:T(8,128)(2,1)S(1)}, bf16[384,512]{1,0:T(8,128)(2,1)S(1)}, u32[]{:S(2)}, u32[]{:S(2)}) %collective-permute-start.41) | collective-permute-done | bytes 393248 | tf_op jit(solution)/shard_map/ppermute | solution.py:81
  184.1 17.2 %collective-permute-done.42.refs_12_.refs_2_ = bf16[384,512]{1,0:T(8,128)(2,1)S(1)} collective-permute-done((bf16[384,512]{1,0:T(8,128)(2,1)S(1)}, bf16[384,512]{1,0:T(8,128)(2,1)S(1)}, u32[]{:S(2)}, u32[]{:S(2)}) %collective-permute-start.42) | collective-permute-done | bytes 393248 | tf_op jit(solution)/shard_map/ppermute | solution.py:81
  202.9 5.0 collective-permute-done.43.refs_13_.refs_3_
  213.9 6.9 %shard_map.181 = (bf16[1024,1536]{1,0:T(8,128)(2,1)}, f32[1024,512]{1,0:T(8,128)}) custom-call(s32[5]{0:T(128)} %stack.15.scal, bf16[128,1536]{1,0:T(8,128)(2,1)} %bitcast.90, bf16[128,1536]{1,0:T(8,128)(2,1)} %collective-permute-done.32.refs_1_, bf16[128,1536]{1,0:T(8,128)(2,1)} %collective-permute-done.33.refs_2_, bf16[64,1536]{1,0:T(8,128)(2,1)} %copy-done.55, ...), custom_call_target="tpu_custom_call" | custom-call | flops 1610612736 | bytes 9961492 | tf_op jit(solution)/shard_map/pallas_call | solution.py:47
  222.0 13.7 %shard_map.182 = (bf16[1024,1664]{1,0:T(8,128)(2,1)}, bf16[1024,512]{1,0:T(8,128)(2,1)}, bf16[1024,1024]{1,0:T(8,128)(2,1)}, bf16[512,1664]{1,0:T(8,128)(2,1)}, bf16[512,1664]{1,0:T(8,128)(2,1)}) custom-call(s32[5]{0:T(128)} %stack.15.scal, bf16[128,1664]{1,0:T(8,128)(2,1)} %get-tuple-element.77.refs_0_, bf16[128,1664]{1,0:T(8,128)(2,1)} %copy-done.28, ...), custom_call_target="tpu_custom_call" | custom-call | flops 6442450944 | bytes 18612244 | tf_op jit(solution)/shard_map/pallas_call | solution.py:47
  236.2 16.0 %shard_map.183 = (bf16[768,1536]{1,0:T(8,128)(2,1)}, bf16[768,1536]{1,0:T(8,128)(2,1)}, bf16[512,1536]{1,0:T(8,128)(2,1)}, bf16[512,1536]{1,0:T(8,128)(2,1)}) custom-call(s32[5]{0:T(128)} %stack.15.scal, bf16[1024,1664]{1,0:T(8,128)(2,1)} %get-tuple-element.79.ngw.refs_18_, bf16[1024,1536]{1,0:T(8,128)(2,1)} %get-tuple-element.80.dyg, ...), custom_call_target="tpu_custom_call" | custom-call | flops 6442450944 | bytes 19136532 | tf_op jit(solution)/shard_map/pallas_call | solution.py:47
  262.1 9.3 %collective-permute-done.49.a1 = bf16[128,1664]{1,0:T(8,128)(2,1)S(1)} collective-permute-done((bf16[128,1664]{1,0:T(8,128)(2,1)}, bf16[128,1664]{1,0:T(8,128)(2,1)S(1)}, u32[]{:S(2)}, u32[]{:S(2)}) %collective-permute-start.49) | collective-permute-done | bytes 426016 | tf_op jit(solution)/shard_map/ppermute | solution.py:78
  271.4 8.0 %collective-permute-done.50.a2 = bf16[128,1664]{1,0:T(8,128)(2,1)S(1)} collective-permute-done((bf16[128,1664]{1,0:T(8,128)(2,1)}, bf16[128,1664]{1,0:T(8,128)(2,1)S(1)}, u32[]{:S(2)}, u32[]{:S(2)}) %collective-permute-start.50) | collective-permute-done | bytes 426016 | tf_op jit(solution)/shard_map/ppermute | solution.py:78
  281.7 6.0 %shard_map.187 = (f32[128,1536]{1,0:T(8,128)}, bf16[128,1664]{1,0:T(8,128)(2,1)}, bf16[128,192]{1,0:T(8,128)(2,1)}, bf16[128,192]{1,0:T(8,128)(2,1)}, bf16[128,1...) custom-call(s32[5]{0:T(128)} %stack.15.scal, ...), custom_call_target="tpu_custom_call" | custom-call | flops 603979776 | bytes 9666580 | tf_op jit(solution)/shard_map/pallas_call | solution.py:47
  300.8 10.3 %shard_map.188 = (bf16[1024,192]{1,0:T(8,128)(2,1)}, f32[2,512,128]{2,1,0:T(8,128)}, bf16[2,512,128]{2,1,0:T(8,128)(2,1)}) custom-call(s32[5]{0:T(128)} %stack.15.scal, bf16[2,3,512,128]{3,2,1,0:T(8,128)(2,1)} %get-tuple-element.67.refs_0_, bf16[2,512,128]{2,1,0:T(8,128)(2,1)} %get-tuple-element.68.refs_1_, bf16[2,512,128]{2,1,0:T(8,128)(2,1)} %copy-done.49, ...), custom_call_target="tpu_custom_call" | custom-call | flops 8053063680 | bytes 3682324 | tf_op jit(solution)/shard_map/pallas_call | solution.py:47
  315.3 11.8 %collective-permute-done.59.refs_0_ = bf16[2,512,128]{2,1,0:T(8,128)(2,1)S(1)} collective-permute-done((bf16[2,512,128]{2,1,0:T(8,128)(2,1)}, bf16[2,512,128]{2,1,0:T(8,128)(2,1)S(1)}, u32[]{:S(2)}, u32[]{:S(2)}) %collective-permute-start.59) | collective-permute-done | bytes 262176 | tf_op jit(solution)/shard_map/ppermute | solution.py:87
  327.8 10.3 %shard_map.189 = (bf16[512,1536]{1,0:T(8,128)(2,1)}, bf16[512,1536]{1,0:T(8,128)(2,1)}, bf16[768,320]{1,0:T(8,128)(2,1)}, bf16[768,320]{1,0:T(8,128)(2,1)}) custom-call(s32[5]{0:T(128)} %stack.15.scal, bf16[1024,192]{1,0:T(8,128)(2,1)} %get-tuple-element.107.gq_ref, f32[2,512,128]{2,1,0:T(8,128)} %get-tuple-element.108.own_ref, ...), custom_call_target="tpu_custom_call" | custom-call | flops 2013265920 | bytes 9437204 | tf_op jit(solution)/shard_map/pallas_call | solution.py:47
  348.5 4.9 collective-permute-done.64
  356.8 7.5 %shard_map.192 = (bf16[768,256]{1,0:T(8,128)(2,1)}, bf16[768,256]{1,0:T(8,128)(2,1)}) custom-call(s32[5]{0:T(128)} %stack.15.scal, bf16[128,1664]{1,0:T(8,128)(2,1)} %get-tuple-element.120.refs_0_, bf16[128,1664]{1,0:T(8,128)(2,1)} %copy-done.8, bf16[128,1664]{1,0:T(8,128)(2,1)} %collective-permute-done.67.refs_2_, ...), custom_call_target="tpu_custom_call" | custom-call | flops 805306368 | bytes 7995412 | tf_op jit(solution)/shard_map/pallas_call | solution.py:47
  367.8 7.4 %collective-permute-done.75 = bf16[768,256]{1,0:T(8,128)(2,1)S(1)} collective-permute-done((bf16[768,256]{1,0:T(8,128)(2,1)}, bf16[768,256]{1,0:T(8,128)(2,1)S(1)}, u32[]{:S(2)}, u32[]{:S(2)}) %collective-permute-start.75) | collective-permute-done | bytes 393248 | tf_op jit(solution)/shard_map/ppermute | solution.py:81
  378.1 45.2 %collective-permute-done.65 = bf16[384,320]{1,0:T(8,128)(2,1)S(1)} collective-permute-done((bf16[384,320]{1,0:T(8,128)(2,1)S(1)}, bf16[384,320]{1,0:T(8,128)(2,1)S(1)}, u32[]{:S(2)}, u32[]{:S(2)}) %collective-permute-start.65) | collective-permute-done | bytes 245792 | tf_op jit(solution)/shard_map/ppermute | solution.py:81
  435.8 4.1 all-to-all-start.4
  442.9 11.3 %all-to-all-done.4 = bf16[8,48,256]{2,1,0:T(8,128)(2,1)S(1)} async-done(((bf16[8,48,256]{2,1,0:T(8,128)(2,1)}), bf16[8,48,256]{2,1,0:T(8,128)(2,1)S(1)}, u32[]{:S(2)}, u32[]{:S(2)}) %all-to-all-start.4) | async-done | bytes 196640 | tf_op jit(solution)/shard_map/all_to_all | solution.py:97
  476.6 6.0 %collective-permute-done.61.a1 = bf16[128,1536]{1,0:T(8,128)(2,1)S(1)} collective-permute-done((bf16[128,1536]{1,0:T(8,128)(2,1)}, bf16[128,1536]{1,0:T(8,128)(2,1)S(1)}, u32[]{:S(2)}, u32[]{:S(2)}) %collective-permute-start.61) | collective-permute-done | bytes 393248 | tf_op jit(solution)/shard_map/ppermute | solution.py:78
  482.6 9.4 %collective-permute-done.62.a2 = bf16[128,1536]{1,0:T(8,128)(2,1)} collective-permute-done((bf16[128,1536]{1,0:T(8,128)(2,1)}, bf16[128,1536]{1,0:T(8,128)(2,1)}, u32[]{:S(2)}, u32[]{:S(2)}) %collective-permute-start.62) | collective-permute-done | bytes 393248 | tf_op jit(solution)/shard_map/ppermute | solution.py:78
  (371 shorter events, 191.5 us)
Async XLA Ops:
  7.2 120.6 %all-gather.2.cloned.1.call-start = ((), (), s32[]{:S(2)}) async-start(), calls=%async_computation.6 | async-start | bytes 5271552 | tf_op jit(solution)/shard_map/all_gather | solution.py:568
  15.9 24.6 %collective-permute-start.1 = (bf16[128,1536]{1,0:T(8,128)(2,1)S(1)}, bf16[128,1536]{1,0:T(8,128)(2,1)}, u32[]{:S(2)}, u32[]{:S(2)}) collective-permute-start(bf16[128,1536]{1,0:T(8,128)(2,1)S(1)} %multiply_convert_fusion.refs_0_), channel_id=1, source_target_pairs={{0,2},{1,3},{2,0},{3,1},{4,6},{5,7},{6,4},{7,5},{8,10},{9,11},{10,... | collective-permute-start | bytes 1179656 | tf_op jit(solution)/shard_map/ppermute | solution.py:78
  17.5 27.0 %collective-permute-start.4 = (bf16[128,1536]{1,0:T(8,128)(2,1)S(1)}, bf16[128,1536]{1,0:T(8,128)(2,1)}, u32[]{:S(2)}, u32[]{:S(2)}) collective-permute-start(bf16[128,1536]{1,0:T(8,128)(2,1)S(1)} %multiply_convert_fusion.refs_0_), channel_id=1, source_target_pairs={{0,1},{1,0},{2,3},{3,2},{4,5},{5,4},{6,7},{7,6},{8,9},{9,8},{10,11... | collective-permute-start | bytes 1179656 | tf_op jit(solution)/shard_map/ppermute | solution.py:78
  30.8 89.0 %all-to-all-start.1 = ((bf16[8,48,1024]{2,1,0:T(8,128)(2,1)}), bf16[8,48,1024]{2,1,0:T(8,128)(2,1)S(1)}, u32[]{:S(2)}, u32[]{:S(2)}) async-start(bf16[8,48,1024]{2,1,0:T(8,128)(2,1)} %reshape.128), calls=%async_computation.1 | async-start | bytes 1572864 | tf_op jit(solution)/shard_map/all_to_all | solution.py:97
  37.5 26.0 %collective-permute-start.9 = (bf16[384,320]{1,0:T(8,128)(2,1)S(1)}, bf16[384,320]{1,0:T(8,128)(2,1)S(1)}, u32[]{:S(2)}, u32[]{:S(2)}) collective-permute-start(bf16[384,320]{1,0:T(8,128)(2,1)S(1)} %bitcast.83), channel_id=1, source_target_pairs={{0,8},{1,9},{2,10},{3,11},{4,12},{5,13},{6,14},{7,15},{8,0},{9,1},... | collective-permute-start | bytes 737288 | tf_op jit(solution)/shard_map/ppermute | solution.py:81
  44.5 26.4 %collective-permute-start.5 = (bf16[128,1536]{1,0:T(8,128)(2,1)}, bf16[128,1536]{1,0:T(8,128)(2,1)S(1)}, u32[]{:S(2)}, u32[]{:S(2)}) collective-permute-start(bf16[128,1536]{1,0:T(8,128)(2,1)} %collective-permute-done.refs_1_), channel_id=1, source_target_pairs={{0,1},{1,0},{2,3},{3,2},{4,5},{5,4},{6,7},{7,6},{8,9},{9,8},{10,11... | collective-permute-start | bytes 1179656 | tf_op jit(solution)/shard_map/ppermute | solution.py:78
  65.5 25.0 %collective-permute-start.32 = (bf16[128,1536]{1,0:T(8,128)(2,1)S(1)}, bf16[128,1536]{1,0:T(8,128)(2,1)}, u32[]{:S(2)}, u32[]{:S(2)}) collective-permute-start(bf16[128,1536]{1,0:T(8,128)(2,1)S(1)} %bitcast.92), channel_id=1, source_target_pairs={{0,4},{1,5},{2,6},{3,7},{4,0},{5,1},{6,2},{7,3},{8,12},{9,13},{10,... | collective-permute-start | bytes 1179656 | tf_op jit(solution)/shard_map/ppermute | solution.py:78
  66.9 26.2 %collective-permute-start.33 = (bf16[128,1536]{1,0:T(8,128)(2,1)S(1)}, bf16[128,1536]{1,0:T(8,128)(2,1)}, u32[]{:S(2)}, u32[]{:S(2)}) collective-permute-start(bf16[128,1536]{1,0:T(8,128)(2,1)S(1)} %bitcast.93), channel_id=1, source_target_pairs={{0,2},{1,3},{2,0},{3,1},{4,6},{5,7},{6,4},{7,5},{8,10},{9,11},{10,... | collective-permute-start | bytes 1179656 | tf_op jit(solution)/shard_map/ppermute | solution.py:78
  119.2 26.8 %collective-permute-start.36 = (bf16[128,1536]{1,0:T(8,128)(2,1)S(1)}, bf16[128,1536]{1,0:T(8,128)(2,1)S(1)}, u32[]{:S(2)}, u32[]{:S(2)}) collective-permute-start(bf16[128,1536]{1,0:T(8,128)(2,1)S(1)} %bitcast.94), channel_id=1, source_target_pairs={{0,1},{1,0},{2,3},{3,2},{4,5},{5,4},{6,7},{7,6},{8,9},{9,8},{10,11... | collective-permute-start | bytes 1179656 | tf_op jit(solution)/shard_map/ppermute | solution.py:78
  119.9 30.0 %all-to-all-start.2 = ((bf16[8,48,512]{2,1,0:T(8,128)(2,1)}), bf16[8,48,512]{2,1,0:T(8,128)(2,1)S(1)}, u32[]{:S(2)}, u32[]{:S(2)}) async-start(bf16[8,48,512]{2,1,0:T(8,128)(2,1)} %copy.86), calls=%async_computation.2 | async-start | bytes 786432 | tf_op jit(solution)/shard_map/all_to_all | solution.py:97
  123.5 26.5 %collective-permute-start.37 = (bf16[128,1536]{1,0:T(8,128)(2,1)}, bf16[128,1536]{1,0:T(8,128)(2,1)}, u32[]{:S(2)}, u32[]{:S(2)}) collective-permute-start(bf16[128,1536]{1,0:T(8,128)(2,1)} %collective-permute-done.32.refs_1_), channel_id=1, source_target_pairs={{0,1},{1,0},{2,3},{3,2},{4,5},{5,4},{6,7},{7,6},{8,9},{9,8},{10,11... | collective-permute-start | bytes 1179656 | tf_op jit(solution)/shard_map/ppermute | solution.py:78
  124.1 25.8 %collective-permute-start.40 = (bf16[64,1536]{1,0:T(8,128)(2,1)}, bf16[64,1536]{1,0:T(8,128)(2,1)}, u32[]{:S(2)}, u32[]{:S(2)}) collective-permute-start(bf16[64,1536]{1,0:T(8,128)(2,1)} %copy-done.56), channel_id=1, source_target_pairs={{0,1},{1,0},{2,3},{3,2},{4,5},{5,4},{6,7},{7,6},{8,9},{9,8},{10,11... | collective-permute-start | bytes 589832 | tf_op jit(solution)/shard_map/ppermute | solution.py:78
  124.6 47.1 %collective-permute-start.29 = (bf16[384,1024]{1,0:T(8,128)(2,1)S(1)}, bf16[384,1024]{1,0:T(8,128)(2,1)}, u32[]{:S(2)}, u32[]{:S(2)}) collective-permute-start(bf16[384,1024]{1,0:T(8,128)(2,1)S(1)} %bitcast.87), channel_id=1, source_target_pairs={{0,8},{1,9},{2,10},{3,11},{4,12},{5,13},{6,14},{7,15},{8,0},{9,1},... | collective-permute-start | bytes 2359304 | tf_op jit(solution)/shard_map/ppermute | solution.py:81
  146.7 32.7 %collective-permute-start.20 = (bf16[128,1664]{1,0:T(8,128)(2,1)}, bf16[128,1664]{1,0:T(8,128)(2,1)S(1)}, u32[]{:S(2)}, u32[]{:S(2)}) collective-permute-start(bf16[128,1664]{1,0:T(8,128)(2,1)} %get-tuple-element.77.refs_0_), channel_id=1, source_target_pairs={{0,4},{1,5},{2,6},{3,7},{4,0},{5,1},{6,2},{7,3},{8,12},{9,13},{10,... | collective-permute-start | bytes 1277960 | tf_op jit(solution)/shard_map/ppermute | solution.py:78
  148.4 33.6 %collective-permute-start.21 = (bf16[128,1664]{1,0:T(8,128)(2,1)}, bf16[128,1664]{1,0:T(8,128)(2,1)S(1)}, u32[]{:S(2)}, u32[]{:S(2)}) collective-permute-start(bf16[128,1664]{1,0:T(8,128)(2,1)} %get-tuple-element.77.refs_0_), channel_id=1, source_target_pairs={{0,2},{1,3},{2,0},{3,1},{4,6},{5,7},{6,4},{7,5},{8,10},{9,11},{10,... | collective-permute-start | bytes 1277960 | tf_op jit(solution)/shard_map/ppermute | solution.py:78
  149.9 29.5 %collective-permute-start.41 = (bf16[384,512]{1,0:T(8,128)(2,1)S(1)}, bf16[384,512]{1,0:T(8,128)(2,1)S(1)}, u32[]{:S(2)}, u32[]{:S(2)}) collective-permute-start(bf16[384,512]{1,0:T(8,128)(2,1)S(1)} %bitcast.96), channel_id=1, source_target_pairs={{0,8},{1,9},{2,10},{3,11},{4,12},{5,13},{6,14},{7,15},{8,0},{9,1},... | collective-permute-start | bytes 1179656 | tf_op jit(solution)/shard_map/ppermute | solution.py:81
  150.0 59.3 %collective-permute-start.30 = (bf16[384,1024]{1,0:T(8,128)(2,1)S(1)}, bf16[384,1024]{1,0:T(8,128)(2,1)S(1)}, u32[]{:S(2)}, u32[]{:S(2)}) collective-permute-start(bf16[384,1024]{1,0:T(8,128)(2,1)S(1)} %bitcast.88), channel_id=1, source_target_pairs={{0,16},{1,17},{2,18},{3,19},{4,20},{5,21},{6,22},{7,23},{8,24},{9,... | collective-permute-start | bytes 2359304 | tf_op jit(solution)/shard_map/ppermute | solution.py:81
  171.6 37.7 %collective-permute-start.31 = (bf16[384,1024]{1,0:T(8,128)(2,1)}, bf16[384,1024]{1,0:T(8,128)(2,1)S(1)}, u32[]{:S(2)}, u32[]{:S(2)}) collective-permute-start(bf16[384,1024]{1,0:T(8,128)(2,1)} %collective-permute-done.29.refs_11_), channel_id=1, source_target_pairs={{0,16},{1,17},{2,18},{3,19},{4,20},{5,21},{6,22},{7,23},{8,24},{9,... | collective-permute-start | bytes 2359304 | tf_op jit(solution)/shard_map/ppermute | solution.py:81
  182.8 25.1 %collective-permute-start.43 = (bf16[384,512]{1,0:T(8,128)(2,1)S(1)}, bf16[384,512]{1,0:T(8,128)(2,1)S(1)}, u32[]{:S(2)}, u32[]{:S(2)}) collective-permute-start(bf16[384,512]{1,0:T(8,128)(2,1)S(1)} %collective-permute-done.41.refs_11_.refs_1_), channel_id=1, source_target_pairs={{0,16},{1,17},{2,18},{3,19},{4,20},{5,21},{6,22},{7,23},{8,24},{9,... | collective-permute-start | bytes 1179656 | tf_op jit(solution)/shard_map/ppermute | solution.py:81
  183.9 36.9 %collective-permute-start.24 = (bf16[128,1664]{1,0:T(8,128)(2,1)}, bf16[128,1664]{1,0:T(8,128)(2,1)S(1)}, u32[]{:S(2)}, u32[]{:S(2)}) collective-permute-start(bf16[128,1664]{1,0:T(8,128)(2,1)} %get-tuple-element.77.refs_0_), channel_id=1, source_target_pairs={{0,1},{1,0},{2,3},{3,2},{4,5},{5,4},{6,7},{7,6},{8,9},{9,8},{10,11... | collective-permute-start | bytes 1277960 | tf_op jit(solution)/shard_map/ppermute | solution.py:78
  252.2 89.4 %collective-permute-start.77 = (bf16[768,1536]{1,0:T(8,128)(2,1)}, bf16[768,1536]{1,0:T(8,128)(2,1)}, u32[]{:S(2)}, u32[]{:S(2)}) collective-permute-start(bf16[768,1536]{1,0:T(8,128)(2,1)} %get-tuple-element.124), channel_id=1, source_target_pairs={{0,16},{1,17},{2,18},{3,19},{4,20},{5,21},{6,22},{7,23},{8,24},{9,... | collective-permute-start | bytes 7077896 | tf_op jit(solution)/shard_map/ppermute | solution.py:81
  312.4 27.9 %collective-permute-start.67 = (bf16[128,1664]{1,0:T(8,128)(2,1)}, bf16[128,1664]{1,0:T(8,128)(2,1)}, u32[]{:S(2)}, u32[]{:S(2)}) collective-permute-start(bf16[128,1664]{1,0:T(8,128)(2,1)} %get-tuple-element.120.refs_0_), channel_id=1, source_target_pairs={{0,2},{1,3},{2,0},{3,1},{4,6},{5,7},{6,4},{7,5},{8,10},{9,11},{10,... | collective-permute-start | bytes 1277960 | tf_op jit(solution)/shard_map/ppermute | solution.py:78
  312.4 29.3 %collective-permute-start.70 = (bf16[128,1664]{1,0:T(8,128)(2,1)}, bf16[128,1664]{1,0:T(8,128)(2,1)}, u32[]{:S(2)}, u32[]{:S(2)}) collective-permute-start(bf16[128,1664]{1,0:T(8,128)(2,1)} %get-tuple-element.120.refs_0_), channel_id=1, source_target_pairs={{0,1},{1,0},{2,3},{3,2},{4,5},{5,4},{6,7},{7,6},{8,9},{9,8},{10,11... | collective-permute-start | bytes 1277960 | tf_op jit(solution)/shard_map/ppermute | solution.py:78
  313.7 28.1 %collective-permute-start.68 = (bf16[64,1664]{1,0:T(8,128)(2,1)S(1)}, bf16[64,1664]{1,0:T(8,128)(2,1)}, u32[]{:S(2)}, u32[]{:S(2)}) collective-permute-start(bf16[64,1664]{1,0:T(8,128)(2,1)S(1)} %slice.102), channel_id=1, source_target_pairs={{0,2},{1,3},{2,0},{3,1},{4,6},{5,7},{6,4},{7,5},{8,10},{9,11},{10,... | collective-permute-start | bytes 638984 | tf_op jit(solution)/shard_map/ppermute | solution.py:78
  327.1 100.4 %collective-permute-start.44 = (bf16[512,1536]{1,0:T(8,128)(2,1)}, bf16[512,1536]{1,0:T(8,128)(2,1)}, u32[]{:S(2)}, u32[]{:S(2)}) collective-permute-start(bf16[512,1536]{1,0:T(8,128)(2,1)} %get-tuple-element.84), channel_id=1, source_target_pairs={{0,1},{1,0},{2,3},{3,2},{4,5},{5,4},{6,7},{7,6},{8,9},{9,8},{10,11... | collective-permute-start | bytes 4718600 | tf_op jit(solution)/shard_map/ppermute | solution.py:78
  356.7 83.2 %collective-permute-start.78 = (bf16[384,1536]{1,0:T(8,128)(2,1)}, bf16[384,1536]{1,0:T(8,128)(2,1)S(1)}, u32[]{:S(2)}, u32[]{:S(2)}) collective-permute-start(bf16[384,1536]{1,0:T(8,128)(2,1)} %fusion.3), channel_id=1, source_target_pairs={{0,8},{1,9},{2,10},{3,11},{4,12},{5,13},{6,14},{7,15},{8,0},{9,1},... | collective-permute-start | bytes 3538952 | tf_op jit(solution)/shard_map/ppermute | solution.py:81
  364.9 58.4 %collective-permute-start.65 = (bf16[384,320]{1,0:T(8,128)(2,1)S(1)}, bf16[384,320]{1,0:T(8,128)(2,1)S(1)}, u32[]{:S(2)}, u32[]{:S(2)}) collective-permute-start(bf16[384,320]{1,0:T(8,128)(2,1)S(1)} %fusion.8), channel_id=1, source_target_pairs={{0,8},{1,9},{2,10},{3,11},{4,12},{5,13},{6,14},{7,15},{8,0},{9,1},... | collective-permute-start | bytes 737288 | tf_op jit(solution)/shard_map/ppermute | solution.py:81
  375.4 58.7 %collective-permute-start.76 = (bf16[384,256]{1,0:T(8,128)(2,1)S(1)}, bf16[384,256]{1,0:T(8,128)(2,1)}, u32[]{:S(2)}, u32[]{:S(2)}) collective-permute-start(bf16[384,256]{1,0:T(8,128)(2,1)S(1)} %fusion.9), channel_id=1, source_target_pairs={{0,8},{1,9},{2,10},{3,11},{4,12},{5,13},{6,14},{7,15},{8,0},{9,1},... | collective-permute-start | bytes 589832 | tf_op jit(solution)/shard_map/ppermute | solution.py:81
  430.6 28.5 %collective-permute-start.45 = (bf16[128,1536]{1,0:T(8,128)(2,1)}, bf16[128,1536]{1,0:T(8,128)(2,1)}, u32[]{:S(2)}, u32[]{:S(2)}) collective-permute-start(bf16[128,1536]{1,0:T(8,128)(2,1)} %get-tuple-element.86), channel_id=1, source_target_pairs={{0,4},{1,5},{2,6},{3,7},{4,0},{5,1},{6,2},{7,3},{8,12},{9,13},{10,... | collective-permute-start | bytes 1179656 | tf_op jit(solution)/shard_map/ppermute | solution.py:78
  432.5 26.6 %collective-permute-start.46 = (bf16[128,1536]{1,0:T(8,128)(2,1)}, bf16[128,1536]{1,0:T(8,128)(2,1)}, u32[]{:S(2)}, u32[]{:S(2)}) collective-permute-start(bf16[128,1536]{1,0:T(8,128)(2,1)} %get-tuple-element.87), channel_id=1, source_target_pairs={{0,2},{1,3},{2,0},{3,1},{4,6},{5,7},{6,4},{7,5},{8,10},{9,11},{10,... | collective-permute-start | bytes 1179656 | tf_op jit(solution)/shard_map/ppermute | solution.py:78
  434.0 25.1 %collective-permute-start.47 = (bf16[128,1536]{1,0:T(8,128)(2,1)}, bf16[128,1536]{1,0:T(8,128)(2,1)}, u32[]{:S(2)}, u32[]{:S(2)}) collective-permute-start(bf16[128,1536]{1,0:T(8,128)(2,1)} %get-tuple-element.88), channel_id=1, source_target_pairs={{0,6},{1,7},{2,4},{3,5},{4,2},{5,3},{6,0},{7,1},{8,14},{9,15},{10,... | collective-permute-start | bytes 1179656 | tf_op jit(solution)/shard_map/ppermute | solution.py:78
  454.2 40.8 %all-to-all-start.5 = ((bf16[8,48,1536]{2,1,0:T(8,128)(2,1)}), bf16[8,48,1536]{2,1,0:T(8,128)(2,1)S(1)}, u32[]{:S(2)}, u32[]{:S(2)}) async-start(bf16[8,48,1536]{2,1,0:T(8,128)(2,1)} %bitcast.35), calls=%async_computation.5 | async-start | bytes 2359296 | tf_op jit(solution)/shard_map/all_to_all | solution.py:97
  (120 other events, 1411.5 us)
Sparse Core Ops, SparseCore 0:
  10.9 83.8 all-gather.1

commit v2 on v1

v2 whole, which is shorter than its diff:
```python
import functools
import math

import jax
import jax.numpy as jnp
from jax import lax
from jax.experimental import pallas as pl
from jax.experimental.pallas import tpu as pltpu
from jax.sharding import PartitionSpec as P

D = 1536
H = 24
KVH = 8
HD = 64
FF = 1024
E = 4
MB = 2
QW = 1536
KW = 512
CUBE = 8
GROUP = H // KVH
HALF = FF // 2
QH = GROUP * HD
SHARD = QH + 2 * HD
SLAB = 384
OUT_SLAB = 256
PAIR = 2 * QH
EXTRA = 128
WIDE = D + EXTRA
ORDER = (0, 4, 2, 6, 1, 5, 3, 7)
LOG2E = 1.4426950408889634
F32 = jnp.float32
BF16 = jnp.bfloat16
NN = (((1,), (0,)), ((), ()))
NT = (((1,), (1,)), ((), ()))
TN = (((0,), (0,)), ((), ()))
AXES = ("dp", "ctx")


def dot(left, right, dims=NN):
    return lax.dot_general(left, right, dims, preferred_element_type=F32)


class Kernels:
    def __init__(self, lengths):
        self.lengths = lengths

    def __call__(self, kernel, outs, ins, far=(), scratch=(), room=0, after=(), busy=0):
        ins, far, after = list(ins), list(far), list(after)
        n_in, n_after = 1 + len(ins) + len(far), len(after)
        vmem = pl.BlockSpec(memory_space=pltpu.VMEM)
        anywhere = pl.BlockSpec(memory_space=pl.ANY)

        def run(lengths, *refs):
            ctx = lax.axis_index("ctx")
            scal = [lax.axis_index("dp"), ctx >> 3, ctx & 7, lengths[0, 0], lengths[1, 0]]
            kernel(scal, *refs[: n_in - 1], *refs[n_in - 1 + n_after :])

        moved = sum(math.prod(a.shape) * a.dtype.itemsize for a in ins + list(outs))
        held = sum(2 * math.prod(s.shape) for s in scratch if hasattr(s, "shape"))
        grant = int(1.1 * moved) + held + (room + 4) * 1024 * 1024
        results = pl.pallas_call(
            run,
            out_shape=list(outs),
            in_specs=[pl.BlockSpec(memory_space=pltpu.SMEM)]
            + [vmem] * len(ins)
            + [anywhere] * (len(far) + n_after),
            out_specs=[vmem] * len(outs),
            scratch_shapes=list(scratch),
            compiler_params=pltpu.CompilerParams(vmem_limit_bytes=min(grant, 56 * 1024 * 1024)),
            cost_estimate=pl.CostEstimate(
                flops=1000 + busy * 10**9, bytes_accessed=1000, transcendentals=0
            ),
        )(
            self.lengths,
            *ins,
            *[pltpu.with_memory_space_constraint(value, pltpu.HBM) for value in far],
            *after,
        )
        return results


def sems(count):
    return pltpu.SemaphoreType.DMA((count,))


def shape(dims, dtype=BF16):
    return jax.ShapeDtypeStruct(dims, dtype)


class Links:
    def __init__(self, nx, nc):
        self.nx, self.nc, self.ng = nx, nc, nc // CUBE

    def _pairs(self, move):
        pairs = []
        for x in range(self.nx):
            for g in range(self.ng):
                for t in range(CUBE):
                    goal = move(x, g, t)
                    if goal is not None:
                        gx, gg, gt = goal
                        pairs.append((x * self.nc + g * CUBE + t, gx * self.nc + gg * CUBE + gt))
        return pairs

    def cube(self, value, bits):
        return lax.ppermute(value, AXES, self._pairs(lambda x, g, t: (x, g, t ^ bits)))

    def outer(self, value, dx, dg):
        return lax.ppermute(value, AXES, self._pairs(lambda x, g, t: (x ^ dx, g ^ dg, t)))

    def climb(self, value, step):
        def move(x, g, t):
            return (x, g + step, t) if 0 <= g + step < self.ng else None

        return lax.ppermute(value, AXES, self._pairs(move))

    def cubes(self):
        return [
            [x * self.nc + g * CUBE + t for t in range(CUBE)]
            for x in range(self.nx)
            for g in range(self.ng)
        ]

    def swap(self, value):
        return lax.all_to_all(
            value, AXES, split_axis=0, concat_axis=0, tiled=True, axis_index_groups=self.cubes()
        )

    def swap_all(self, value):
        return lax.all_to_all(value, AXES, split_axis=0, concat_axis=0, tiled=True)

    def near(self, rows):
        return [self.cube(rows, bits) for bits in ORDER[1:4]]

    def core(self, rows):
        return self.cube(rows, 1)

    def cores(self):
        return [list(range(core, self.nx * self.nc, 2)) for core in range(2)]

    def outers(self):
        return [
            [x * self.nc + g * CUBE + t for x in range(self.nx) for g in range(self.ng)]
            for t in range(CUBE)
        ]

    def outer_direct(self, rows):
        return [rows] + [
            self.outer(rows, dx, dg)
            for dx in range(self.nx)
            for dg in range(self.ng)
            if dx or dg
        ]


def fence(*values):
    return lax.optimization_barrier(values)


def stack_copies(refs, out, sem):
    rows = refs[0].shape[0]
    return [
        pltpu.make_async_copy(ref, out.at[pl.ds(n * rows, rows)], sem.at[n])
        for n, ref in enumerate(refs)
    ]


def outer_copies(refs, out, sem, scal, ng):
    rows = refs[0].shape[0]
    copies = []
    for j, ref in enumerate(refs):
        place = (scal[0] ^ (j // ng)) * ng + (scal[1] ^ (j % ng))
        spot = pl.ds(pl.multiple_of(place * rows, 16), rows)
        copies.append(pltpu.make_async_copy(ref, out.at[spot], sem.at[j]))
    return copies


def start_all(copies):
    for copy in copies:
        copy.start()


def wait_all(copies):
    for copy in copies:
        copy.wait()


def prep_kernel(scal, w_ref, gain_ref, tok_ref, routes_ref, out_ref, tok_out):
    wr = w_ref.shape[0]
    fill = column(gain_ref, SLAB - SHARD).astype(BF16)
    for k in range(CUBE):
        out_ref[k] = jnp.concatenate(
            [
                w_ref[:, k * QH : (k + 1) * QH],
                w_ref[:, QW + k * HD : QW + (k + 1) * HD],
                w_ref[:, QW + KW + k * HD : QW + KW + (k + 1) * HD],
                fill,
            ],
            axis=1,
        )
    rows = tok_ref.shape[0]
    tok_out[:, :D] = tok_ref[...]
    lane = lax.broadcasted_iota(jnp.int32, (rows, EXTRA), 1)
    names = jnp.where(lane == 0, routes_ref[:, 0:1], routes_ref[:, 1:2])
    tok_out[:, D:] = names.astype(F32).astype(BF16)


def column(row_ref, width):
    return jnp.broadcast_to(row_ref[...].astype(F32), (width, row_ref.shape[1])).T


def as_row(values):
    return jnp.broadcast_to(values, (values.shape[0], EXTRA)).T[0:1, :]


def prep_rest_kernel(scal, gu_ref, dn_ref, wo_ref, rt_ref, gain_ref, moe_out, wo_out):
    for k in range(CUBE):
        e, h = k // 2, k % 2
        moe_out[k, :, :HALF] = gu_ref[e, :, h * HALF : (h + 1) * HALF]
        moe_out[k, :, HALF : 2 * HALF] = gu_ref[e, :, FF + h * HALF : FF + (h + 1) * HALF]
        moe_out[k, :, 2 * HALF :] = dn_ref[e, :, h * HALF : (h + 1) * HALF]
    wr = wo_ref.shape[0]
    rt = rt_ref[...].astype(F32)
    rows = jnp.concatenate(
        [rt, rt, gain_ref[...].astype(F32), jnp.zeros((EXTRA - 2 * E - 1, wr), F32)], axis=0
    )
    wo_out[:, :QW] = wo_ref[...]
    wo_out[:, QW:] = rows.T.astype(BF16)


def split_kernel(scal, both_ref, gu_ref, dn_ref):
    gu_ref[...] = both_ref[:, : 2 * HALF]
    dn_ref[...] = both_ref[:, 2 * HALF :]


def pack_kernel(scal, *refs):
    rows = refs[0].shape[0]
    for n, ref in enumerate(refs[:-1]):
        refs[-1][n * rows : (n + 1) * rows, :] = ref[...]


def qkv_kernel(ng, n_outer, scal, even_ref, odd_ref, *refs):
    t = scal[2]
    weights, (xg, q_out, kv_out, gain_ref, w_ref, sem) = refs[:n_outer], refs[n_outer:]
    copies = outer_copies(weights, w_ref, sem, scal, ng)
    start_all(copies)
    wait_all(copies)
    rows = even_ref.shape[0] // 4
    slots = rows // MB
    blank = jnp.zeros((slots, HD), BF16)
    gain = w_ref[:, 256:].astype(F32).T[SHARD - 256 : SHARD - 248, :]
    gain_ref[...] = gain
    gain = gain[0:1]
    for p, k in enumerate(ORDER):
        source = even_ref if p < 4 else odd_ref
        values = source[(p % 4) * rows : (p % 4 + 1) * rows, :D].astype(F32)
        scale = lax.rsqrt(jnp.mean(values * values, axis=-1, keepdims=True) + 1e-05)
        packed = (values * scale * gain).astype(BF16)
        xg[p * rows : (p + 1) * rows, :] = packed
        y = dot(packed, w_ref[...]).astype(BF16)
        for m in range(MB):
            part = y[m * slots : (m + 1) * slots]
            spot = pl.ds(pl.multiple_of((t ^ k) * slots, 64), slots)
            for h in range(GROUP):
                q_out[m, h, spot, :] = jnp.concatenate(
                    [part[:, h * HD : (h + 1) * HD], blank], axis=1
                )
            kv_out[m, spot, :] = part[:, QH:SHARD]


def key_bias(extent, g, step, length):
    local = lax.broadcasted_iota(jnp.int32, (extent, 1), 0)
    seen = ((g - step) * extent + local < length) & (g >= step)
    return jnp.where(seen, 0.0, -1e30).astype(F32)


def causal_bias(extent):
    keys = lax.broadcasted_iota(jnp.int32, (extent, extent), 0)
    rows = lax.broadcasted_iota(jnp.int32, (extent, extent), 1)
    return jnp.where(keys <= rows, 0.0, -1e30).astype(F32)


def attend_kernel(slots, scal, *refs):
    g = scal[1]
    n_keys = len(refs) - 4
    q_ref, kv_refs, (att_ref, ot_ref, lse_ref) = refs[0], refs[1 : 1 + n_keys], refs[1 + n_keys :]
    extent = q_ref.shape[2]
    causal = causal_bias(extent)
    for m in range(MB):
        length = scal[3 + m]
        biases = [key_bias(extent, g, s, length) for s in range(n_keys)]
        for h in range(GROUP):
            q = q_ref[m, h]
            top = total = acc = None
            for s in range(n_keys):
                kv = kv_refs[s][m]
                st = dot(kv, q, NT) * (0.125 * LOG2E) + biases[s]
                if s == 0:
                    st = st + causal
                peak = jnp.max(st, axis=0, keepdims=True)
                if s == 0:
                    pt = jnp.exp2(st - peak)
                    top, total = peak, jnp.sum(pt, axis=0, keepdims=True)
                    acc = dot(kv, pt.astype(BF16), TN)
                else:
                    fresh = jnp.maximum(top, peak)
                    scale = jnp.exp2(top - fresh)
                    pt = jnp.exp2(st - fresh)
                    total = total * scale + jnp.sum(pt, axis=0, keepdims=True)
                    acc = acc * scale + dot(kv, pt.astype(BF16), TN)
                    top = fresh
            ot = acc[HD:, :] / total
            ot_ref[m, h] = ot
            lse_ref[m, h : h + 1, :] = top + jnp.log2(total)
            o = ot.T.astype(BF16)
            for k in range(CUBE):
                place = (k // 4) * QH + h * HD
                base = (k % 4) * MB * slots + m * slots
                att_ref[base : base + slots, place : place + HD] = o[k * slots : (k + 1) * slots]


def row_valid(scal, rows):
    slots = rows // MB
    spot = lax.broadcasted_iota(jnp.int32, (rows, 1), 0)
    place = (scal[1] * CUBE + scal[2]) * slots
    length = jnp.where(spot < slots, scal[3], scal[4])
    inner = jnp.where(spot < slots, spot, spot - slots)
    return jnp.where(place + inner < length, 1.0, 0.0).astype(F32)


def gain_row(rest):
    return rest.astype(F32).T[2 * E : 2 * E + 1, :]


def att_block(ref, base, rows, j):
    spot = pl.ds(pl.multiple_of(base + (j & 3) * rows, 16), rows)
    both = ref[spot, :]
    return jnp.where(j >= 4, both[:, QH:], both[:, :QH])


def mix_kernel(scal, even_ref, odd_ref, toke_ref, toko_ref, wo_ref, *refs):
    t = scal[2]
    nge, ngo, mixed_ref, comb_ref, att = refs
    rows = mixed_ref.shape[0]
    slots = rows // MB
    for q in range(4):
        head = t ^ ORDER[q]
        lanes = pl.ds(pl.multiple_of((head >> 1) * PAIR, 128), PAIR)
        for p, k in enumerate(ORDER):
            low = att_block(even_ref, q * 4 * rows, rows, t ^ k)
            high = att_block(odd_ref, q * 4 * rows, rows, t ^ k)
            flip = (head & 1) == 1
            att[p * rows : (p + 1) * rows, lanes] = jnp.concatenate(
                [jnp.where(flip, high, low), jnp.where(flip, low, high)], axis=1
            )
    rest = wo_ref[:, QW:]
    gain = gain_row(rest)
    lane = lax.broadcasted_iota(jnp.int32, (2 * rows, EXTRA), 1)
    spot = lax.broadcasted_iota(jnp.int32, (2 * rows, 1), 0)
    inner = spot & (rows - 1)
    second = inner >= slots
    length = jnp.where(second, scal[4], scal[3])
    slot = jnp.where(second, inner - slots, inner)
    for p in range(0, CUBE, 2):
        tok_ref, out_ref = (toke_ref, nge) if p < 4 else (toko_ref, ngo)
        local = slice((p % 4) * rows, (p % 4 + 2) * rows)
        owner = jnp.where(spot < rows, t ^ ORDER[p], t ^ ORDER[p + 1])
        place = (scal[1] * CUBE + owner) * slots + slot
        valid = jnp.where(place < length, 1.0, 0.0).astype(F32)
        branch = dot(att[p * rows : (p + 2) * rows, :], wo_ref[:, :QW], NT)
        mixed = tok_ref[local, :D].astype(F32) + valid * branch
        scale = lax.rsqrt(jnp.mean(mixed * mixed, axis=-1, keepdims=True) + 1e-05)
        low = (mixed * scale * gain).astype(BF16)
        logits = dot(low, rest)
        names = tok_ref[local, D:].astype(F32)
        expert = (lane & (E - 1)).astype(F32)
        chosen = ((expert == names[:, 0:1]) | (expert == names[:, 1:2])) & (lane < 2 * E)
        peak = jnp.max(jnp.where(chosen, logits, -3e38), axis=-1, keepdims=True)
        expo = jnp.where(chosen, jnp.exp(logits - peak), 0.0)
        comb = expo / (0.5 * jnp.sum(expo, axis=-1, keepdims=True))
        if p == 0:
            mixed_ref[...] = mixed[:rows]
            comb_ref[...] = jnp.where(lane < E, comb, 0.0)[:rows]
        comb = comb * valid
        high = comb.astype(BF16)
        tail = (comb - high.astype(F32)).astype(BF16)
        out_ref[local, :D] = low
        out_ref[local, D:] = jnp.where(lane < E, high, tail)


def row_valid(scal, rows):
    slots = rows // MB
    spot = lax.broadcasted_iota(jnp.int32, (rows, 1), 0)
    place = (scal[1] * CUBE + scal[2]) * slots
    length = jnp.where(spot < slots, scal[3], scal[4])
    inner = jnp.where(spot < slots, spot, spot - slots)
    return jnp.where(place + inner < length, 1.0, 0.0).astype(F32)


def cot_kernel(ng, n_outer, scal, even_ref, odd_ref, *refs):
    dn_blocks, (q_ref, w_dn, sem) = refs[:n_outer], refs[n_outer:]
    copies = outer_copies(dn_blocks, w_dn, sem, scal, ng)
    start_all(copies)
    wait_all(copies)
    step = even_ref.shape[0] // 2
    for part, source in enumerate((even_ref, odd_ref)):

        @pl.loop(0, 2)
        def _(i):
            local = pl.ds(pl.multiple_of(i * step, 128), step)
            spot = pl.ds(pl.multiple_of((2 * part + i) * step, 128), step)
            q_ref[spot, :] = dot(source[local, :], w_dn[...])


def own_share(wide, scal):
    lane = lax.broadcasted_iota(jnp.int32, wide.shape, 1)
    expert = scal[2] // 2
    mine = (lane == expert) | (lane == expert + E)
    return jnp.sum(jnp.where(mine, wide.astype(F32), 0.0), axis=-1, keepdims=True)


def expert_kernel(base, ng, n_outer, scal, ngw, q_ref, *refs):
    if base:
        blocks, (act_ref, ggu_ref, out_ref, w_ref, sem) = refs[:n_outer], refs[n_outer:]
        copies = outer_copies(blocks, w_ref, sem, scal, ng)
        start_all(copies)
        wait_all(copies)
    else:
        w_ref, act_ref, ggu_ref, out_ref = refs
    step = ngw.shape[0] // 2
    expert = scal[2] // 2

    @pl.loop(0, 2)
    def _(i):
        spot = pl.ds(pl.multiple_of(i * step, 128), step)
        share = own_share(ngw[spot, D:], scal)
        gu = dot(ngw[spot, :D], w_ref[...])
        gate, up = gu[:, :HALF], gu[:, HALF:]
        sig = 1.0 / (1.0 + jnp.exp(-gate))
        soft = gate * sig
        act = (soft * up).astype(BF16)
        act_ref[spot, :] = act
        back = q_ref[pl.ds(pl.multiple_of(base + i * step, 128), step), :]
        dots = jnp.sum(act.astype(F32) * back, axis=-1, keepdims=True)
        back = back * share
        ggu_ref[spot, :HALF] = (back * up * (sig * (1.0 + gate * (1.0 - sig)))).astype(BF16)
        ggu_ref[spot, HALF:] = (back * soft).astype(BF16)
        out_ref[spot, :D] = dot(ggu_ref[spot, :], w_ref[...], NT).astype(BF16)
        high = dots.astype(BF16)
        rest = (dots - high.astype(F32)).astype(BF16)
        lane = lax.broadcasted_iota(jnp.int32, (step, EXTRA), 1)
        out_ref[spot, D:] = jnp.where(
            lane == expert, high, jnp.where(lane == expert + E, rest, jnp.zeros_like(rest))
        )


def expert_grad_kernel(
    scal, dye, dyo, nge, ngo, acte, acto, ggue, gguo, gu_other, dn_other, gu_mine, dn_mine, cae, cao
):
    for wide, act, out in ((nge, acte, cae), (ngo, acto, cao)):
        out[...] = (act[...].astype(F32) * own_share(wide[:, D:], scal)).astype(BF16)
    cut = D // 6
    for flip, gu_ref, dn_ref in ((1, gu_other, dn_other), (0, gu_mine, dn_mine)):

        @pl.loop(0, 3)
        def _(i):
            cols = pl.ds(pl.multiple_of((scal[0] ^ flip) * (D // 2) + i * cut, 128), cut)
            spot = pl.ds(pl.multiple_of(i * cut, 128), cut)
            total = dot(nge[:, cols], ggue[...], TN) + dot(ngo[:, cols], gguo[...], TN)
            gu_ref[spot, :] = total.astype(BF16)
            total = dot(dye[:, cols], cae[...], TN) + dot(dyo[:, cols], cao[...], TN)
            dn_ref[spot, :] = total.astype(BF16)


def expert_out_kernel(scal, w_ref, nge, ngo, acte, acto, even_ref, odd_ref):
    step = acte.shape[0] // 2
    for wide, act, out_ref in ((nge, acte, even_ref), (ngo, acto, odd_ref)):

        @pl.loop(0, 2)
        def _(i):
            spot = pl.ds(pl.multiple_of(i * step, 128), step)
            share = own_share(wide[spot, D:], scal)
            out_ref[spot, :] = (dot(act[spot, :], w_ref[...], NT) * share).astype(BF16)


def fold_kernel(ng, scal, mine_ref, got_ref, *refs):
    rows = mine_ref.shape[0] // ng
    for dg, out in enumerate(refs):
        spot = pl.ds(pl.multiple_of((scal[1] ^ dg) * rows, 16), rows)
        total = mine_ref[spot, :].astype(F32) + got_ref[spot, :].astype(F32)
        out[...] = total.astype(out.dtype)


def fold_last_kernel(n_in, scal, *refs):
    base = 0
    for ins in (refs[:n_in], refs[n_in:-1]):
        total = ins[0][...]
        for ref in ins[1:]:
            total = total + ref[...].astype(F32)
        refs[-1][:, base : base + total.shape[1]] = total.astype(BF16)
        base += total.shape[1]


def fold_parts_kernel(n_in, scal, *refs):
    ins, outs = refs[:n_in], refs[n_in:]
    wr = outs[0].shape[0]
    for j in range(CUBE):
        spot = slice(j * wr, (j + 1) * wr)
        total = ins[0][spot, :]
        for ref in ins[1:]:
            total = total + ref[spot, :].astype(F32)
        outs[-1][j] = total.astype(BF16)
    for k, out in enumerate(outs[:-1]):
        out[...] = outs[-1][scal[2] ^ k]


def pair_kernel(scal, even_ref, odd_ref, *outs):
    rows = outs[0].shape[0]
    for p, out in enumerate(outs):
        spot = slice(p * rows, (p + 1) * rows)
        out[...] = (even_ref[spot, :].astype(F32) + odd_ref[spot, :].astype(F32)).astype(BF16)


def norm_back(grad, values, scale):
    unit = values * scale
    return scale * (grad - unit * jnp.mean(grad * unit, axis=-1, keepdims=True))


def turn_kernel(scal, a0, a1, a2, a3, mixed_ref, cot_ref, comb_ref, wo_ref, grad_ref, wide_ref):
    rest = wo_ref[:, QW:]
    rows = mixed_ref.shape[0]
    total = (
        a0[...].astype(F32) + a1[...].astype(F32) + a2[...].astype(F32) + a3[...].astype(F32)
    )
    valid = row_valid(scal, rows)
    lane = lax.broadcasted_iota(jnp.int32, (rows, EXTRA), 1)
    dots = total[:, D:]
    dots = (dots + pltpu.roll(dots, EXTRA - E, 1)) * valid
    comb = comb_ref[...]
    inner = jnp.sum(comb * dots, axis=-1, keepdims=True)
    grad_logits = jnp.where(lane < E, comb * (dots - inner), 0.0).astype(BF16)
    grad_normed = (total[:, :D] + dot(grad_logits, rest, NT)) * gain_row(rest)
    mixed = mixed_ref[...]
    scale = lax.rsqrt(jnp.mean(mixed * mixed, axis=-1, keepdims=True) + 1e-05)
    grad_mixed = cot_ref[...].astype(F32) + norm_back(grad_normed, mixed, scale)
    grad_ref[...] = grad_mixed
    branch = (valid * grad_mixed).astype(BF16)
    wide_ref[:, :D] = branch
    wide_ref[:, D:] = grad_logits


def grad_rows_kernel(scal, w_ref, even_ref, odd_ref, ga_ref):
    t = scal[2]
    rows = ga_ref.shape[1]
    window = w_ref[:, pl.ds(pl.multiple_of(((3 * t) >> 1) * 128, 128), 256)]
    weight = jnp.where((t & 1) == 1, window[:, HD:], window[:, :QH])
    for part, wide in enumerate((even_ref, odd_ref)):
        for n in range(2):
            spot = slice(2 * n * rows, 2 * (n + 1) * rows)
            grad = dot(wide[spot, :D], weight).astype(BF16)
            for i in range(2):
                ga_ref[t ^ ORDER[4 * part + 2 * n + i]] = grad[i * rows : (i + 1) * rows]


def attend_back_kernel(slots, n_keys, scal, *refs):
    g = scal[1]
    q_ref, kv_refs, refs = refs[0], refs[1 : 1 + n_keys], refs[1 + n_keys :]
    ot_ref, lse_ref, ga_ref, gq_ref, refs = refs[0], refs[1], refs[2], refs[3], refs[4:]
    gkv_refs, (do_ref,) = refs[:n_keys], refs[n_keys:]
    extent = q_ref.shape[2]
    causal = causal_bias(extent)
    blank = jnp.zeros((slots, HD), BF16)
    for m in range(MB):
        length = scal[3 + m]
        biases = [key_bias(extent, g, s, length) for s in range(n_keys)]
        sums = [None] * n_keys
        for h in range(GROUP):
            for k in range(CUBE):
                part = ga_ref[k, m * slots : (m + 1) * slots, h * HD : (h + 1) * HD]
                do_ref[k * slots : (k + 1) * slots, :] = jnp.concatenate([blank, part], axis=1)
            q = q_ref[m, h]
            do = do_ref[...]
            dot_t = do.astype(F32).T[HD:, :]
            delta = jnp.sum(dot_t * ot_ref[m, h], axis=0, keepdims=True)
            lse = lse_ref[m, h : h + 1, :]
            grad_q = None
            for s in range(n_keys):
                kv = kv_refs[s][m]
                st = dot(kv, q, NT) * (0.125 * LOG2E) + biases[s]
                if s == 0:
                    st = st + causal
                pt = jnp.exp2(st - lse)
                dpt = dot(kv, do, NT)
                dst = (pt * (dpt - delta) * 0.125).astype(BF16)
                part = dot(dst, q) + dot(pt.astype(BF16), do)
                sums[s] = part if sums[s] is None else sums[s] + part
                part = dot(kv, dst, TN)
                grad_q = part if grad_q is None else grad_q + part
            gq = grad_q[:HD, :].T.astype(BF16)
            for k in range(CUBE):
                gq_ref[k, m * slots : (m + 1) * slots, h * HD : (h + 1) * HD] = gq[
                    k * slots : (k + 1) * slots
                ]
        for s in range(n_keys):
            gkv_refs[s][m] = sums[s].astype(gkv_refs[s].dtype)


def close_kernel(n_keys, scal, gq_ref, w_ref, own_ref, *refs):
    t = scal[2]
    others, (gqkv, even_ref, odd_ref) = refs[: n_keys - 1], refs[n_keys - 1 :]
    rows = gq_ref.shape[1]
    slots = rows // MB
    gqkv[:, SHARD:] = jnp.zeros((CUBE * rows, SLAB - SHARD), BF16)
    for p, k in enumerate(ORDER):
        gqkv[p * rows : (p + 1) * rows, :QH] = gq_ref[t ^ k]
        for m in range(MB):
            spot = pl.ds(pl.multiple_of((t ^ k) * slots, 64), slots)
            total = own_ref[m, spot, :]
            for other in others:
                total = total + other[m, spot, :].astype(F32)
            base = p * rows + m * slots
            gqkv[base : base + slots, QH:SHARD] = total.astype(BF16)
    step = 2 * rows
    for part, out_ref in enumerate((even_ref, odd_ref)):

        @pl.loop(0, 2)
        def _(i):
            local = pl.ds(pl.multiple_of(i * step, 128), step)
            spot = pl.ds(pl.multiple_of(part * 2 * step + i * step, 128), step)
            out_ref[local, :] = dot(gqkv[spot, :], w_ref[...], NT).astype(BF16)


def qkv_grad_kernel(scal, xg, gqkv, wo_ref, other_ref, mine_ref):
    cut = D // 6
    for flip, out_ref in ((1, other_ref), (0, mine_ref)):

        @pl.loop(0, 3)
        def _(i):
            cols = pl.ds(pl.multiple_of((scal[0] ^ flip) * (D // 2) + i * cut, 128), cut)
            spot = pl.ds(pl.multiple_of(i * cut, 128), cut)
            out_ref[spot, :SLAB] = dot(xg[:, cols], gqkv[...], TN).astype(BF16)
            out_ref[spot, SLAB:] = wo_ref[cols, :]


def out_grad_kernel(scal, ge_ref, go_ref, att_ref, nge, ngo, w_out, ate, ato):
    rows = ge_ref.shape[0] // 4
    for p, k in enumerate(ORDER):
        out = ate if p < 4 else ato
        out[(p % 4) * rows : (p % 4 + 1) * rows, :] = att_block(att_ref, 0, rows, scal[2] ^ k)
    cut = D // 4

    @pl.loop(0, 4)
    def _(i):
        cols = pl.ds(pl.multiple_of(i * cut, 128), cut)
        total = dot(ge_ref[:, cols], ate[...], TN) + dot(go_ref[:, cols], ato[...], TN)
        w_out[cols, :QH] = total.astype(BF16)
        low = dot(nge[:, cols], ge_ref[:, D:], TN) + dot(ngo[:, cols], go_ref[:, D:], TN)
        w_out[cols, QH:] = low[:, : OUT_SLAB - QH].astype(BF16)


def finish_attention_kernel(scal, w_ref, gain_ref, *refs):
    parts, (out_ref, gain_out, wo_out, rt_out, got) = refs[:CUBE], refs[CUBE:]
    for k, ref in enumerate(parts):
        got[scal[2] ^ k] = ref[...]
    for k in range(CUBE):
        part = got[k].astype(F32)
        out_ref[:, k * QH : (k + 1) * QH] = part[:, :QH]
        out_ref[:, QW + k * HD : QW + (k + 1) * HD] = part[:, QH : QH + HD]
        out_ref[:, QW + KW + k * HD : QW + KW + (k + 1) * HD] = part[:, QH + HD : SHARD]
        wo_out[:, k * QH : (k + 1) * QH] = part[:, SLAB : SLAB + QH]
        if k == 0:
            rt_out[...] = part[:, SLAB + EXTRA :].T[QH - EXTRA : QH - EXTRA + 8]
    total = jnp.sum(out_ref[...] * w_ref[...].astype(F32), axis=-1, keepdims=True)
    gain_out[...] = as_row(total) / gain_ref[...].astype(F32)


def finish_experts_kernel(
    scal, got, w_ref, rg_ref, rt_ref, gain_ref, out_ref, gain_out, dn_out
):
    total = jnp.zeros((out_ref.shape[1], 1), F32)
    for k in range(CUBE):
        e, h = k // 2, k % 2
        for at, base in ((h * HALF, 0), (FF + h * HALF, HALF)):
            part = got[k, :, base : base + HALF].astype(F32)
            out_ref[e, :, at : at + HALF] = part
            weight = w_ref[e, :, at : at + HALF].astype(F32)
            total = total + jnp.sum(part * weight, axis=-1, keepdims=True)
        dn_out[e, :, h * HALF : (h + 1) * HALF] = got[k, :, 2 * HALF :].astype(F32)
    router = jnp.sum(rg_ref[:E] * rt_ref[...].astype(F32), axis=0, keepdims=True)
    gain_out[...] = (as_row(total) + router) / gain_ref[...].astype(F32)


def output_kernel(scal, a0, a1, a2, a3, mixed_ref, out_ref):
    total = (
        a0[...].astype(F32) + a1[...].astype(F32) + a2[...].astype(F32) + a3[...].astype(F32)
    )
    out_ref[...] = (mixed_ref[...] + total).astype(BF16)


def tokens_kernel(scal, a0, a1, a2, a3, x_ref, grad_ref, gain_ref, out_ref):
    total = (
        a0[...].astype(F32) + a1[...].astype(F32) + a2[...].astype(F32) + a3[...].astype(F32)
    )
    x = x_ref[...].astype(F32)
    scale = lax.rsqrt(jnp.mean(x * x, axis=-1, keepdims=True) + 1e-05)
    out_ref[...] = (grad_ref[...] + norm_back(total * gain_ref[0:1, :], x, scale)).astype(BF16)


def body(
    tokens,
    lengths,
    routes,
    cotangent,
    attn_gain,
    qkv_weight,
    out_weight,
    moe_gain,
    router,
    gateup_weight,
    down_weight,
):
    nx, nc = lax.axis_size("dp"), lax.axis_size("ctx")
    links = Links(nx, nc)
    ng = links.ng
    n_outer = nx * ng
    slots = tokens.shape[2]
    rows = MB * slots
    extent = CUBE * slots
    wr = attn_gain.shape[0]
    out_rows = CUBE * rows

    half_rows = out_rows // 2
    tok = tokens.reshape(rows, D)
    cot = cotangent.reshape(rows, D)
    call = Kernels(lengths)
    bf, vm = shape, pltpu.VMEM

    def hbm(dims, dtype=BF16):
        return pltpu.HBM(dims, dtype)

    def f32(*dims):
        return shape(dims, F32)

    def pair(even, got):
        return call(pair_kernel, [bf((rows, even.shape[1]))] * 4, [even, got])

    def spread(parts):
        return [links.cube(part, bits) for part, bits in zip(parts[1:], ORDER[1:4])]

    def fold(mine, got):
        part = (CUBE * wr, mine.shape[1])
        kept = call(
            functools.partial(fold_kernel, ng),
            [shape(part, F32)] + [bf(part)] * (ng - 1),
            [mine, got],
            room=2,
        )
        return list(kept)

    def send_groups(kept):
        return [kept[0]] + [links.outer(kept[dg], 0, dg) for dg in range(1, ng)]

    def pack(blocks):
        own = blocks[0].shape
        return call(pack_kernel, [bf((4 * own[0], own[1]))], blocks)[0]

    wq_parts, tok_wide = call(
        prep_kernel,
        [bf((CUBE, wr, SLAB)), bf((rows, WIDE))],
        [qkv_weight, attn_gain.reshape(1, wr), tok, routes.reshape(rows, 2)],
        room=3,
    )
    tok_wide, wq_parts, gateup_in, down_in = fence(
        tok_wide, wq_parts, gateup_weight, down_weight.transpose(0, 2, 1)
    )
    tok_near = links.near(tok_wide)
    wq_group = links.swap(wq_parts).reshape(CUBE * wr, SLAB)
    moe_parts, wo_part = call(
        prep_rest_kernel,
        [bf((CUBE, wr, 3 * HALF)), bf((wr, WIDE))],
        [gateup_in, down_in, out_weight.T, router.T, moe_gain.reshape(1, wr)],
        room=3,
        busy=20,
    )
    wo = lax.all_gather(wo_part, AXES, axis=0, tiled=True)
    tok_wide, tok_near, wq_group, moe_parts = fence(tok_wide, tok_near, wq_group, moe_parts)
    tok_even = pack([tok_wide] + list(tok_near))
    tok_even, wq_group, moe_parts = fence(tok_even, wq_group, moe_parts)
    tok_odd = links.core(tok_even)
    wq_blocks = links.outer_direct(wq_group)
    moe_group = links.swap(moe_parts).reshape(CUBE * wr, 3 * HALF)
    tok_even, tok_odd, wq_blocks, moe_group, cot = fence(
        tok_even, tok_odd, wq_blocks, moe_group, cot
    )
    xg, q, kv, gain1, wq = call(
        functools.partial(qkv_kernel, ng, n_outer),
        [
            hbm((out_rows, D)),
            bf((MB, GROUP, extent, 2 * HD)),
            bf((MB, extent, 2 * HD)),
            hbm((8, D), F32),
            hbm((D, SLAB)),
        ],
        [tok_even, tok_odd],
        wq_blocks,
        [sems(n_outer)],
        room=4,
    )
    gu_group, dn_group = call(
        split_kernel, [bf((CUBE * wr, 2 * HALF)), bf((CUBE * wr, HALF))], [moe_group], after=[kv]
    )
    kv, dn_group, gu_group, cot = fence(kv, dn_group, gu_group, cot)
    kvs = [links.climb(kv, step) for step in range(1, ng)]
    cot_near = links.near(cot)
    dn_far = [links.outer(dn_group, 0, dg) for dg in range(1, ng)]
    gu_side = [links.outer(gu_group, dx, 0) for dx in range(1, nx)]
    kv, kvs, dn_group, dn_far, gu_group, gu_side, cot, cot_near, wo = fence(
        kv, kvs, dn_group, dn_far, gu_group, gu_side, cot, cot_near, wo
    )
    kvs = [kv] + list(kvs)
    cot_even = pack([cot] + list(cot_near))
    att, ot, lse = call(
        functools.partial(attend_kernel, slots),
        [bf((4 * rows, PAIR)), hbm((MB, GROUP, HD, extent), F32), hbm((MB, GROUP, extent), F32)],
        [q] + kvs,
        room=10,
    )
    att, cot_even, dn_group, dn_far, gu_group = fence(att, cot_even, dn_group, dn_far, gu_group)
    att_near = links.near(att)
    cot_odd = links.core(cot_even)
    dn_blocks = [dn_group] + list(dn_far)
    for dx in range(1, nx):
        dn_blocks += [links.outer(block, dx, 0) for block in dn_blocks[:ng]]
    gu_far = [links.outer(gu_group, 0, dg) for dg in range(1, ng)]
    att, att_near, cot_odd, dn_blocks, gu_far = fence(att, att_near, cot_odd, dn_blocks, gu_far)
    att_even = pack([att] + list(att_near))
    att_even, gu_far = fence(att_even, gu_far)
    att_odd = links.core(att_even)
    gu_blocks = [gu_group] + list(gu_far)
    for dx in range(1, nx):
        gu_blocks += [gu_side[dx - 1]] + [links.outer(block, dx, 0) for block in gu_far]
    back, w_dn = call(
        functools.partial(cot_kernel, ng, n_outer),
        [f32(out_rows, HALF), bf((D, HALF))],
        [cot_even, cot_odd],
        list(dn_blocks),
        [sems(n_outer)],
        room=4,
        busy=20,
    )
    att_odd, back = fence(att_odd, back)
    nge, ngo, mixed, comb = call(
        mix_kernel,
        [bf((half_rows, WIDE)), bf((half_rows, WIDE)), hbm((rows, D), F32), hbm((rows, EXTRA), F32)],
        [att_even, att_odd, tok_even, tok_odd, wo],
        scratch=[vm((out_rows, D), BF16)],
        room=8,
    )
    gu_blocks, nge, ngo = fence(gu_blocks, nge, ngo)

    def experts(wide, weights, base):
        outs = [bf((half_rows, HALF)), bf((half_rows, 2 * HALF)), bf((half_rows, WIDE))]
        kernel = functools.partial(expert_kernel, base, ng, n_outer)
        if base:
            outs.append(bf((D, 2 * HALF)))
            return call(kernel, outs, [wide, back], weights, [sems(n_outer)], room=8)
        return call(kernel, outs, [wide, back, weights], room=8)

    acto, gguo, odd, w_gu = experts(ngo, list(gu_blocks), half_rows)
    odd, nge = fence(odd, nge)
    odd_got = links.core(odd)
    acte, ggue, even = experts(nge, w_gu, 0)
    odd_got, even, acte, ggue = fence(odd_got, even, acte, ggue)
    sums = pair(even, odd_got)
    sums = fence(*sums)
    got = spread(sums)
    sums, got = fence(sums, got)
    grad_mixed, grad_wide = call(
        turn_kernel,
        [f32(rows, D), bf((rows, WIDE))],
        [sums[0]] + list(got) + [mixed, cot, comb, wo],
        room=8,
    )
    grad_wide, nge, ngo, acte, acto = fence(grad_wide, nge, ngo, acte, acto)
    grad_near = links.near(grad_wide)
    gu_other, dn_other, gu_mine, dn_mine = call(
        expert_grad_kernel,
        [bf((D // 2, 2 * HALF)), bf((D // 2, HALF))] * 2,
        [cot_even, cot_odd, nge, ngo, acte, acto, ggue, gguo],
        scratch=[vm((half_rows, HALF), BF16), vm((half_rows, HALF), BF16)],
        room=4,
        busy=20,
    )
    out_even, out_odd = call(
        expert_out_kernel, [bf((half_rows, D))] * 2, [w_dn, nge, ngo, acte, acto], room=4, busy=10
    )
    grad_wide, grad_near, out_odd, gu_other, dn_other, gu_mine, dn_mine = fence(
        grad_wide, grad_near, out_odd, gu_other, dn_other, gu_mine, dn_mine
    )
    dn_got = links.outer(dn_other, 1, 0)
    gu_got = links.outer(gu_other, 1, 0)
    grad_even = pack([grad_wide] + list(grad_near))
    grad_even, out_odd = fence(grad_even, out_odd)
    grad_odd = links.core(grad_even)
    out_got = links.core(out_odd)
    grad_odd, out_got = fence(grad_odd, out_got)
    out_sums = pair(out_even, out_got)
    grad_heads = call(
        grad_rows_kernel, [bf((CUBE, rows, QH))], [wo, grad_even, grad_odd], room=3
    )[0]
    grads = call(
        functools.partial(attend_back_kernel, slots, ng),
        [bf((CUBE, rows, QH)), f32(MB, extent, 2 * HD)] + [bf((MB, extent, 2 * HD))] * (ng - 1),
        [q] + kvs + [ot, lse, grad_heads],
        scratch=[vm((extent, 2 * HD), BF16)],
        room=12,
    )
    gq, gkv, grads = grads[0], grads[1], grads[2:]
    gq, gkv, grads, grad_even, grad_odd, out_sums, dn_got, dn_mine = fence(
        gq, gkv, grads, grad_even, grad_odd, out_sums, dn_got, dn_mine
    )
    out_got = spread(out_sums)
    gkv_others = [links.climb(grads[step - 1], -step) for step in range(1, ng)]
    wo_weight = call(
        out_grad_kernel,
        [hbm((D, OUT_SLAB))],
        [grad_even, grad_odd, att, nge, ngo],
        scratch=[vm((half_rows, QH), BF16), vm((half_rows, QH), BF16)],
        room=3,
        busy=20,
    )[0]
    dn_kept = fold(dn_mine, dn_got)
    gkv_others, gq, gkv, out_got, wo_weight, dn_kept = fence(
        gkv_others, gq, gkv, out_got, wo_weight, dn_kept
    )
    dn_groups = send_groups(dn_kept)
    gqkv, even, odd = call(
        functools.partial(close_kernel, ng),
        [bf((out_rows, SLAB)), bf((half_rows, D)), bf((half_rows, D))],
        [gq, wq, gkv] + list(gkv_others),
        room=3,
    )
    odd, gqkv, even = fence(odd, gqkv, even)
    odd_got = links.core(odd)
    gu_kept = fold(gu_mine, gu_got)
    qkvo_other, qkvo_mine = call(
        qkv_grad_kernel,
        [bf((D // 2, SLAB + OUT_SLAB))] * 2,
        [xg, gqkv, wo_weight],
        room=3,
    )
    odd_got, gu_kept, qkvo_other, even, dn_groups = fence(
        odd_got, gu_kept, qkvo_other, even, dn_groups
    )
    gu_groups = send_groups(gu_kept)
    qkvo_got = links.outer(qkvo_other, 1, 0)
    sums = pair(even, odd_got)
    got = spread(sums)
    qkvo_kept = fold(qkvo_mine, qkvo_got)
    sums, got, qkvo_kept = fence(sums, got, qkvo_kept)
    qkvo_groups = send_groups(qkvo_kept)
    grad_tokens = call(
        tokens_kernel, [bf((rows, D))], [sums[0]] + list(got) + [tok, grad_mixed, gain1]
    )[0]
    gu_groups, grad_tokens = fence(gu_groups, grad_tokens)
    moe_sum = call(
        functools.partial(fold_last_kernel, ng),
        [bf((CUBE * wr, 3 * HALF))],
        list(gu_groups) + list(dn_groups),
        room=2,
    )[0]
    expert_parts = links.swap(moe_sum.reshape(CUBE, wr, 3 * HALF))
    cuts = call(
        functools.partial(fold_parts_kernel, ng),
        [bf((wr, SLAB + OUT_SLAB))] * CUBE,
        qkvo_groups,
        scratch=[vm((CUBE, wr, SLAB + OUT_SLAB), BF16)],
        room=2,
    )
    qkvo_parts = [cuts[0]] + [links.cube(cuts[k], k) for k in range(1, CUBE)]
    output = call(output_kernel, [bf((rows, D))], [out_sums[0]] + list(out_got) + [mixed])[0]
    grad_qkv, grad_attn_gain, grad_out, grad_router = call(
        finish_attention_kernel,
        [f32(wr, QW + 2 * KW), f32(1, wr), f32(wr, QW), f32(8, wr)],
        [qkv_weight, attn_gain.reshape(1, wr)] + qkvo_parts,
        scratch=[vm((CUBE, wr, SLAB + OUT_SLAB), BF16)],
        room=3,
    )
    grad_gateup, grad_moe_gain, grad_down = call(
        finish_experts_kernel,
        [f32(E, wr, 2 * FF), f32(1, wr), f32(E, wr, FF)],
        [expert_parts, gateup_weight, grad_router, router.T, moe_gain.reshape(1, wr)],
        room=3,
    )
    return (
        output.reshape(MB, 1, slots, D),
        grad_tokens.reshape(MB, 1, slots, D),
        grad_attn_gain.reshape(wr),
        grad_qkv,
        grad_out.T,
        grad_moe_gain.reshape(wr),
        grad_router[:E].T,
        grad_gateup,
        grad_down.transpose(0, 2, 1),
    )


def solution(mesh):
    in_specs = (
        P(None, "dp", "ctx", None),
        P(None, "dp"),
        P(None, "dp", "ctx", None),
        P(None, "dp", "ctx", None),
        P(("dp", "ctx")),
        P(("dp", "ctx"), None),
        P(None, ("dp", "ctx")),
        P(("dp", "ctx")),
        P(("dp", "ctx"), None),
        P(None, ("dp", "ctx"), None),
        P(None, None, ("dp", "ctx")),
    )
    out_specs = (
        P(None, "dp", "ctx", None),
        P(None, "dp", "ctx", None),
        P(("dp", "ctx")),
        P(("dp", "ctx"), None),
        P(None, ("dp", "ctx")),
        P(("dp", "ctx")),
        P(("dp", "ctx"), None),
        P(None, ("dp", "ctx"), None),
        P(None, None, ("dp", "ctx")),
    )
    return jax.shard_map(body, mesh=mesh, in_specs=in_specs, out_specs=out_specs, check_vma=False)
```

time: 522 us -> 461 us (0.88)
  local copies, waits for them, and re-layouts: 60.6 us -> 21.9 us
  other arithmetic: 17.7 us -> 0.01 us
    ppermute x62 -> x35, waiting for transfers between devices: 66.5 us -> 106 us  [cube(): lax.ppermute(value, AXES, self._pairs(lambda x, g, t: (x, g, t ^ bits)))]
    ppermute x15, waiting for transfers between devices: 112 us -> 89.8 us  [outer(): lax.ppermute(value, AXES, self._pairs(lambda x, g, t: (x ^ dx, g ^ dg, t)))]
    transpose x14 -> x1, local copies, waits for them, and re-layouts: 18 us -> 0.58 us  [body(): grad_router[:E]]
    all_to_all x6 -> x3, waiting for transfers between devices: 16.8 us -> 2.07 us  [swap(): lax.all_to_all(value, AXES, split_axis=0, concat_axis=0, tiled=True, axis...]
    reshape x16 -> x0, local copies, waits for them, and re-layouts: 10.1 us -> none  [the longest x2 5.25 us: body(): gu_unit = moe_f[:, :, :2 * HALF].reshape(E, 2, wr, 2, HALF).transpose(0,...]
    slice x13 -> x0, local copies, waits for them, and re-layouts: 9.42 us -> none  [the longest x4 3.8 us: cube_gather(): high = self.cube(side[half:], 4)]
    all_to_all x6 -> x3, starting transfers between devices: 22 us -> 13.1 us  [swap(): lax.all_to_all(value, AXES, split_axis=0, concat_axis=0, tiled=True, axis...]
    convert_element_type x12 -> x0, other arithmetic: 8.68 us -> none  [the longest x1 3.02 us: body(): moe_grad = links.swap(moe_sum.astype(BF16).reshape(CUBE, wr, 3 * HALF))]
  transfers between devices with their start and end apart: 86 -> 56, of which waited for: 24 -> 28; matrix products, arithmetic and copies ran while one was open for 10% -> 0% of each run, Pallas kernels for 18% -> 18%
where the time goes in v2:
time: 461 us; the launch traced here: 457 us
  waiting for transfers between devices  211 us (46%)
  Pallas kernels  106 us (23%)
  starting transfers between devices  103 us (22%)
  local copies, waits for them, and re-layouts  21.9 us (5%)
  between operations  14.9 us (3%)
    pallas_call x33, Pallas kernels, __call__(): pl.pallas_call(run, out_shape=list(outs), in_specs=[pl.BlockSpec(memory_s...  106 us
    ppermute x35, waiting for transfers between devices, cube(): lax.ppermute(value, AXES, self._pairs(lambda x, g, t: (x, g, t ^ bits)))  106 us
    ppermute x15, waiting for transfers between devices, outer(): lax.ppermute(value, AXES, self._pairs(lambda x, g, t: (x ^ dx, g ^ dg, t)))  89.8 us
    ppermute x35, starting transfers between devices, cube(): lax.ppermute(value, AXES, self._pairs(lambda x, g, t: (x, g, t ^ bits)))  54.6 us
    ppermute x15, starting transfers between devices, outer(): lax.ppermute(value, AXES, self._pairs(lambda x, g, t: (x ^ dx, g ^ dg, t)))  31.5 us
    unnamed x124, local copies, waits for them, and re-layouts  21.4 us
    all_to_all x3, starting transfers between devices, swap(): lax.all_to_all(value, AXES, split_axis=0, concat_axis=0, tiled=True, axis...  13.1 us
    ppermute x2, waiting for transfers between devices, climb(): return lax.ppermute(value, AXES, self._pairs(move))  12.5 us
  transfers between devices with their start and end apart: 56, of which 28 were waited for; matrix products, arithmetic and copies ran while one was open for 0% of the time, Pallas kernels for 18%

profile of v2, /device:TPU:0, one launch (start us, length us, event | category | flops | bytes accessed | tf_op | source)
XLA Modules:
  0.0 457.3 jit_solution(15769181054503603534)
XLA Ops:
  18.9 5.3 %all-to-all-start = ((bf16[8,48,384]{2,1,0:T(8,128)(2,1)}), bf16[8,48,384]{2,1,0:T(8,128)(2,1)}, u32[]{:S(2)}, u32[]{:S(2)}) async-start(bf16[8,48,384]{2,1,0:T(8,128)(2,1)} %get-tuple-element.216), calls=%async_computation | async-start | bytes 589824 | tf_op jit(solution)/shard_map/all_to_all | solution.py:126
  27.7 15.2 %collective-permute-done.2.refs_3_ = bf16[128,1664]{1,0:T(8,128)(2,1)S(1)} collective-permute-done((bf16[128,1664]{1,0:T(8,128)(2,1)S(1)}, bf16[128,1664]{1,0:T(8,128)(2,1)S(1)}, u32[]{:S(2)}, u32[]{:S(2)}) %collective-permute-start.2) | collective-permute-done | bytes 426016 | tf_op jit(solution)/shard_map/ppermute | solution.py:107
  42.8 7.1 %collective-permute-done.1.refs_2_ = bf16[128,1664]{1,0:T(8,128)(2,1)S(1)} collective-permute-done((bf16[128,1664]{1,0:T(8,128)(2,1)S(1)}, bf16[128,1664]{1,0:T(8,128)(2,1)S(1)}, u32[]{:S(2)}, u32[]{:S(2)}) %collective-permute-start.1) | collective-permute-done | bytes 426016 | tf_op jit(solution)/shard_map/ppermute | solution.py:107
  53.0 4.3 all-to-all-start.1
  57.6 3.7 collective-permute-start.6
  62.0 19.9 %collective-permute-done.6.refs_5_ = bf16[384,384]{1,0:T(8,128)(2,1)S(1)} collective-permute-done((bf16[384,384]{1,0:T(8,128)(2,1)}, bf16[384,384]{1,0:T(8,128)(2,1)S(1)}, u32[]{:S(2)}, u32[]{:S(2)}) %collective-permute-start.6) | collective-permute-done | bytes 294944 | tf_op jit(solution)/shard_map/ppermute | solution.py:110
  82.6 7.0 %collective-permute-done.4.refs_3_ = bf16[384,384]{1,0:T(8,128)(2,1)S(1)} collective-permute-done((bf16[384,384]{1,0:T(8,128)(2,1)}, bf16[384,384]{1,0:T(8,128)(2,1)S(1)}, u32[]{:S(2)}, u32[]{:S(2)}) %collective-permute-start.4) | collective-permute-done | bytes 294944 | tf_op jit(solution)/shard_map/ppermute | solution.py:110
  92.4 6.0 %shard_map.181 = (bf16[1024,1536]{1,0:T(8,128)(2,1)}, bf16[2,3,512,128]{3,2,1,0:T(8,128)(2,1)S(1)}, bf16[2,512,128]{2,1,0:T(8,128)(2,1)S(1)}, f32[8,1536]{1,0:T(8,128)}, bf16[1536,384]{1,0:T(8,128)(2,1)}) custom-call(s32[2,1]{1,0:T(2,128)S(1)} %copy.43.lengths, bf16[512,1664]{1,0:T(8,128)(2,1)S(1)} %shard_map.180.refs_0_.refs_2_, ...), custom_call_target="tpu_custom_call" | custom-call | flops 1000 | bytes 1000 | tf_op jit(solution)/shard_map/pallas_call | solution.py:62
  105.9 6.4 %collective-permute-start.12 = (bf16[128,1536]{1,0:T(8,128)(2,1)S(1)}, bf16[128,1536]{1,0:T(8,128)(2,1)S(1)}, u32[]{:S(2)}, u32[]{:S(2)}) collective-permute-start(bf16[128,1536]{1,0:T(8,128)(2,1)S(1)} %bitcast.25), channel_id=1, source_target_pairs={{0,6},{1,7},{2,4},{3,5},{4,2},{5,3},{6,0},{7,1},{8,14},{9,15},{10,... | collective-permute-start | bytes 1179656 | tf_op jit(solution)/shard_map/ppermute | solution.py:107
  114.4 13.2 %collective-permute-start.10 = (bf16[128,1536]{1,0:T(8,128)(2,1)S(1)}, bf16[128,1536]{1,0:T(8,128)(2,1)S(1)}, u32[]{:S(2)}, u32[]{:S(2)}) collective-permute-start(bf16[128,1536]{1,0:T(8,128)(2,1)S(1)} %bitcast.27), channel_id=1, source_target_pairs={{0,4},{1,5},{2,6},{3,7},{4,0},{5,1},{6,2},{7,3},{8,12},{9,13},{10,... | collective-permute-start | bytes 1179656 | tf_op jit(solution)/shard_map/ppermute | solution.py:107
  130.9 5.9 %collective-permute-done.10.refs_1_ = bf16[128,1536]{1,0:T(8,128)(2,1)S(1)} collective-permute-done((bf16[128,1536]{1,0:T(8,128)(2,1)S(1)}, bf16[128,1536]{1,0:T(8,128)(2,1)S(1)}, u32[]{:S(2)}, u32[]{:S(2)}) %collective-permute-start.10) | collective-permute-done | bytes 393248 | tf_op jit(solution)/shard_map/ppermute | solution.py:107
  140.6 7.3 %shard_map.183 = (bf16[512,384]{1,0:T(8,128)(2,1)S(1)}, f32[2,3,64,512]{3,2,1,0:T(8,128)}, f32[2,3,512]{2,1,0:T(4,128)}) custom-call(s32[2,1]{1,0:T(2,128)S(1)} %copy.43.lengths, bf16[2,3,512,128]{3,2,1,0:T(8,128)(2,1)S(1)} %copy-done.3, bf16[2,512,128]{2,1,0:T(8,128)(2,1)S(1)} %copy-done.6, bf16[2,512,128]{2,1,0:T(8,128)(2,1)S(1)} %copy-done.14), custom_call_target="tpu_custom_call" | custom-call | flops 1000 | bytes 1000 | tf_op jit(solution)/shard_map/pallas_call | solution.py:62
  152.0 7.8 %collective-permute-start.19 = (bf16[384,1024]{1,0:T(8,128)(2,1)S(1)}, bf16[384,1024]{1,0:T(8,128)(2,1)S(1)}, u32[]{:S(2)}, u32[]{:S(2)}) collective-permute-start(bf16[384,1024]{1,0:T(8,128)(2,1)S(1)} %copy-done.23), channel_id=1, source_target_pairs={{0,8},{1,9},{2,10},{3,11},{4,12},{5,13},{6,14},{7,15},{8,0},{9,1},... | collective-permute-start | bytes 2359304 | tf_op jit(solution)/shard_map/ppermute | solution.py:110
  163.7 5.9 %collective-permute-done.18.refs_5_ = bf16[384,512]{1,0:T(8,128)(2,1)S(1)} collective-permute-done((bf16[384,512]{1,0:T(8,128)(2,1)S(1)}, bf16[384,512]{1,0:T(8,128)(2,1)S(1)}, u32[]{:S(2)}, u32[]{:S(2)}) %collective-permute-start.18) | collective-permute-done | bytes 393248 | tf_op jit(solution)/shard_map/ppermute | solution.py:110
  171.9 14.3 %collective-permute-done.15.refs_3_ = bf16[512,384]{1,0:T(8,128)(2,1)S(1)} collective-permute-done((bf16[512,384]{1,0:T(8,128)(2,1)S(1)}, bf16[512,384]{1,0:T(8,128)(2,1)S(1)}, u32[]{:S(2)}, u32[]{:S(2)}) %collective-permute-start.15) | collective-permute-done | bytes 393248 | tf_op jit(solution)/shard_map/ppermute | solution.py:107
  186.2 9.2 %collective-permute-done.13.refs_1_ = bf16[512,384]{1,0:T(8,128)(2,1)S(1)} collective-permute-done((bf16[512,384]{1,0:T(8,128)(2,1)S(1)}, bf16[512,384]{1,0:T(8,128)(2,1)S(1)}, u32[]{:S(2)}, u32[]{:S(2)}) %collective-permute-start.13) | collective-permute-done | bytes 393248 | tf_op jit(solution)/shard_map/ppermute | solution.py:107
  196.9 4.5 shard_map.186
  201.4 10.5 %shard_map.187 = (bf16[512,1664]{1,0:T(8,128)(2,1)S(1)}, bf16[512,1664]{1,0:T(8,128)(2,1)S(1)}, f32[128,1536]{1,0:T(8,128)}, f32[128,128]{1,0:T(8,128)}) custom-call(s32[2,1]{1,0:T(2,128)S(1)} %copy.43.lengths, bf16[2048,384]{1,0:T(8,128)(2,1)S(1)} %shard_map.185.refs_0_, bf16[2048,384]{1,0:T(8,128)(2,1)S(1)} %collective-permute-done.21.refs_1_, ...), custom_call_target="tpu_custom_call" | custom-call | flops 1000 | bytes 1000 | tf_op jit(solution)/shard_map/pallas_call | solution.py:62
  214.5 6.6 %shard_map.188 = (bf16[512,512]{1,0:T(8,128)(2,1)S(1)}, bf16[512,1024]{1,0:T(8,128)(2,1)S(1)}, bf16[512,1664]{1,0:T(8,128)(2,1)S(1)}, bf16[1536,1024]{1,0:T(8,128)(2,1)S(1)}) custom-call(s32[2,1]{1,0:T(2,128)S(1)} %copy.43.lengths, bf16[512,1664]{1,0:T(8,128)(2,1)S(1)} %get-tuple-element.313.refs_0_.refs_2_.refs_3_.refs_4_, ...), custom_call_target="tpu_custom_call" | custom-call | flops 1000 | bytes 1000 | tf_op jit(solution)/shard_map/pallas_call | solution.py:62
  221.2 16.0 %shard_map.189 = (bf16[512,512]{1,0:T(8,128)(2,1)S(1)}, bf16[512,1024]{1,0:T(8,128)(2,1)S(1)}, bf16[512,1664]{1,0:T(8,128)(2,1)S(1)}) custom-call(s32[2,1]{1,0:T(2,128)S(1)} %copy.43.lengths, bf16[512,1664]{1,0:T(8,128)(2,1)S(1)} %get-tuple-element.312.refs_0_.refs_1_.refs_2_.refs_3_, f32[1024,512]{1,0:T(8,128)S(1)} %get-tuple-element.282.refs_1_, ...), custom_call_target="tpu_custom_call" | custom-call | flops 1000 | bytes 1000 | tf_op jit(solution)/shard_map/pallas_call | solution.py:62
  241.8 9.1 %collective-permute-done.23.refs_1_ = bf16[128,1664]{1,0:T(8,128)(2,1)S(1)} collective-permute-done((bf16[128,1664]{1,0:T(8,128)(2,1)S(1)}, bf16[128,1664]{1,0:T(8,128)(2,1)S(1)}, u32[]{:S(2)}, u32[]{:S(2)}) %collective-permute-start.23) | collective-permute-done | bytes 426016 | tf_op jit(solution)/shard_map/ppermute | solution.py:107
  250.9 10.0 %collective-permute-done.24.refs_2_ = bf16[128,1664]{1,0:T(8,128)(2,1)S(1)} collective-permute-done((bf16[128,1664]{1,0:T(8,128)(2,1)S(1)}, bf16[128,1664]{1,0:T(8,128)(2,1)S(1)}, u32[]{:S(2)}, u32[]{:S(2)}) %collective-permute-start.24) | collective-permute-done | bytes 426016 | tf_op jit(solution)/shard_map/ppermute | solution.py:107
  265.8 7.0 %shard_map.193 = (bf16[768,1024]{1,0:T(8,128)(2,1)S(1)}, bf16[768,512]{1,0:T(8,128)(2,1)S(1)}, bf16[768,1024]{1,0:T(8,128)(2,1)S(1)}, bf16[768,512]{1,0:T(8,128)(2,1)S(1)}) custom-call(s32[2,1]{1,0:T(2,128)S(1)} %copy.43.lengths, bf16[512,1536]{1,0:T(8,128)(2,1)S(1)} %shard_map.184.refs_0_, bf16[512,1536]{1,0:T(8,128)(2,1)S(1)} %collective-permute-done.16.refs_1_, ...), custom_call_target="tpu_custom_call" | custom-call | flops 20000000000 | bytes 1000 | tf_op jit(solution)/shard_map/pallas_call | solution.py:62
  276.0 7.5 %collective-permute-done.27.refs_2_ = bf16[128,1664]{1,0:T(8,128)(2,1)S(1)} collective-permute-done((bf16[128,1664]{1,0:T(8,128)(2,1)S(1)}, bf16[128,1664]{1,0:T(8,128)(2,1)S(1)}, u32[]{:S(2)}, u32[]{:S(2)}) %collective-permute-start.27) | collective-permute-done | bytes 426016 | tf_op jit(solution)/shard_map/ppermute | solution.py:107
  293.6 8.6 %shard_map.196 = (bf16[8,128,192]{2,1,0:T(8,128)(2,1)S(1)}, f32[2,512,128]{2,1,0:T(8,128)S(1)}, bf16[2,512,128]{2,1,0:T(8,128)(2,1)S(1)}) custom-call(s32[2,1]{1,0:T(2,128)S(1)} %copy.43.lengths, bf16[2,3,512,128]{3,2,1,0:T(8,128)(2,1)S(1)} %copy-done.4, bf16[2,512,128]{2,1,0:T(8,128)(2,1)S(1)} %copy-done.7, bf16[2,512,128]{2,1,0:T(8,128)(2,1)S(1)} %copy-done.15, ...), custom_call_target="tpu_custom_call" | custom-call | flops 1000 | bytes 1000 | tf_op jit(solution)/shard_map/pallas_call | solution.py:62
  310.0 4.7 %shard_map.198.refs_2_ = bf16[1536,256]{1,0:T(8,128)(2,1)} custom-call(s32[2,1]{1,0:T(2,128)S(1)} %copy.43.lengths, bf16[512,1664]{1,0:T(8,128)(2,1)S(1)} %shard_map.194.refs_1_.refs_0_, bf16[512,1664]{1,0:T(8,128)(2,1)S(1)} %collective-permute-done.29.refs_2_.refs_1_, bf16[512,384]{1,0:T(8,128)(2,1)S(1)} %get-tuple-element.264.refs_0_.refs_2_, ...), custom_call_target="tpu_custom_call" | custom-call | flops 20000000000 | bytes 1000 | tf_op jit(solution)/shard_map/pallas_call | solution.py:62
  315.4 12.5 %collective-permute-done.32.refs_3_ = bf16[2,512,128]{2,1,0:T(8,128)(2,1)S(1)} collective-permute-done((bf16[2,512,128]{2,1,0:T(8,128)(2,1)S(1)}, bf16[2,512,128]{2,1,0:T(8,128)(2,1)S(1)}, u32[]{:S(2)}, u32[]{:S(2)}) %collective-permute-start.32) | collective-permute-done | bytes 262176 | tf_op jit(solution)/shard_map/ppermute | solution.py:116
  334.5 10.3 %collective-permute-start.38 = (bf16[384,512]{1,0:T(8,128)(2,1)S(1)}, bf16[384,512]{1,0:T(8,128)(2,1)S(1)}, u32[]{:S(2)}, u32[]{:S(2)}) collective-permute-start(bf16[384,512]{1,0:T(8,128)(2,1)S(1)} %get-tuple-element.376), channel_id=1, source_target_pairs={{0,8},{1,9},{2,10},{3,11},{4,12},{5,13},{6,14},{7,15},{8,0},{9,1},... | collective-permute-start | bytes 1179656 | tf_op jit(solution)/shard_map/ppermute | solution.py:110
  349.3 12.2 %collective-permute-done.38.refs_3_ = bf16[384,512]{1,0:T(8,128)(2,1)S(1)} collective-permute-done((bf16[384,512]{1,0:T(8,128)(2,1)S(1)}, bf16[384,512]{1,0:T(8,128)(2,1)S(1)}, u32[]{:S(2)}, u32[]{:S(2)}) %collective-permute-start.38) | collective-permute-done | bytes 393248 | tf_op jit(solution)/shard_map/ppermute | solution.py:110
  368.9 16.3 %collective-permute-done.43.refs_1_ = bf16[768,640]{1,0:T(8,128)(2,1)S(1)} collective-permute-done((bf16[768,640]{1,0:T(8,128)(2,1)S(1)}, bf16[768,640]{1,0:T(8,128)(2,1)S(1)}, u32[]{:S(2)}, u32[]{:S(2)}) %collective-permute-start.43) | collective-permute-done | bytes 983072 | tf_op jit(solution)/shard_map/ppermute | solution.py:110
  389.6 11.9 %collective-permute-done.42.refs_3_ = bf16[128,1536]{1,0:T(8,128)(2,1)S(1)} collective-permute-done((bf16[128,1536]{1,0:T(8,128)(2,1)S(1)}, bf16[128,1536]{1,0:T(8,128)(2,1)S(1)}, u32[]{:S(2)}, u32[]{:S(2)}) %collective-permute-start.42) | collective-permute-done | bytes 393248 | tf_op jit(solution)/shard_map/ppermute | solution.py:107
  409.2 23.8 %collective-permute-done.44.refs_1_ = bf16[384,640]{1,0:T(8,128)(2,1)S(1)} collective-permute-done((bf16[384,640]{1,0:T(8,128)(2,1)}, bf16[384,640]{1,0:T(8,128)(2,1)S(1)}, u32[]{:S(2)}, u32[]{:S(2)}) %collective-permute-start.44) | collective-permute-done | bytes 491552 | tf_op jit(solution)/shard_map/ppermute | solution.py:110
  (240 shorter events, 132.5 us)
Async XLA Ops:
  7.2 130.4 %all-gather.2.cloned.1.call-start = ((), (), s32[]{:S(2)}) async-start(), calls=%async_computation.3 | async-start | bytes 5271552 | tf_op jit(solution)/shard_map/all_gather | solution.py:786
  18.9 33.4 %all-to-all-start = ((bf16[8,48,384]{2,1,0:T(8,128)(2,1)}), bf16[8,48,384]{2,1,0:T(8,128)(2,1)}, u32[]{:S(2)}, u32[]{:S(2)}) async-start(bf16[8,48,384]{2,1,0:T(8,128)(2,1)} %get-tuple-element.216), calls=%async_computation | async-start | bytes 589824 | tf_op jit(solution)/shard_map/all_to_all | solution.py:126
  27.1 22.9 %collective-permute-start.1 = (bf16[128,1664]{1,0:T(8,128)(2,1)S(1)}, bf16[128,1664]{1,0:T(8,128)(2,1)S(1)}, u32[]{:S(2)}, u32[]{:S(2)}) collective-permute-start(bf16[128,1664]{1,0:T(8,128)(2,1)S(1)} %get-tuple-element.220.refs_0_), channel_id=1, source_target_pairs={{0,2},{1,3},{2,0},{3,1},{4,6},{5,7},{6,4},{7,5},{8,10},{9,11},{10,... | collective-permute-start | bytes 1277960 | tf_op jit(solution)/shard_map/ppermute | solution.py:107
  27.6 24.7 %collective-permute-start = (bf16[128,1664]{1,0:T(8,128)(2,1)S(1)}, bf16[128,1664]{1,0:T(8,128)(2,1)S(1)}, u32[]{:S(2)}, u32[]{:S(2)}) collective-permute-start(bf16[128,1664]{1,0:T(8,128)(2,1)S(1)} %get-tuple-element.220.refs_0_), channel_id=1, source_target_pairs={{0,4},{1,5},{2,6},{3,7},{4,0},{5,1},{6,2},{7,3},{8,12},{9,13},{10,... | collective-permute-start | bytes 1277960 | tf_op jit(solution)/shard_map/ppermute | solution.py:107
  53.0 39.4 %all-to-all-start.1 = ((bf16[8,48,1536]{2,1,0:T(8,128)(2,1)}), bf16[8,48,1536]{2,1,0:T(8,128)(2,1)}, u32[]{:S(2)}, u32[]{:S(2)}) async-start(bf16[8,48,1536]{2,1,0:T(8,128)(2,1)} %get-tuple-element.228), calls=%async_computation.1 | async-start | bytes 2359296 | tf_op jit(solution)/shard_map/all_to_all | solution.py:126
  57.2 33.1 %collective-permute-start.3 = (bf16[512,1664]{1,0:T(8,128)(2,1)S(1)}, bf16[512,1664]{1,0:T(8,128)(2,1)S(1)}, u32[]{:S(2)}, u32[]{:S(2)}) collective-permute-start(bf16[512,1664]{1,0:T(8,128)(2,1)S(1)} %shard_map.180.refs_0_.refs_2_), channel_id=1, source_target_pairs={{0,1},{1,0},{2,3},{3,2},{4,5},{5,4},{6,7},{7,6},{8,9},{9,8},{10,11... | collective-permute-start | bytes 5111816 | tf_op jit(solution)/shard_map/ppermute | solution.py:107
  57.6 24.2 %collective-permute-start.6 = (bf16[384,384]{1,0:T(8,128)(2,1)}, bf16[384,384]{1,0:T(8,128)(2,1)S(1)}, u32[]{:S(2)}, u32[]{:S(2)}) collective-permute-start(bf16[384,384]{1,0:T(8,128)(2,1)} %bitcast.4.refs_2_), channel_id=1, source_target_pairs={{0,24},{1,25},{2,26},{3,27},{4,28},{5,29},{6,30},{7,31},{8,16},{9,... | collective-permute-start | bytes 884744 | tf_op jit(solution)/shard_map/ppermute | solution.py:110
  61.3 20.6 %collective-permute-start.5 = (bf16[384,384]{1,0:T(8,128)(2,1)}, bf16[384,384]{1,0:T(8,128)(2,1)S(1)}, u32[]{:S(2)}, u32[]{:S(2)}) collective-permute-start(bf16[384,384]{1,0:T(8,128)(2,1)} %bitcast.4.refs_2_), channel_id=1, source_target_pairs={{0,16},{1,17},{2,18},{3,19},{4,20},{5,21},{6,22},{7,23},{8,24},{9,... | collective-permute-start | bytes 884744 | tf_op jit(solution)/shard_map/ppermute | solution.py:110
  61.8 27.8 %collective-permute-start.4 = (bf16[384,384]{1,0:T(8,128)(2,1)}, bf16[384,384]{1,0:T(8,128)(2,1)S(1)}, u32[]{:S(2)}, u32[]{:S(2)}) collective-permute-start(bf16[384,384]{1,0:T(8,128)(2,1)} %bitcast.4.refs_2_), channel_id=1, source_target_pairs={{0,8},{1,9},{2,10},{3,11},{4,12},{5,13},{6,14},{7,15},{8,0},{9,1},... | collective-permute-start | bytes 884744 | tf_op jit(solution)/shard_map/ppermute | solution.py:110
  100.8 36.7 %collective-permute-start.9 = (bf16[384,1024]{1,0:T(8,128)(2,1)S(1)}, bf16[384,1024]{1,0:T(8,128)(2,1)}, u32[]{:S(2)}, u32[]{:S(2)}) collective-permute-start(bf16[384,1024]{1,0:T(8,128)(2,1)S(1)} %get-tuple-element.283.refs_2_), channel_id=1, source_target_pairs={{0,16},{1,17},{2,18},{3,19},{4,20},{5,21},{6,22},{7,23},{8,24},{9,... | collective-permute-start | bytes 2359304 | tf_op jit(solution)/shard_map/ppermute | solution.py:110
  105.8 21.8 %collective-permute-start.8 = (bf16[384,512]{1,0:T(8,128)(2,1)S(1)}, bf16[384,512]{1,0:T(8,128)(2,1)S(1)}, u32[]{:S(2)}, u32[]{:S(2)}) collective-permute-start(bf16[384,512]{1,0:T(8,128)(2,1)S(1)} %get-tuple-element.273.refs_2_), channel_id=1, source_target_pairs={{0,8},{1,9},{2,10},{3,11},{4,12},{5,13},{6,14},{7,15},{8,0},{9,1},... | collective-permute-start | bytes 1179656 | tf_op jit(solution)/shard_map/ppermute | solution.py:110
  105.9 22.7 %collective-permute-start.12 = (bf16[128,1536]{1,0:T(8,128)(2,1)S(1)}, bf16[128,1536]{1,0:T(8,128)(2,1)S(1)}, u32[]{:S(2)}, u32[]{:S(2)}) collective-permute-start(bf16[128,1536]{1,0:T(8,128)(2,1)S(1)} %bitcast.25), channel_id=1, source_target_pairs={{0,6},{1,7},{2,4},{3,5},{4,2},{5,3},{6,0},{7,1},{8,14},{9,15},{10,... | collective-permute-start | bytes 1179656 | tf_op jit(solution)/shard_map/ppermute | solution.py:107
  114.4 22.4 %collective-permute-start.10 = (bf16[128,1536]{1,0:T(8,128)(2,1)S(1)}, bf16[128,1536]{1,0:T(8,128)(2,1)S(1)}, u32[]{:S(2)}, u32[]{:S(2)}) collective-permute-start(bf16[128,1536]{1,0:T(8,128)(2,1)S(1)} %bitcast.27), channel_id=1, source_target_pairs={{0,4},{1,5},{2,6},{3,7},{4,0},{5,1},{6,2},{7,3},{8,12},{9,13},{10,... | collective-permute-start | bytes 1179656 | tf_op jit(solution)/shard_map/ppermute | solution.py:107
  149.6 45.9 %collective-permute-start.16 = (bf16[512,1536]{1,0:T(8,128)(2,1)S(1)}, bf16[512,1536]{1,0:T(8,128)(2,1)S(1)}, u32[]{:S(2)}, u32[]{:S(2)}) collective-permute-start(bf16[512,1536]{1,0:T(8,128)(2,1)S(1)} %shard_map.184.refs_0_), channel_id=1, source_target_pairs={{0,1},{1,0},{2,3},{3,2},{4,5},{5,4},{6,7},{7,6},{8,9},{9,8},{10,11... | collective-permute-start | bytes 4718600 | tf_op jit(solution)/shard_map/ppermute | solution.py:107
  152.0 43.5 %collective-permute-start.19 = (bf16[384,1024]{1,0:T(8,128)(2,1)S(1)}, bf16[384,1024]{1,0:T(8,128)(2,1)S(1)}, u32[]{:S(2)}, u32[]{:S(2)}) collective-permute-start(bf16[384,1024]{1,0:T(8,128)(2,1)S(1)} %copy-done.23), channel_id=1, source_target_pairs={{0,8},{1,9},{2,10},{3,11},{4,12},{5,13},{6,14},{7,15},{8,0},{9,1},... | collective-permute-start | bytes 2359304 | tf_op jit(solution)/shard_map/ppermute | solution.py:110
  159.8 26.4 %collective-permute-start.15 = (bf16[512,384]{1,0:T(8,128)(2,1)S(1)}, bf16[512,384]{1,0:T(8,128)(2,1)S(1)}, u32[]{:S(2)}, u32[]{:S(2)}) collective-permute-start(bf16[512,384]{1,0:T(8,128)(2,1)S(1)} %get-tuple-element.264.refs_0_.refs_2_), channel_id=1, source_target_pairs={{0,6},{1,7},{2,4},{3,5},{4,2},{5,3},{6,0},{7,1},{8,14},{9,15},{10,... | collective-permute-start | bytes 1179656 | tf_op jit(solution)/shard_map/ppermute | solution.py:107
  162.8 23.5 %collective-permute-start.14 = (bf16[512,384]{1,0:T(8,128)(2,1)S(1)}, bf16[512,384]{1,0:T(8,128)(2,1)S(1)}, u32[]{:S(2)}, u32[]{:S(2)}) collective-permute-start(bf16[512,384]{1,0:T(8,128)(2,1)S(1)} %get-tuple-element.264.refs_0_.refs_2_), channel_id=1, source_target_pairs={{0,2},{1,3},{2,0},{3,1},{4,6},{5,7},{6,4},{7,5},{8,10},{9,11},{10,... | collective-permute-start | bytes 1179656 | tf_op jit(solution)/shard_map/ppermute | solution.py:107
  169.6 25.8 %collective-permute-start.13 = (bf16[512,384]{1,0:T(8,128)(2,1)S(1)}, bf16[512,384]{1,0:T(8,128)(2,1)S(1)}, u32[]{:S(2)}, u32[]{:S(2)}) collective-permute-start(bf16[512,384]{1,0:T(8,128)(2,1)S(1)} %get-tuple-element.264.refs_0_.refs_2_), channel_id=1, source_target_pairs={{0,4},{1,5},{2,6},{3,7},{4,0},{5,1},{6,2},{7,3},{8,12},{9,13},{10,... | collective-permute-start | bytes 1179656 | tf_op jit(solution)/shard_map/ppermute | solution.py:107
  239.9 21.1 %collective-permute-start.24 = (bf16[128,1664]{1,0:T(8,128)(2,1)S(1)}, bf16[128,1664]{1,0:T(8,128)(2,1)S(1)}, u32[]{:S(2)}, u32[]{:S(2)}) collective-permute-start(bf16[128,1664]{1,0:T(8,128)(2,1)S(1)} %get-tuple-element.299), channel_id=1, source_target_pairs={{0,2},{1,3},{2,0},{3,1},{4,6},{5,7},{6,4},{7,5},{8,10},{9,11},{10,... | collective-permute-start | bytes 1277960 | tf_op jit(solution)/shard_map/ppermute | solution.py:107
  286.4 58.4 %collective-permute-start.37 = (bf16[768,1024]{1,0:T(8,128)(2,1)S(1)}, bf16[768,1024]{1,0:T(8,128)(2,1)S(1)}, u32[]{:S(2)}, u32[]{:S(2)}) collective-permute-start(bf16[768,1024]{1,0:T(8,128)(2,1)S(1)} %get-tuple-element.367), channel_id=1, source_target_pairs={{0,16},{1,17},{2,18},{3,19},{4,20},{5,21},{6,22},{7,23},{8,24},{9,... | collective-permute-start | bytes 4718600 | tf_op jit(solution)/shard_map/ppermute | solution.py:110
  305.1 22.8 %collective-permute-start.32 = (bf16[2,512,128]{2,1,0:T(8,128)(2,1)S(1)}, bf16[2,512,128]{2,1,0:T(8,128)(2,1)S(1)}, u32[]{:S(2)}, u32[]{:S(2)}) collective-permute-start(bf16[2,512,128]{2,1,0:T(8,128)(2,1)S(1)} %get-tuple-element.343), channel_id=1, source_target_pairs={{8,0},{9,1},{10,2},{11,3},{12,4},{13,5},{14,6},{15,7},{24,16},{25,... | collective-permute-start | bytes 786440 | tf_op jit(solution)/shard_map/ppermute | solution.py:116
  306.4 21.5 %collective-permute-start.33 = (bf16[128,1536]{1,0:T(8,128)(2,1)S(1)}, bf16[128,1536]{1,0:T(8,128)(2,1)S(1)}, u32[]{:S(2)}, u32[]{:S(2)}) collective-permute-start(bf16[128,1536]{1,0:T(8,128)(2,1)S(1)} %get-tuple-element.346), channel_id=1, source_target_pairs={{0,4},{1,5},{2,6},{3,7},{4,0},{5,1},{6,2},{7,3},{8,12},{9,13},{10,... | collective-permute-start | bytes 1179656 | tf_op jit(solution)/shard_map/ppermute | solution.py:107
  308.5 21.9 %collective-permute-start.35 = (bf16[128,1536]{1,0:T(8,128)(2,1)S(1)}, bf16[128,1536]{1,0:T(8,128)(2,1)S(1)}, u32[]{:S(2)}, u32[]{:S(2)}) collective-permute-start(bf16[128,1536]{1,0:T(8,128)(2,1)S(1)} %get-tuple-element.348), channel_id=1, source_target_pairs={{0,6},{1,7},{2,4},{3,5},{4,2},{5,3},{6,0},{7,1},{8,14},{9,15},{10,... | collective-permute-start | bytes 1179656 | tf_op jit(solution)/shard_map/ppermute | solution.py:107
  334.4 27.1 %collective-permute-start.36 = (bf16[512,1536]{1,0:T(8,128)(2,1)S(1)}, bf16[512,1536]{1,0:T(8,128)(2,1)S(1)}, u32[]{:S(2)}, u32[]{:S(2)}) collective-permute-start(bf16[512,1536]{1,0:T(8,128)(2,1)S(1)} %get-tuple-element.365), channel_id=1, source_target_pairs={{0,1},{1,0},{2,3},{3,2},{4,5},{5,4},{6,7},{7,6},{8,9},{9,8},{10,11... | collective-permute-start | bytes 4718600 | tf_op jit(solution)/shard_map/ppermute | solution.py:107
  334.5 27.0 %collective-permute-start.38 = (bf16[384,512]{1,0:T(8,128)(2,1)S(1)}, bf16[384,512]{1,0:T(8,128)(2,1)S(1)}, u32[]{:S(2)}, u32[]{:S(2)}) collective-permute-start(bf16[384,512]{1,0:T(8,128)(2,1)S(1)} %get-tuple-element.376), channel_id=1, source_target_pairs={{0,8},{1,9},{2,10},{3,11},{4,12},{5,13},{6,14},{7,15},{8,0},{9,1},... | collective-permute-start | bytes 1179656 | tf_op jit(solution)/shard_map/ppermute | solution.py:110
  361.5 23.8 %collective-permute-start.43 = (bf16[768,640]{1,0:T(8,128)(2,1)S(1)}, bf16[768,640]{1,0:T(8,128)(2,1)S(1)}, u32[]{:S(2)}, u32[]{:S(2)}) collective-permute-start(bf16[768,640]{1,0:T(8,128)(2,1)S(1)} %get-tuple-element.386), channel_id=1, source_target_pairs={{0,16},{1,17},{2,18},{3,19},{4,20},{5,21},{6,22},{7,23},{8,24},{9,... | collective-permute-start | bytes 2949128 | tf_op jit(solution)/shard_map/ppermute | solution.py:110
  363.2 40.2 %collective-permute-start.39 = (bf16[384,1024]{1,0:T(8,128)(2,1)S(1)}, bf16[384,1024]{1,0:T(8,128)(2,1)S(1)}, u32[]{:S(2)}, u32[]{:S(2)}) collective-permute-start(bf16[384,1024]{1,0:T(8,128)(2,1)S(1)} %get-tuple-element.378), channel_id=1, source_target_pairs={{0,8},{1,9},{2,10},{3,11},{4,12},{5,13},{6,14},{7,15},{8,0},{9,1},... | collective-permute-start | bytes 2359304 | tf_op jit(solution)/shard_map/ppermute | solution.py:110
  364.1 25.4 %collective-permute-start.40 = (bf16[128,1536]{1,0:T(8,128)(2,1)S(1)}, bf16[128,1536]{1,0:T(8,128)(2,1)S(1)}, u32[]{:S(2)}, u32[]{:S(2)}) collective-permute-start(bf16[128,1536]{1,0:T(8,128)(2,1)S(1)} %get-tuple-element.382), channel_id=1, source_target_pairs={{0,4},{1,5},{2,6},{3,7},{4,0},{5,1},{6,2},{7,3},{8,12},{9,13},{10,... | collective-permute-start | bytes 1179656 | tf_op jit(solution)/shard_map/ppermute | solution.py:107
  367.4 22.2 %collective-permute-start.41 = (bf16[128,1536]{1,0:T(8,128)(2,1)S(1)}, bf16[128,1536]{1,0:T(8,128)(2,1)S(1)}, u32[]{:S(2)}, u32[]{:S(2)}) collective-permute-start(bf16[128,1536]{1,0:T(8,128)(2,1)S(1)} %get-tuple-element.383), channel_id=1, source_target_pairs={{0,2},{1,3},{2,0},{3,1},{4,6},{5,7},{6,4},{7,5},{8,10},{9,11},{10,... | collective-permute-start | bytes 1179656 | tf_op jit(solution)/shard_map/ppermute | solution.py:107
  368.4 33.1 %collective-permute-start.42 = (bf16[128,1536]{1,0:T(8,128)(2,1)S(1)}, bf16[128,1536]{1,0:T(8,128)(2,1)S(1)}, u32[]{:S(2)}, u32[]{:S(2)}) collective-permute-start(bf16[128,1536]{1,0:T(8,128)(2,1)S(1)} %get-tuple-element.384), channel_id=1, source_target_pairs={{0,6},{1,7},{2,4},{3,5},{4,2},{5,3},{6,0},{7,1},{8,14},{9,15},{10,... | collective-permute-start | bytes 1179656 | tf_op jit(solution)/shard_map/ppermute | solution.py:107
  405.1 42.9 %all-to-all-start.2 = ((bf16[8,48,1536]{2,1,0:T(8,128)(2,1)}), bf16[8,48,1536]{2,1,0:T(8,128)(2,1)S(1)}, u32[]{:S(2)}, u32[]{:S(2)}) async-start(bf16[8,48,1536]{2,1,0:T(8,128)(2,1)} %bitcast.16), calls=%async_computation.2 | async-start | bytes 2359296 | tf_op jit(solution)/shard_map/all_to_all | solution.py:126
  408.7 24.3 %collective-permute-start.44 = (bf16[384,640]{1,0:T(8,128)(2,1)}, bf16[384,640]{1,0:T(8,128)(2,1)S(1)}, u32[]{:S(2)}, u32[]{:S(2)}) collective-permute-start(bf16[384,640]{1,0:T(8,128)(2,1)} %copy-done.45), channel_id=1, source_target_pairs={{0,8},{1,9},{2,10},{3,11},{4,12},{5,13},{6,14},{7,15},{8,0},{9,1},... | collective-permute-start | bytes 1474568 | tf_op jit(solution)/shard_map/ppermute | solution.py:110
  (85 other events, 870.5 us)
Sparse Core Ops, SparseCore 0:
  19.0 88.9 all-gather.1

commit v3 on v2

--- a/solution.py
+++ b/solution.py
@@ -214,19 +214,22 @@
     return jnp.broadcast_to(values, (values.shape[0], EXTRA)).T[0:1, :]
 
 
-def prep_rest_kernel(scal, gu_ref, dn_ref, wo_ref, rt_ref, gain_ref, moe_out, wo_out):
+def prep_out_kernel(scal, wo_ref, rt_ref, gain_ref, wo_out):
+    wr = wo_ref.shape[0]
+    rt = rt_ref[...].astype(F32)
+    rows = jnp.concatenate(
+        [rt, rt, gain_ref[...].astype(F32), jnp.zeros((EXTRA - 2 * E - 1, wr), F32)], axis=0
+    )
+    wo_out[:, :QW] = wo_ref[...]
+    wo_out[:, QW:] = rows.T.astype(BF16)
+
+
+def prep_experts_kernel(scal, gu_ref, dn_ref, moe_out):
     for k in range(CUBE):
         e, h = k // 2, k % 2
         moe_out[k, :, :HALF] = gu_ref[e, :, h * HALF : (h + 1) * HALF]
         moe_out[k, :, HALF : 2 * HALF] = gu_ref[e, :, FF + h * HALF : FF + (h + 1) * HALF]
         moe_out[k, :, 2 * HALF :] = dn_ref[e, :, h * HALF : (h + 1) * HALF]
-    wr = wo_ref.shape[0]
-    rt = rt_ref[...].astype(F32)
-    rows = jnp.concatenate(
-        [rt, rt, gain_ref[...].astype(F32), jnp.zeros((EXTRA - 2 * E - 1, wr), F32)], axis=0
-    )
-    wo_out[:, :QW] = wo_ref[...]
-    wo_out[:, QW:] = rows.T.astype(BF16)
 
 
 def split_kernel(scal, both_ref, gu_ref, dn_ref):
@@ -771,24 +774,30 @@
         [qkv_weight, attn_gain.reshape(1, wr), tok, routes.reshape(rows, 2)],
         room=3,
     )
-    tok_wide, wq_parts, gateup_in, down_in = fence(
-        tok_wide, wq_parts, gateup_weight, down_weight.transpose(0, 2, 1)
-    )
+    tok_wide, wq_parts, out_in = fence(tok_wide, wq_parts, out_weight.T)
     tok_near = links.near(tok_wide)
     wq_group = links.swap(wq_parts).reshape(CUBE * wr, SLAB)
-    moe_parts, wo_part = call(
-        prep_rest_kernel,
-        [bf((CUBE, wr, 3 * HALF)), bf((wr, WIDE))],
-        [gateup_in, down_in, out_weight.T, router.T, moe_gain.reshape(1, wr)],
+    wo_part = call(
+        prep_out_kernel,
+        [bf((wr, WIDE))],
+        [out_in, router.T, moe_gain.reshape(1, wr)],
         room=3,
         busy=20,
-    )
+    )[0]
     wo = lax.all_gather(wo_part, AXES, axis=0, tiled=True)
-    tok_wide, tok_near, wq_group, moe_parts = fence(tok_wide, tok_near, wq_group, moe_parts)
+    wq_group, gateup_in, down_in = fence(
+        wq_group, gateup_weight, down_weight.transpose(0, 2, 1)
+    )
+    moe_parts = call(
+        prep_experts_kernel, [bf((CUBE, wr, 3 * HALF))], [gateup_in, down_in], room=3
+    )[0]
+    tok_wide, tok_near = fence(tok_wide, tok_near)
     tok_even = pack([tok_wide] + list(tok_near))
-    tok_even, wq_group, moe_parts = fence(tok_even, wq_group, moe_parts)
     tok_odd = links.core(tok_even)
-    wq_blocks = links.outer_direct(wq_group)
+    wq_far = [links.outer(wq_group, 0, dg) for dg in range(1, ng)]
+    wq_blocks = [wq_group] + wq_far
+    for dx in range(1, nx):
+        wq_blocks += [links.outer(block, dx, 0) for block in wq_blocks[:ng]]
     moe_group = links.swap(moe_parts).reshape(CUBE * wr, 3 * HALF)
     tok_even, tok_odd, wq_blocks, moe_group, cot = fence(
         tok_even, tok_odd, wq_blocks, moe_group, cot
@@ -808,9 +817,9 @@
         room=4,
     )
     gu_group, dn_group = call(
-        split_kernel, [bf((CUBE * wr, 2 * HALF)), bf((CUBE * wr, HALF))], [moe_group], after=[kv]
-    )
-    kv, dn_group, gu_group, cot = fence(kv, dn_group, gu_group, cot)
+        split_kernel, [bf((CUBE * wr, 2 * HALF)), bf((CUBE * wr, HALF))], [moe_group]
+    )
+    dn_group, gu_group, cot = fence(dn_group, gu_group, cot)
     kvs = [links.climb(kv, step) for step in range(1, ng)]
     cot_near = links.near(cot)
     dn_far = [links.outer(dn_group, 0, dg) for dg in range(1, ng)]
@@ -826,7 +835,7 @@
         [q] + kvs,
         room=10,
     )
-    att, cot_even, dn_group, dn_far, gu_group = fence(att, cot_even, dn_group, dn_far, gu_group)
+    cot_even, dn_group, dn_far, gu_group = fence(cot_even, dn_group, dn_far, gu_group)
     att_near = links.near(att)
     cot_odd = links.core(cot_even)
     dn_blocks = [dn_group] + list(dn_far)
@@ -950,9 +959,7 @@
         [xg, gqkv, wo_weight],
         room=3,
     )
-    odd_got, gu_kept, qkvo_other, even, dn_groups = fence(
-        odd_got, gu_kept, qkvo_other, even, dn_groups
-    )
+    odd_got, gu_kept, even, dn_groups = fence(odd_got, gu_kept, even, dn_groups)
     gu_groups = send_groups(gu_kept)
     qkvo_got = links.outer(qkvo_other, 1, 0)
     sums = pair(even, odd_got)

time: 461 us -> 451 us (0.978)
  waiting for transfers between devices: 211 us -> 199 us
    ppermute x15, waiting for transfers between devices: 89.8 us -> 71.9 us  [outer(): lax.ppermute(value, AXES, self._pairs(lambda x, g, t: (x ^ dx, g ^ dg, t)))]
    ppermute x35, waiting for transfers between devices: 106 us -> 116 us  [cube(): lax.ppermute(value, AXES, self._pairs(lambda x, g, t: (x, g, t ^ bits)))]
    ppermute x2, waiting for transfers between devices: 12.5 us -> 7.86 us  [climb(): return lax.ppermute(value, AXES, self._pairs(move))]
    unnamed x124 -> x130, local copies, waits for them, and re-layouts: 21.4 us -> 24.8 us
    pallas_call x33 -> x34, Pallas kernels: 106 us -> 108 us  [__call__(): pl.pallas_call(run, out_shape=list(outs), in_specs=[pl.BlockSpec(memory_s...]
  transfers between devices with their start and end apart: 56 -> 56, of which waited for: 28 -> 26; matrix products, arithmetic and copies ran while one was open for 0% -> 0% of each run, Pallas kernels for 18% -> 20%
where the time goes in v3:
time: 451 us; the launch traced here: 446 us
  waiting for transfers between devices  199 us (44%)
  Pallas kernels  108 us (24%)
  starting transfers between devices  99.9 us (22%)
  local copies, waits for them, and re-layouts  25.4 us (6%)
  between operations  14.9 us (3%)
    ppermute x35, waiting for transfers between devices, cube(): lax.ppermute(value, AXES, self._pairs(lambda x, g, t: (x, g, t ^ bits)))  116 us
    pallas_call x34, Pallas kernels, __call__(): pl.pallas_call(run, out_shape=list(outs), in_specs=[pl.BlockSpec(memory_s...  108 us
    ppermute x15, waiting for transfers between devices, outer(): lax.ppermute(value, AXES, self._pairs(lambda x, g, t: (x ^ dx, g ^ dg, t)))  71.9 us
    ppermute x35, starting transfers between devices, cube(): lax.ppermute(value, AXES, self._pairs(lambda x, g, t: (x, g, t ^ bits)))  50.6 us
    ppermute x15, starting transfers between devices, outer(): lax.ppermute(value, AXES, self._pairs(lambda x, g, t: (x ^ dx, g ^ dg, t)))  27.2 us
    unnamed x130, local copies, waits for them, and re-layouts  24.8 us
    all_to_all x3, starting transfers between devices, swap(): lax.all_to_all(value, AXES, split_axis=0, concat_axis=0, tiled=True, axis...  14.7 us
  transfers between devices with their start and end apart: 56, of which 26 were waited for; matrix products, arithmetic and copies ran while one was open for 0% of the time, Pallas kernels for 20%

profile of v3, /device:TPU:0, one launch (start us, length us, event | category | flops | bytes accessed | tf_op | source)
XLA Modules:
  0.0 446.4 jit_solution(17911628747039509500)
XLA Ops:
  16.3 5.3 %all-to-all-start = ((bf16[8,48,384]{2,1,0:T(8,128)(2,1)}), bf16[8,48,384]{2,1,0:T(8,128)(2,1)S(1)}, u32[]{:S(2)}, u32[]{:S(2)}) async-start(bf16[8,48,384]{2,1,0:T(8,128)(2,1)} %get-tuple-element.212), calls=%async_computation | async-start | bytes 589824 | tf_op jit(solution)/shard_map/all_to_all | solution.py:126
  30.1 5.9 %all-to-all-start.1 = ((bf16[8,48,1536]{2,1,0:T(8,128)(2,1)}), bf16[8,48,1536]{2,1,0:T(8,128)(2,1)}, u32[]{:S(2)}, u32[]{:S(2)}) async-start(bf16[8,48,1536]{2,1,0:T(8,128)(2,1)} %shard_map.180), calls=%async_computation.1 | async-start | bytes 2359296 | tf_op jit(solution)/shard_map/all_to_all | solution.py:126
  36.0 4.3 collective-permute-done.2.refs_3_
  40.3 7.2 %collective-permute-done.1.refs_2_ = bf16[128,1664]{1,0:T(8,128)(2,1)S(1)} collective-permute-done((bf16[128,1664]{1,0:T(8,128)(2,1)S(1)}, bf16[128,1664]{1,0:T(8,128)(2,1)S(1)}, u32[]{:S(2)}, u32[]{:S(2)}) %collective-permute-start.1) | collective-permute-done | bytes 426016 | tf_op jit(solution)/shard_map/ppermute | solution.py:107
  55.1 18.4 %collective-permute-done.4.refs_3_ = bf16[384,384]{1,0:T(8,128)(2,1)S(1)} collective-permute-done((bf16[384,384]{1,0:T(8,128)(2,1)S(1)}, bf16[384,384]{1,0:T(8,128)(2,1)S(1)}, u32[]{:S(2)}, u32[]{:S(2)}) %collective-permute-start.4) | collective-permute-done | bytes 294944 | tf_op jit(solution)/shard_map/ppermute | solution.py:110
  75.0 8.5 %collective-permute-done.6.refs_5_ = bf16[384,384]{1,0:T(8,128)(2,1)S(1)} collective-permute-done((bf16[384,384]{1,0:T(8,128)(2,1)S(1)}, bf16[384,384]{1,0:T(8,128)(2,1)S(1)}, u32[]{:S(2)}, u32[]{:S(2)}) %collective-permute-start.6) | collective-permute-done | bytes 294944 | tf_op jit(solution)/shard_map/ppermute | solution.py:110
  88.3 6.0 %shard_map.181 = (bf16[1024,1536]{1,0:T(8,128)(2,1)}, bf16[2,3,512,128]{3,2,1,0:T(8,128)(2,1)S(1)}, bf16[2,512,128]{2,1,0:T(8,128)(2,1)S(1)}, f32[8,1536]{1,0:T(8,128)}, bf16[1536,384]{1,0:T(8,128)(2,1)}) custom-call(s32[2,1]{1,0:T(2,128)S(1)} %copy.44.lengths, bf16[512,1664]{1,0:T(8,128)(2,1)S(1)} %shard_map.179.refs_0_.refs_2_, ...), custom_call_target="tpu_custom_call" | custom-call | flops 1000 | bytes 1000 | tf_op jit(solution)/shard_map/pallas_call | solution.py:62
  95.2 6.0 %collective-permute-start.7 = (bf16[2,512,128]{2,1,0:T(8,128)(2,1)S(1)}, bf16[2,512,128]{2,1,0:T(8,128)(2,1)S(1)}, u32[]{:S(2)}, u32[]{:S(2)}) collective-permute-start(bf16[2,512,128]{2,1,0:T(8,128)(2,1)S(1)} %get-tuple-element.232.refs_1_), channel_id=1, source_target_pairs={{0,8},{1,9},{2,10},{3,11},{4,12},{5,13},{6,14},{7,15},{16,24},{17,... | collective-permute-start | bytes 786440 | tf_op jit(solution)/shard_map/ppermute | solution.py:116
  108.8 14.7 %collective-permute-start.10 = (bf16[128,1536]{1,0:T(8,128)(2,1)S(1)}, bf16[128,1536]{1,0:T(8,128)(2,1)S(1)}, u32[]{:S(2)}, u32[]{:S(2)}) collective-permute-start(bf16[128,1536]{1,0:T(8,128)(2,1)S(1)} %bitcast.27), channel_id=1, source_target_pairs={{0,4},{1,5},{2,6},{3,7},{4,0},{5,1},{6,2},{7,3},{8,12},{9,13},{10,... | collective-permute-start | bytes 1179656 | tf_op jit(solution)/shard_map/ppermute | solution.py:107
  125.4 6.5 %collective-permute-done.10.refs_1_ = bf16[128,1536]{1,0:T(8,128)(2,1)S(1)} collective-permute-done((bf16[128,1536]{1,0:T(8,128)(2,1)S(1)}, bf16[128,1536]{1,0:T(8,128)(2,1)S(1)}, u32[]{:S(2)}, u32[]{:S(2)}) %collective-permute-start.10) | collective-permute-done | bytes 393248 | tf_op jit(solution)/shard_map/ppermute | solution.py:107
  139.6 8.2 %collective-permute-start.19 = (bf16[384,1024]{1,0:T(8,128)(2,1)S(1)}, bf16[384,1024]{1,0:T(8,128)(2,1)S(1)}, u32[]{:S(2)}, u32[]{:S(2)}) collective-permute-start(bf16[384,1024]{1,0:T(8,128)(2,1)S(1)} %copy-done.23), channel_id=1, source_target_pairs={{0,8},{1,9},{2,10},{3,11},{4,12},{5,13},{6,14},{7,15},{8,0},{9,1},... | collective-permute-start | bytes 2359304 | tf_op jit(solution)/shard_map/ppermute | solution.py:110
  147.8 7.3 %shard_map.184 = (bf16[512,384]{1,0:T(8,128)(2,1)S(1)}, f32[2,3,64,512]{3,2,1,0:T(8,128)}, f32[2,3,512]{2,1,0:T(4,128)}) custom-call(s32[2,1]{1,0:T(2,128)S(1)} %copy.44.lengths, bf16[2,3,512,128]{3,2,1,0:T(8,128)(2,1)S(1)} %copy-done.5, bf16[2,512,128]{2,1,0:T(8,128)(2,1)S(1)} %copy-done.13, bf16[2,512,128]{2,1,0:T(8,128)(2,1)S(1)} %copy-done.15), custom_call_target="tpu_custom_call" | custom-call | flops 1000 | bytes 1000 | tf_op jit(solution)/shard_map/pallas_call | solution.py:62
  159.7 23.9 %collective-permute-done.15.refs_3_ = bf16[512,384]{1,0:T(8,128)(2,1)S(1)} collective-permute-done((bf16[512,384]{1,0:T(8,128)(2,1)S(1)}, bf16[512,384]{1,0:T(8,128)(2,1)S(1)}, u32[]{:S(2)}, u32[]{:S(2)}) %collective-permute-start.15) | collective-permute-done | bytes 393248 | tf_op jit(solution)/shard_map/ppermute | solution.py:107
  183.6 6.4 %collective-permute-done.13.refs_1_ = bf16[512,384]{1,0:T(8,128)(2,1)S(1)} collective-permute-done((bf16[512,384]{1,0:T(8,128)(2,1)S(1)}, bf16[512,384]{1,0:T(8,128)(2,1)S(1)}, u32[]{:S(2)}, u32[]{:S(2)}) %collective-permute-start.13) | collective-permute-done | bytes 393248 | tf_op jit(solution)/shard_map/ppermute | solution.py:107
  192.1 4.5 %shard_map.187 = (f32[1024,512]{1,0:T(8,128)S(1)}, bf16[1536,512]{1,0:T(8,128)(2,1)S(1)}) custom-call(s32[2,1]{1,0:T(2,128)S(1)} %copy.44.lengths, bf16[512,1536]{1,0:T(8,128)(2,1)S(1)} %shard_map.185.refs_0_, bf16[512,1536]{1,0:T(8,128)(2,1)S(1)} %collective-permute-done.16.refs_1_, bf16[384,512]{1,0:T(8,128)(2,1)} %copy-done.48, ...), custom_call_target="tpu_custom_call" | custom-call | flops 20000000000 | bytes 1000 | tf_op jit(solution)/shard_map/pallas_call | solution.py:62
  196.6 10.5 %shard_map.188 = (bf16[512,1664]{1,0:T(8,128)(2,1)S(1)}, bf16[512,1664]{1,0:T(8,128)(2,1)S(1)}, f32[128,1536]{1,0:T(8,128)}, f32[128,128]{1,0:T(8,128)}) custom-call(s32[2,1]{1,0:T(2,128)S(1)} %copy.44.lengths, bf16[2048,384]{1,0:T(8,128)(2,1)S(1)} %shard_map.186.refs_0_, bf16[2048,384]{1,0:T(8,128)(2,1)S(1)} %collective-permute-done.21.refs_1_, ...), custom_call_target="tpu_custom_call" | custom-call | flops 1000 | bytes 1000 | tf_op jit(solution)/shard_map/pallas_call | solution.py:62
  209.8 6.5 %shard_map.189 = (bf16[512,512]{1,0:T(8,128)(2,1)S(1)}, bf16[512,1024]{1,0:T(8,128)(2,1)S(1)}, bf16[512,1664]{1,0:T(8,128)(2,1)S(1)}, bf16[1536,1024]{1,0:T(8,128)(2,1)S(1)}) custom-call(s32[2,1]{1,0:T(2,128)S(1)} %copy.44.lengths, bf16[512,1664]{1,0:T(8,128)(2,1)S(1)} %get-tuple-element.298.refs_0_.refs_2_.refs_3_.refs_4_, ...), custom_call_target="tpu_custom_call" | custom-call | flops 1000 | bytes 1000 | tf_op jit(solution)/shard_map/pallas_call | solution.py:62
  216.4 16.0 %shard_map.190 = (bf16[512,512]{1,0:T(8,128)(2,1)S(1)}, bf16[512,1024]{1,0:T(8,128)(2,1)S(1)}, bf16[512,1664]{1,0:T(8,128)(2,1)S(1)}) custom-call(s32[2,1]{1,0:T(2,128)S(1)} %copy.44.lengths, bf16[512,1664]{1,0:T(8,128)(2,1)S(1)} %get-tuple-element.297.refs_0_.refs_1_.refs_2_.refs_3_, f32[1024,512]{1,0:T(8,128)S(1)} %get-tuple-element.267.refs_1_, ...), custom_call_target="tpu_custom_call" | custom-call | flops 1000 | bytes 1000 | tf_op jit(solution)/shard_map/pallas_call | solution.py:62
  237.0 9.1 %collective-permute-done.23.refs_1_ = bf16[128,1664]{1,0:T(8,128)(2,1)S(1)} collective-permute-done((bf16[128,1664]{1,0:T(8,128)(2,1)S(1)}, bf16[128,1664]{1,0:T(8,128)(2,1)S(1)}, u32[]{:S(2)}, u32[]{:S(2)}) %collective-permute-start.23) | collective-permute-done | bytes 426016 | tf_op jit(solution)/shard_map/ppermute | solution.py:107
  246.1 9.8 %collective-permute-done.25.refs_3_ = bf16[128,1664]{1,0:T(8,128)(2,1)S(1)} collective-permute-done((bf16[128,1664]{1,0:T(8,128)(2,1)S(1)}, bf16[128,1664]{1,0:T(8,128)(2,1)S(1)}, u32[]{:S(2)}, u32[]{:S(2)}) %collective-permute-start.25) | collective-permute-done | bytes 426016 | tf_op jit(solution)/shard_map/ppermute | solution.py:107
  260.7 7.0 %shard_map.194 = (bf16[768,1024]{1,0:T(8,128)(2,1)S(1)}, bf16[768,512]{1,0:T(8,128)(2,1)S(1)}, bf16[768,1024]{1,0:T(8,128)(2,1)S(1)}, bf16[768,512]{1,0:T(8,128)(2,1)S(1)}) custom-call(s32[2,1]{1,0:T(2,128)S(1)} %copy.44.lengths, bf16[512,1536]{1,0:T(8,128)(2,1)S(1)} %shard_map.185.refs_0_, bf16[512,1536]{1,0:T(8,128)(2,1)S(1)} %collective-permute-done.16.refs_1_, ...), custom_call_target="tpu_custom_call" | custom-call | flops 20000000000 | bytes 1000 | tf_op jit(solution)/shard_map/pallas_call | solution.py:62
  270.9 7.8 %collective-permute-done.27.refs_2_ = bf16[128,1664]{1,0:T(8,128)(2,1)S(1)} collective-permute-done((bf16[128,1664]{1,0:T(8,128)(2,1)S(1)}, bf16[128,1664]{1,0:T(8,128)(2,1)S(1)}, u32[]{:S(2)}, u32[]{:S(2)}) %collective-permute-start.27) | collective-permute-done | bytes 426016 | tf_op jit(solution)/shard_map/ppermute | solution.py:107
  288.4 8.6 %shard_map.197 = (bf16[8,128,192]{2,1,0:T(8,128)(2,1)S(1)}, f32[2,512,128]{2,1,0:T(8,128)S(1)}, bf16[2,512,128]{2,1,0:T(8,128)(2,1)S(1)}) custom-call(s32[2,1]{1,0:T(2,128)S(1)} %copy.44.lengths, bf16[2,3,512,128]{3,2,1,0:T(8,128)(2,1)S(1)} %copy-done.5, bf16[2,512,128]{2,1,0:T(8,128)(2,1)S(1)} %copy-done.13, bf16[2,512,128]{2,1,0:T(8,128)(2,1)S(1)} %copy-done.15, ...), custom_call_target="tpu_custom_call" | custom-call | flops 1000 | bytes 1000 | tf_op jit(solution)/shard_map/pallas_call | solution.py:62
  305.2 4.7 %shard_map.199.refs_2_ = bf16[1536,256]{1,0:T(8,128)(2,1)} custom-call(s32[2,1]{1,0:T(2,128)S(1)} %copy.44.lengths, bf16[512,1664]{1,0:T(8,128)(2,1)S(1)} %shard_map.195.refs_1_.refs_0_, bf16[512,1664]{1,0:T(8,128)(2,1)S(1)} %collective-permute-done.29.refs_2_.refs_1_, bf16[512,384]{1,0:T(8,128)(2,1)S(1)} %get-tuple-element.249.refs_0_.refs_2_, ...), custom_call_target="tpu_custom_call" | custom-call | flops 20000000000 | bytes 1000 | tf_op jit(solution)/shard_map/pallas_call | solution.py:62
  310.7 5.8 %collective-permute-done.32.refs_3_ = bf16[2,512,128]{2,1,0:T(8,128)(2,1)S(1)} collective-permute-done((bf16[2,512,128]{2,1,0:T(8,128)(2,1)S(1)}, bf16[2,512,128]{2,1,0:T(8,128)(2,1)S(1)}, u32[]{:S(2)}, u32[]{:S(2)}) %collective-permute-start.32) | collective-permute-done | bytes 262176 | tf_op jit(solution)/shard_map/ppermute | solution.py:116
  320.1 5.1 %collective-permute-done.35.refs_3_ = bf16[128,1536]{1,0:T(8,128)(2,1)S(1)} collective-permute-done((bf16[128,1536]{1,0:T(8,128)(2,1)S(1)}, bf16[128,1536]{1,0:T(8,128)(2,1)S(1)}, u32[]{:S(2)}, u32[]{:S(2)}) %collective-permute-start.35) | collective-permute-done | bytes 393248 | tf_op jit(solution)/shard_map/ppermute | solution.py:107
  329.2 4.1 collective-permute-start.38
  338.8 11.2 %collective-permute-done.38.refs_3_ = bf16[384,512]{1,0:T(8,128)(2,1)S(1)} collective-permute-done((bf16[384,512]{1,0:T(8,128)(2,1)S(1)}, bf16[384,512]{1,0:T(8,128)(2,1)S(1)}, u32[]{:S(2)}, u32[]{:S(2)}) %collective-permute-start.38) | collective-permute-done | bytes 393248 | tf_op jit(solution)/shard_map/ppermute | solution.py:110
  355.8 4.9 %collective-permute-done.43.refs_1_ = bf16[768,640]{1,0:T(8,128)(2,1)S(1)} collective-permute-done((bf16[768,640]{1,0:T(8,128)(2,1)S(1)}, bf16[768,640]{1,0:T(8,128)(2,1)S(1)}, u32[]{:S(2)}, u32[]{:S(2)}) %collective-permute-start.43) | collective-permute-done | bytes 983072 | tf_op jit(solution)/shard_map/ppermute | solution.py:110
  362.4 14.0 %collective-permute-done.40.refs_1_ = bf16[128,1536]{1,0:T(8,128)(2,1)S(1)} collective-permute-done((bf16[128,1536]{1,0:T(8,128)(2,1)S(1)}, bf16[128,1536]{1,0:T(8,128)(2,1)S(1)}, u32[]{:S(2)}, u32[]{:S(2)}) %collective-permute-start.40) | collective-permute-done | bytes 393248 | tf_op jit(solution)/shard_map/ppermute | solution.py:107
  376.4 12.1 %collective-permute-done.42.refs_3_ = bf16[128,1536]{1,0:T(8,128)(2,1)S(1)} collective-permute-done((bf16[128,1536]{1,0:T(8,128)(2,1)S(1)}, bf16[128,1536]{1,0:T(8,128)(2,1)S(1)}, u32[]{:S(2)}, u32[]{:S(2)}) %collective-permute-start.42) | collective-permute-done | bytes 393248 | tf_op jit(solution)/shard_map/ppermute | solution.py:107
  396.3 23.7 %collective-permute-done.44.refs_1_ = bf16[384,640]{1,0:T(8,128)(2,1)S(1)} collective-permute-done((bf16[384,640]{1,0:T(8,128)(2,1)S(1)}, bf16[384,640]{1,0:T(8,128)(2,1)S(1)}, u32[]{:S(2)}, u32[]{:S(2)}) %collective-permute-start.44) | collective-permute-done | bytes 491552 | tf_op jit(solution)/shard_map/ppermute | solution.py:110
  (247 shorter events, 137.6 us)
Async XLA Ops:
  7.2 125.4 %all-gather.2.cloned.1.call-start = ((), (), s32[]{:S(2)}) async-start(), calls=%async_computation.3 | async-start | bytes 5271552 | tf_op jit(solution)/shard_map/all_gather | solution.py:787
  24.5 23.0 %collective-permute-start.1 = (bf16[128,1664]{1,0:T(8,128)(2,1)S(1)}, bf16[128,1664]{1,0:T(8,128)(2,1)S(1)}, u32[]{:S(2)}, u32[]{:S(2)}) collective-permute-start(bf16[128,1664]{1,0:T(8,128)(2,1)S(1)} %get-tuple-element.208.refs_0_), channel_id=1, source_target_pairs={{0,2},{1,3},{2,0},{3,1},{4,6},{5,7},{6,4},{7,5},{8,10},{9,11},{10,... | collective-permute-start | bytes 1277960 | tf_op jit(solution)/shard_map/ppermute | solution.py:107
  25.1 25.1 %collective-permute-start = (bf16[128,1664]{1,0:T(8,128)(2,1)S(1)}, bf16[128,1664]{1,0:T(8,128)(2,1)S(1)}, u32[]{:S(2)}, u32[]{:S(2)}) collective-permute-start(bf16[128,1664]{1,0:T(8,128)(2,1)S(1)} %get-tuple-element.208.refs_0_), channel_id=1, source_target_pairs={{0,4},{1,5},{2,6},{3,7},{4,0},{5,1},{6,2},{7,3},{8,12},{9,13},{10,... | collective-permute-start | bytes 1277960 | tf_op jit(solution)/shard_map/ppermute | solution.py:107
  30.1 54.2 %all-to-all-start.1 = ((bf16[8,48,1536]{2,1,0:T(8,128)(2,1)}), bf16[8,48,1536]{2,1,0:T(8,128)(2,1)}, u32[]{:S(2)}, u32[]{:S(2)}) async-start(bf16[8,48,1536]{2,1,0:T(8,128)(2,1)} %shard_map.180), calls=%async_computation.1 | async-start | bytes 2359296 | tf_op jit(solution)/shard_map/all_to_all | solution.py:126
  50.9 33.4 %collective-permute-start.3 = (bf16[512,1664]{1,0:T(8,128)(2,1)S(1)}, bf16[512,1664]{1,0:T(8,128)(2,1)S(1)}, u32[]{:S(2)}, u32[]{:S(2)}) collective-permute-start(bf16[512,1664]{1,0:T(8,128)(2,1)S(1)} %shard_map.179.refs_0_.refs_2_), channel_id=1, source_target_pairs={{0,1},{1,0},{2,3},{3,2},{4,5},{5,4},{6,7},{7,6},{8,9},{9,8},{10,11... | collective-permute-start | bytes 5111816 | tf_op jit(solution)/shard_map/ppermute | solution.py:107
  51.0 22.5 %collective-permute-start.4 = (bf16[384,384]{1,0:T(8,128)(2,1)S(1)}, bf16[384,384]{1,0:T(8,128)(2,1)S(1)}, u32[]{:S(2)}, u32[]{:S(2)}) collective-permute-start(bf16[384,384]{1,0:T(8,128)(2,1)S(1)} %bitcast.42), channel_id=1, source_target_pairs={{0,8},{1,9},{2,10},{3,11},{4,12},{5,13},{6,14},{7,15},{8,0},{9,1},... | collective-permute-start | bytes 884744 | tf_op jit(solution)/shard_map/ppermute | solution.py:110
  53.6 21.4 %collective-permute-start.5 = (bf16[384,384]{1,0:T(8,128)(2,1)S(1)}, bf16[384,384]{1,0:T(8,128)(2,1)S(1)}, u32[]{:S(2)}, u32[]{:S(2)}) collective-permute-start(bf16[384,384]{1,0:T(8,128)(2,1)S(1)} %bitcast.43), channel_id=1, source_target_pairs={{0,16},{1,17},{2,18},{3,19},{4,20},{5,21},{6,22},{7,23},{8,24},{9,... | collective-permute-start | bytes 884744 | tf_op jit(solution)/shard_map/ppermute | solution.py:110
  85.7 46.9 %collective-permute-start.9 = (bf16[384,1024]{1,0:T(8,128)(2,1)S(1)}, bf16[384,1024]{1,0:T(8,128)(2,1)}, u32[]{:S(2)}, u32[]{:S(2)}) collective-permute-start(bf16[384,1024]{1,0:T(8,128)(2,1)S(1)} %get-tuple-element.268.refs_2_), channel_id=1, source_target_pairs={{0,16},{1,17},{2,18},{3,19},{4,20},{5,21},{6,22},{7,23},{8,24},{9,... | collective-permute-start | bytes 2359304 | tf_op jit(solution)/shard_map/ppermute | solution.py:110
  101.9 21.6 %collective-permute-start.8 = (bf16[384,512]{1,0:T(8,128)(2,1)S(1)}, bf16[384,512]{1,0:T(8,128)(2,1)S(1)}, u32[]{:S(2)}, u32[]{:S(2)}) collective-permute-start(bf16[384,512]{1,0:T(8,128)(2,1)S(1)} %get-tuple-element.258.refs_2_), channel_id=1, source_target_pairs={{0,8},{1,9},{2,10},{3,11},{4,12},{5,13},{6,14},{7,15},{8,0},{9,1},... | collective-permute-start | bytes 1179656 | tf_op jit(solution)/shard_map/ppermute | solution.py:110
  101.9 22.0 %collective-permute-start.12 = (bf16[128,1536]{1,0:T(8,128)(2,1)S(1)}, bf16[128,1536]{1,0:T(8,128)(2,1)S(1)}, u32[]{:S(2)}, u32[]{:S(2)}) collective-permute-start(bf16[128,1536]{1,0:T(8,128)(2,1)S(1)} %bitcast.25), channel_id=1, source_target_pairs={{0,6},{1,7},{2,4},{3,5},{4,2},{5,3},{6,0},{7,1},{8,14},{9,15},{10,... | collective-permute-start | bytes 1179656 | tf_op jit(solution)/shard_map/ppermute | solution.py:107
  108.8 23.0 %collective-permute-start.10 = (bf16[128,1536]{1,0:T(8,128)(2,1)S(1)}, bf16[128,1536]{1,0:T(8,128)(2,1)S(1)}, u32[]{:S(2)}, u32[]{:S(2)}) collective-permute-start(bf16[128,1536]{1,0:T(8,128)(2,1)S(1)} %bitcast.27), channel_id=1, source_target_pairs={{0,4},{1,5},{2,6},{3,7},{4,0},{5,1},{6,2},{7,3},{8,12},{9,13},{10,... | collective-permute-start | bytes 1179656 | tf_op jit(solution)/shard_map/ppermute | solution.py:107
  137.3 52.7 %collective-permute-start.16 = (bf16[512,1536]{1,0:T(8,128)(2,1)S(1)}, bf16[512,1536]{1,0:T(8,128)(2,1)S(1)}, u32[]{:S(2)}, u32[]{:S(2)}) collective-permute-start(bf16[512,1536]{1,0:T(8,128)(2,1)S(1)} %shard_map.185.refs_0_), channel_id=1, source_target_pairs={{0,1},{1,0},{2,3},{3,2},{4,5},{5,4},{6,7},{7,6},{8,9},{9,8},{10,11... | collective-permute-start | bytes 4718600 | tf_op jit(solution)/shard_map/ppermute | solution.py:107
  137.6 21.1 %collective-permute-start.17 = (bf16[384,512]{1,0:T(8,128)(2,1)S(1)}, bf16[384,512]{1,0:T(8,128)(2,1)S(1)}, u32[]{:S(2)}, u32[]{:S(2)}) collective-permute-start(bf16[384,512]{1,0:T(8,128)(2,1)S(1)} %copy-done.49), channel_id=1, source_target_pairs={{0,16},{1,17},{2,18},{3,19},{4,20},{5,21},{6,22},{7,23},{8,24},{9,... | collective-permute-start | bytes 1179656 | tf_op jit(solution)/shard_map/ppermute | solution.py:110
  139.2 19.9 %collective-permute-start.18 = (bf16[384,512]{1,0:T(8,128)(2,1)S(1)}, bf16[384,512]{1,0:T(8,128)(2,1)S(1)}, u32[]{:S(2)}, u32[]{:S(2)}) collective-permute-start(bf16[384,512]{1,0:T(8,128)(2,1)S(1)} %copy-done.59), channel_id=1, source_target_pairs={{0,16},{1,17},{2,18},{3,19},{4,20},{5,21},{6,22},{7,23},{8,24},{9,... | collective-permute-start | bytes 1179656 | tf_op jit(solution)/shard_map/ppermute | solution.py:110
  139.6 50.4 %collective-permute-start.19 = (bf16[384,1024]{1,0:T(8,128)(2,1)S(1)}, bf16[384,1024]{1,0:T(8,128)(2,1)S(1)}, u32[]{:S(2)}, u32[]{:S(2)}) collective-permute-start(bf16[384,1024]{1,0:T(8,128)(2,1)S(1)} %copy-done.23), channel_id=1, source_target_pairs={{0,8},{1,9},{2,10},{3,11},{4,12},{5,13},{6,14},{7,15},{8,0},{9,1},... | collective-permute-start | bytes 2359304 | tf_op jit(solution)/shard_map/ppermute | solution.py:110
  155.1 28.5 %collective-permute-start.15 = (bf16[512,384]{1,0:T(8,128)(2,1)S(1)}, bf16[512,384]{1,0:T(8,128)(2,1)S(1)}, u32[]{:S(2)}, u32[]{:S(2)}) collective-permute-start(bf16[512,384]{1,0:T(8,128)(2,1)S(1)} %get-tuple-element.249.refs_0_.refs_2_), channel_id=1, source_target_pairs={{0,6},{1,7},{2,4},{3,5},{4,2},{5,3},{6,0},{7,1},{8,14},{9,15},{10,... | collective-permute-start | bytes 1179656 | tf_op jit(solution)/shard_map/ppermute | solution.py:107
  158.7 24.9 %collective-permute-start.14 = (bf16[512,384]{1,0:T(8,128)(2,1)S(1)}, bf16[512,384]{1,0:T(8,128)(2,1)S(1)}, u32[]{:S(2)}, u32[]{:S(2)}) collective-permute-start(bf16[512,384]{1,0:T(8,128)(2,1)S(1)} %get-tuple-element.249.refs_0_.refs_2_), channel_id=1, source_target_pairs={{0,2},{1,3},{2,0},{3,1},{4,6},{5,7},{6,4},{7,5},{8,10},{9,11},{10,... | collective-permute-start | bytes 1179656 | tf_op jit(solution)/shard_map/ppermute | solution.py:107
  159.1 30.9 %collective-permute-start.13 = (bf16[512,384]{1,0:T(8,128)(2,1)S(1)}, bf16[512,384]{1,0:T(8,128)(2,1)S(1)}, u32[]{:S(2)}, u32[]{:S(2)}) collective-permute-start(bf16[512,384]{1,0:T(8,128)(2,1)S(1)} %get-tuple-element.249.refs_0_.refs_2_), channel_id=1, source_target_pairs={{0,4},{1,5},{2,6},{3,7},{4,0},{5,1},{6,2},{7,3},{8,12},{9,13},{10,... | collective-permute-start | bytes 1179656 | tf_op jit(solution)/shard_map/ppermute | solution.py:107
  235.2 20.7 %collective-permute-start.25 = (bf16[128,1664]{1,0:T(8,128)(2,1)S(1)}, bf16[128,1664]{1,0:T(8,128)(2,1)S(1)}, u32[]{:S(2)}, u32[]{:S(2)}) collective-permute-start(bf16[128,1664]{1,0:T(8,128)(2,1)S(1)} %get-tuple-element.285), channel_id=1, source_target_pairs={{0,6},{1,7},{2,4},{3,5},{4,2},{5,3},{6,0},{7,1},{8,14},{9,15},{10,... | collective-permute-start | bytes 1277960 | tf_op jit(solution)/shard_map/ppermute | solution.py:107
  259.0 19.7 %collective-permute-start.27 = (bf16[128,1664]{1,0:T(8,128)(2,1)S(1)}, bf16[128,1664]{1,0:T(8,128)(2,1)S(1)}, u32[]{:S(2)}, u32[]{:S(2)}) collective-permute-start(bf16[128,1664]{1,0:T(8,128)(2,1)S(1)} %get-tuple-element.308.refs_0_), channel_id=1, source_target_pairs={{0,2},{1,3},{2,0},{3,1},{4,6},{5,7},{6,4},{7,5},{8,10},{9,11},{10,... | collective-permute-start | bytes 1277960 | tf_op jit(solution)/shard_map/ppermute | solution.py:107
  280.0 20.4 %collective-permute-start.31 = (bf16[768,512]{1,0:T(8,128)(2,1)S(1)}, bf16[768,512]{1,0:T(8,128)(2,1)S(1)}, u32[]{:S(2)}, u32[]{:S(2)}) collective-permute-start(bf16[768,512]{1,0:T(8,128)(2,1)S(1)} %get-tuple-element.325), channel_id=1, source_target_pairs={{0,16},{1,17},{2,18},{3,19},{4,20},{5,21},{6,22},{7,23},{8,24},{9,... | collective-permute-start | bytes 2359304 | tf_op jit(solution)/shard_map/ppermute | solution.py:110
  280.4 57.4 %collective-permute-start.37 = (bf16[768,1024]{1,0:T(8,128)(2,1)S(1)}, bf16[768,1024]{1,0:T(8,128)(2,1)S(1)}, u32[]{:S(2)}, u32[]{:S(2)}) collective-permute-start(bf16[768,1024]{1,0:T(8,128)(2,1)S(1)} %get-tuple-element.352), channel_id=1, source_target_pairs={{0,16},{1,17},{2,18},{3,19},{4,20},{5,21},{6,22},{7,23},{8,24},{9,... | collective-permute-start | bytes 4718600 | tf_op jit(solution)/shard_map/ppermute | solution.py:110
  303.7 21.5 %collective-permute-start.35 = (bf16[128,1536]{1,0:T(8,128)(2,1)S(1)}, bf16[128,1536]{1,0:T(8,128)(2,1)S(1)}, u32[]{:S(2)}, u32[]{:S(2)}) collective-permute-start(bf16[128,1536]{1,0:T(8,128)(2,1)S(1)} %get-tuple-element.333), channel_id=1, source_target_pairs={{0,6},{1,7},{2,4},{3,5},{4,2},{5,3},{6,0},{7,1},{8,14},{9,15},{10,... | collective-permute-start | bytes 1179656 | tf_op jit(solution)/shard_map/ppermute | solution.py:107
  329.1 20.9 %collective-permute-start.36 = (bf16[512,1536]{1,0:T(8,128)(2,1)S(1)}, bf16[512,1536]{1,0:T(8,128)(2,1)S(1)}, u32[]{:S(2)}, u32[]{:S(2)}) collective-permute-start(bf16[512,1536]{1,0:T(8,128)(2,1)S(1)} %get-tuple-element.350), channel_id=1, source_target_pairs={{0,1},{1,0},{2,3},{3,2},{4,5},{5,4},{6,7},{7,6},{8,9},{9,8},{10,11... | collective-permute-start | bytes 4718600 | tf_op jit(solution)/shard_map/ppermute | solution.py:107
  329.2 20.8 %collective-permute-start.38 = (bf16[384,512]{1,0:T(8,128)(2,1)S(1)}, bf16[384,512]{1,0:T(8,128)(2,1)S(1)}, u32[]{:S(2)}, u32[]{:S(2)}) collective-permute-start(bf16[384,512]{1,0:T(8,128)(2,1)S(1)} %get-tuple-element.357), channel_id=1, source_target_pairs={{0,8},{1,9},{2,10},{3,11},{4,12},{5,13},{6,14},{7,15},{8,0},{9,1},... | collective-permute-start | bytes 1179656 | tf_op jit(solution)/shard_map/ppermute | solution.py:110
  336.8 23.9 %collective-permute-start.43 = (bf16[768,640]{1,0:T(8,128)(2,1)S(1)}, bf16[768,640]{1,0:T(8,128)(2,1)S(1)}, u32[]{:S(2)}, u32[]{:S(2)}) collective-permute-start(bf16[768,640]{1,0:T(8,128)(2,1)S(1)} %get-tuple-element.370), channel_id=1, source_target_pairs={{0,16},{1,17},{2,18},{3,19},{4,20},{5,21},{6,22},{7,23},{8,24},{9,... | collective-permute-start | bytes 2949128 | tf_op jit(solution)/shard_map/ppermute | solution.py:110
  350.1 40.4 %collective-permute-start.39 = (bf16[384,1024]{1,0:T(8,128)(2,1)S(1)}, bf16[384,1024]{1,0:T(8,128)(2,1)S(1)}, u32[]{:S(2)}, u32[]{:S(2)}) collective-permute-start(bf16[384,1024]{1,0:T(8,128)(2,1)S(1)} %get-tuple-element.359), channel_id=1, source_target_pairs={{0,8},{1,9},{2,10},{3,11},{4,12},{5,13},{6,14},{7,15},{8,0},{9,1},... | collective-permute-start | bytes 2359304 | tf_op jit(solution)/shard_map/ppermute | solution.py:110
  351.0 25.4 %collective-permute-start.40 = (bf16[128,1536]{1,0:T(8,128)(2,1)S(1)}, bf16[128,1536]{1,0:T(8,128)(2,1)S(1)}, u32[]{:S(2)}, u32[]{:S(2)}) collective-permute-start(bf16[128,1536]{1,0:T(8,128)(2,1)S(1)} %get-tuple-element.363), channel_id=1, source_target_pairs={{0,4},{1,5},{2,6},{3,7},{4,0},{5,1},{6,2},{7,3},{8,12},{9,13},{10,... | collective-permute-start | bytes 1179656 | tf_op jit(solution)/shard_map/ppermute | solution.py:107
  354.3 22.1 %collective-permute-start.41 = (bf16[128,1536]{1,0:T(8,128)(2,1)S(1)}, bf16[128,1536]{1,0:T(8,128)(2,1)S(1)}, u32[]{:S(2)}, u32[]{:S(2)}) collective-permute-start(bf16[128,1536]{1,0:T(8,128)(2,1)S(1)} %get-tuple-element.364), channel_id=1, source_target_pairs={{0,2},{1,3},{2,0},{3,1},{4,6},{5,7},{6,4},{7,5},{8,10},{9,11},{10,... | collective-permute-start | bytes 1179656 | tf_op jit(solution)/shard_map/ppermute | solution.py:107
  355.2 33.3 %collective-permute-start.42 = (bf16[128,1536]{1,0:T(8,128)(2,1)S(1)}, bf16[128,1536]{1,0:T(8,128)(2,1)S(1)}, u32[]{:S(2)}, u32[]{:S(2)}) collective-permute-start(bf16[128,1536]{1,0:T(8,128)(2,1)S(1)} %get-tuple-element.365), channel_id=1, source_target_pairs={{0,6},{1,7},{2,4},{3,5},{4,2},{5,3},{6,0},{7,1},{8,14},{9,15},{10,... | collective-permute-start | bytes 1179656 | tf_op jit(solution)/shard_map/ppermute | solution.py:107
  392.2 45.0 %all-to-all-start.2 = ((bf16[8,48,1536]{2,1,0:T(8,128)(2,1)}), bf16[8,48,1536]{2,1,0:T(8,128)(2,1)S(1)}, u32[]{:S(2)}, u32[]{:S(2)}) async-start(bf16[8,48,1536]{2,1,0:T(8,128)(2,1)} %bitcast.16), calls=%async_computation.2 | async-start | bytes 2359296 | tf_op jit(solution)/shard_map/all_to_all | solution.py:126
  395.8 24.2 %collective-permute-start.44 = (bf16[384,640]{1,0:T(8,128)(2,1)S(1)}, bf16[384,640]{1,0:T(8,128)(2,1)S(1)}, u32[]{:S(2)}, u32[]{:S(2)}) collective-permute-start(bf16[384,640]{1,0:T(8,128)(2,1)S(1)} %get-tuple-element.381), channel_id=1, source_target_pairs={{0,8},{1,9},{2,10},{3,11},{4,12},{5,13},{6,14},{7,15},{8,0},{9,1},... | collective-permute-start | bytes 1474568 | tf_op jit(solution)/shard_map/ppermute | solution.py:110
  (88 other events, 826.6 us)
Sparse Core Ops, SparseCore 0:
  16.5 91.4 all-gather.1

commit v4 on v3

--- a/solution.py
+++ b/solution.py
@@ -220,8 +220,16 @@
     rows = jnp.concatenate(
         [rt, rt, gain_ref[...].astype(F32), jnp.zeros((EXTRA - 2 * E - 1, wr), F32)], axis=0
     )
-    wo_out[:, :QW] = wo_ref[...]
-    wo_out[:, QW:] = rows.T.astype(BF16)
+    wo_out[0, :, :QW] = wo_ref[...]
+    wo_out[0, :, QW:] = rows.T.astype(BF16)
+
+
+def order_kernel(ng, n_outer, scal, even_ref, odd_ref, out_ref):
+    for q, k in enumerate(ORDER):
+        source = even_ref if q < 4 else odd_ref
+        for j in range(n_outer):
+            group = (scal[0] ^ (j // ng)) * ng + (scal[1] ^ (j % ng))
+            out_ref[group * CUBE + (scal[2] ^ k)] = source[(q % 4) * n_outer + j]
 
 
 def prep_experts_kernel(scal, gu_ref, dn_ref, moe_out):
@@ -768,6 +776,10 @@
         own = blocks[0].shape
         return call(pack_kernel, [bf((4 * own[0], own[1]))], blocks)[0]
 
+    def pile(blocks):
+        own = blocks[0].shape
+        return call(pack_kernel, [bf((len(blocks) * own[0],) + own[1:])], blocks)[0]
+
     wq_parts, tok_wide = call(
         prep_kernel,
         [bf((CUBE, wr, SLAB)), bf((rows, WIDE))],
@@ -779,29 +791,32 @@
     wq_group = links.swap(wq_parts).reshape(CUBE * wr, SLAB)
     wo_part = call(
         prep_out_kernel,
-        [bf((wr, WIDE))],
+        [bf((1, wr, WIDE))],
         [out_in, router.T, moe_gain.reshape(1, wr)],
         room=3,
         busy=20,
     )[0]
-    wo = lax.all_gather(wo_part, AXES, axis=0, tiled=True)
     wq_group, gateup_in, down_in = fence(
         wq_group, gateup_weight, down_weight.transpose(0, 2, 1)
     )
     moe_parts = call(
         prep_experts_kernel, [bf((CUBE, wr, 3 * HALF))], [gateup_in, down_in], room=3
     )[0]
-    tok_wide, tok_near = fence(tok_wide, tok_near)
+    tok_wide, tok_near, wo_part = fence(tok_wide, tok_near, wo_part)
     tok_even = pack([tok_wide] + list(tok_near))
     tok_odd = links.core(tok_even)
     wq_far = [links.outer(wq_group, 0, dg) for dg in range(1, ng)]
+    wo_far = [links.outer(wo_part, 0, dg) for dg in range(1, ng)]
     wq_blocks = [wq_group] + wq_far
     for dx in range(1, nx):
         wq_blocks += [links.outer(block, dx, 0) for block in wq_blocks[:ng]]
     moe_group = links.swap(moe_parts).reshape(CUBE * wr, 3 * HALF)
-    tok_even, tok_odd, wq_blocks, moe_group, cot = fence(
-        tok_even, tok_odd, wq_blocks, moe_group, cot
-    )
+    tok_even, tok_odd, wq_blocks, moe_group, cot, wo_far = fence(
+        tok_even, tok_odd, wq_blocks, moe_group, cot, wo_far
+    )
+    wo_row = pile([wo_part] + list(wo_far))
+    wo_block = pile([wo_row] + [links.outer(wo_row, dx, 0) for dx in range(1, nx)])
+    wo_even = pile([wo_block] + links.near(wo_block))
     xg, q, kv, gain1, wq = call(
         functools.partial(qkv_kernel, ng, n_outer),
         [
@@ -824,9 +839,10 @@
     cot_near = links.near(cot)
     dn_far = [links.outer(dn_group, 0, dg) for dg in range(1, ng)]
     gu_side = [links.outer(gu_group, dx, 0) for dx in range(1, nx)]
-    kv, kvs, dn_group, dn_far, gu_group, gu_side, cot, cot_near, wo = fence(
-        kv, kvs, dn_group, dn_far, gu_group, gu_side, cot, cot_near, wo
-    )
+    kv, kvs, dn_group, dn_far, gu_group, gu_side, cot, cot_near, wo_even = fence(
+        kv, kvs, dn_group, dn_far, gu_group, gu_side, cot, cot_near, wo_even
+    )
+    wo_odd = links.core(wo_even)
     kvs = [kv] + list(kvs)
     cot_even = pack([cot] + list(cot_near))
     att, ot, lse = call(
@@ -849,6 +865,12 @@
     gu_blocks = [gu_group] + list(gu_far)
     for dx in range(1, nx):
         gu_blocks += [gu_side[dx - 1]] + [links.outer(block, dx, 0) for block in gu_far]
+    wo = call(
+        functools.partial(order_kernel, ng, n_outer),
+        [bf((n_outer * CUBE, wr, WIDE))],
+        [wo_even, wo_odd],
+        room=2,
+    )[0].reshape(D, WIDE)
     back, w_dn = call(
         functools.partial(cot_kernel, ng, n_outer),
         [f32(out_rows, HALF), bf((D, HALF))],

time: 451 us -> 445 us (0.987)
  waiting for transfers between devices: 199 us -> 236 us
  starting transfers between devices: 99.9 us -> 79.7 us
  between operations: 14.9 us -> 1.55 us
  local copies, waits for them, and re-layouts: 25.4 us -> 17.1 us
    ppermute x15 -> x17, waiting for transfers between devices: 71.9 us -> 89.6 us  [outer(): lax.ppermute(value, AXES, self._pairs(lambda x, g, t: (x ^ dx, g ^ dg, t)))]
    ppermute x2, waiting for transfers between devices: 7.86 us -> 21.8 us  [climb(): return lax.ppermute(value, AXES, self._pairs(move))]
    ppermute x35 -> x39, starting transfers between devices: 50.6 us -> 38.1 us  [cube(): lax.ppermute(value, AXES, self._pairs(lambda x, g, t: (x, g, t ^ bits)))]
    unnamed x130 -> x98, local copies, waits for them, and re-layouts: 24.8 us -> 16.5 us
    ppermute x35 -> x39, waiting for transfers between devices: 116 us -> 122 us  [cube(): lax.ppermute(value, AXES, self._pairs(lambda x, g, t: (x, g, t ^ bits)))]
    ppermute x15 -> x17, starting transfers between devices: 27.2 us -> 21.6 us  [outer(): lax.ppermute(value, AXES, self._pairs(lambda x, g, t: (x ^ dx, g ^ dg, t)))]
    pallas_call x34 -> x38, Pallas kernels: 108 us -> 110 us  [__call__(): pl.pallas_call(run, out_shape=list(outs), in_specs=[pl.BlockSpec(memory_s...]
  transfers between devices with their start and end apart: 56 -> 61, of which waited for: 26 -> 28; matrix products, arithmetic and copies ran while one was open for 0% -> 0% of each run, Pallas kernels for 20% -> 21%
where the time goes in v4:
time: 445 us
  waiting for transfers between devices  236 us (53%)
  Pallas kernels  110 us (25%)
  starting transfers between devices  79.7 us (18%)
  local copies, waits for them, and re-layouts  17.1 us (4%)
    ppermute x39, waiting for transfers between devices, cube(): lax.ppermute(value, AXES, self._pairs(lambda x, g, t: (x, g, t ^ bits)))  122 us
    pallas_call x38, Pallas kernels, __call__(): pl.pallas_call(run, out_shape=list(outs), in_specs=[pl.BlockSpec(memory_s...  110 us
    ppermute x17, waiting for transfers between devices, outer(): lax.ppermute(value, AXES, self._pairs(lambda x, g, t: (x ^ dx, g ^ dg, t)))  89.6 us
    ppermute x39, starting transfers between devices, cube(): lax.ppermute(value, AXES, self._pairs(lambda x, g, t: (x, g, t ^ bits)))  38.1 us
    ppermute x2, waiting for transfers between devices, climb(): return lax.ppermute(value, AXES, self._pairs(move))  21.8 us
    ppermute x17, starting transfers between devices, outer(): lax.ppermute(value, AXES, self._pairs(lambda x, g, t: (x ^ dx, g ^ dg, t)))  21.6 us
    unnamed x98, local copies, waits for them, and re-layouts  16.5 us
    all_to_all x3, starting transfers between devices, swap(): lax.all_to_all(value, AXES, split_axis=0, concat_axis=0, tiled=True, axis...  13.2 us
  transfers between devices with their start and end apart: 61, of which 28 were waited for; matrix products, arithmetic and copies ran while one was open for 0% of the time, Pallas kernels for 21%

profile of v4, /device:TPU:0, one launch (start us, length us, event | category | flops | bytes accessed | tf_op | source)
XLA Modules:
  0.0 444.6 jit_solution(16384778077648678840)
XLA Ops:
  6.3 5.3 %all-to-all-start = ((bf16[8,48,384]{2,1,0:T(8,128)(2,1)}), bf16[8,48,384]{2,1,0:T(8,128)(2,1)S(1)}, u32[]{:S(2)}, u32[]{:S(2)}) async-start(bf16[8,48,384]{2,1,0:T(8,128)(2,1)} %get-tuple-element.215), calls=%async_computation | async-start | bytes 589824 | tf_op jit(solution)/shard_map/all_to_all | solution.py:126
  27.5 10.1 %collective-permute-done.2.refs_3_ = bf16[128,1664]{1,0:T(8,128)(2,1)S(1)} collective-permute-done((bf16[128,1664]{1,0:T(8,128)(2,1)S(1)}, bf16[128,1664]{1,0:T(8,128)(2,1)S(1)}, u32[]{:S(2)}, u32[]{:S(2)}) %collective-permute-start.2) | collective-permute-done | bytes 426016 | tf_op jit(solution)/shard_map/ppermute | solution.py:107
  42.5 10.6 %collective-permute-done.4.refs_3_ = bf16[384,384]{1,0:T(8,128)(2,1)S(1)} collective-permute-done((bf16[384,384]{1,0:T(8,128)(2,1)S(1)}, bf16[384,384]{1,0:T(8,128)(2,1)S(1)}, u32[]{:S(2)}, u32[]{:S(2)}) %collective-permute-start.4) | collective-permute-done | bytes 294944 | tf_op jit(solution)/shard_map/ppermute | solution.py:110
  58.1 7.3 %collective-permute-done.7.refs_1_ = bf16[1,48,1664]{2,1,0:T(8,128)(2,1)S(1)} collective-permute-done((bf16[1,48,1664]{2,1,0:T(8,128)(2,1)S(1)}, bf16[1,48,1664]{2,1,0:T(8,128)(2,1)S(1)}, u32[]{:S(2)}, u32[]{:S(2)}) %collective-permute-start.7) | collective-permute-done | bytes 159776 | tf_op jit(solution)/shard_map/ppermute | solution.py:110
  70.5 6.5 %collective-permute-done.14.refs_1_ = bf16[2,48,1664]{2,1,0:T(8,128)(2,1)S(1)} collective-permute-done((bf16[2,48,1664]{2,1,0:T(8,128)(2,1)S(1)}, bf16[2,48,1664]{2,1,0:T(8,128)(2,1)S(1)}, u32[]{:S(2)}, u32[]{:S(2)}) %collective-permute-start.14) | collective-permute-done | bytes 319520 | tf_op jit(solution)/shard_map/ppermute | solution.py:110
  84.0 6.0 %shard_map.182 = (bf16[1024,1536]{1,0:T(8,128)(2,1)}, bf16[2,3,512,128]{3,2,1,0:T(8,128)(2,1)S(1)}, bf16[2,512,128]{2,1,0:T(8,128)(2,1)S(1)}, f32[8,1536]{1,0:T(8,128)}, bf16[1536,384]{1,0:T(8,128)(2,1)}) custom-call(s32[2,1]{1,0:T(2,128)S(1)} %copy.48.lengths, bf16[512,1664]{1,0:T(8,128)(2,1)S(1)} %shard_map.180.refs_0_.refs_2_, ...), custom_call_target="tpu_custom_call" | custom-call | flops 1000 | bytes 1000 | tf_op jit(solution)/shard_map/pallas_call | solution.py:62
  90.1 5.5 %collective-permute-start.8 = (bf16[2,512,128]{2,1,0:T(8,128)(2,1)S(1)}, bf16[2,512,128]{2,1,0:T(8,128)(2,1)S(1)}, u32[]{:S(2)}, u32[]{:S(2)}) collective-permute-start(bf16[2,512,128]{2,1,0:T(8,128)(2,1)S(1)} %get-tuple-element.236.refs_1_), channel_id=1, source_target_pairs={{0,8},{1,9},{2,10},{3,11},{4,12},{5,13},{6,14},{7,15},{16,24},{17,... | collective-permute-start | bytes 786440 | tf_op jit(solution)/shard_map/ppermute | solution.py:116
  95.6 17.0 %collective-permute-done.8.refs_2_ = bf16[2,512,128]{2,1,0:T(8,128)(2,1)S(1)} collective-permute-done((bf16[2,512,128]{2,1,0:T(8,128)(2,1)S(1)}, bf16[2,512,128]{2,1,0:T(8,128)(2,1)S(1)}, u32[]{:S(2)}, u32[]{:S(2)}) %collective-permute-start.8) | collective-permute-done | bytes 262176 | tf_op jit(solution)/shard_map/ppermute | solution.py:116
  120.2 7.2 %collective-permute-done.9.refs_3_ = bf16[384,512]{1,0:T(8,128)(2,1)S(1)} collective-permute-done((bf16[384,512]{1,0:T(8,128)(2,1)S(1)}, bf16[384,512]{1,0:T(8,128)(2,1)S(1)}, u32[]{:S(2)}, u32[]{:S(2)}) %collective-permute-start.9) | collective-permute-done | bytes 393248 | tf_op jit(solution)/shard_map/ppermute | solution.py:110
  127.4 7.8 %collective-permute-done.11.refs_1_ = bf16[128,1536]{1,0:T(8,128)(2,1)S(1)} collective-permute-done((bf16[128,1536]{1,0:T(8,128)(2,1)S(1)}, bf16[128,1536]{1,0:T(8,128)(2,1)S(1)}, u32[]{:S(2)}, u32[]{:S(2)}) %collective-permute-start.11) | collective-permute-done | bytes 393248 | tf_op jit(solution)/shard_map/ppermute | solution.py:107
  135.2 7.6 %collective-permute-done.13.refs_3_ = bf16[128,1536]{1,0:T(8,128)(2,1)S(1)} collective-permute-done((bf16[128,1536]{1,0:T(8,128)(2,1)S(1)}, bf16[128,1536]{1,0:T(8,128)(2,1)S(1)}, u32[]{:S(2)}, u32[]{:S(2)}) %collective-permute-start.13) | collective-permute-done | bytes 393248 | tf_op jit(solution)/shard_map/ppermute | solution.py:107
  143.7 7.3 %shard_map.187 = (bf16[512,384]{1,0:T(8,128)(2,1)S(1)}, f32[2,3,64,512]{3,2,1,0:T(8,128)}, f32[2,3,512]{2,1,0:T(4,128)}) custom-call(s32[2,1]{1,0:T(2,128)S(1)} %copy.48.lengths, bf16[2,3,512,128]{3,2,1,0:T(8,128)(2,1)S(1)} %get-tuple-element.226.refs_0_, bf16[2,512,128]{2,1,0:T(8,128)(2,1)S(1)} %get-tuple-element.236.refs_1_, ...), custom_call_target="tpu_custom_call" | custom-call | flops 1000 | bytes 1000 | tf_op jit(solution)/shard_map/pallas_call | solution.py:62
  154.6 21.5 %collective-permute-done.19.refs_1_ = bf16[512,384]{1,0:T(8,128)(2,1)S(1)} collective-permute-done((bf16[512,384]{1,0:T(8,128)(2,1)S(1)}, bf16[512,384]{1,0:T(8,128)(2,1)S(1)}, u32[]{:S(2)}, u32[]{:S(2)}) %collective-permute-start.19) | collective-permute-done | bytes 393248 | tf_op jit(solution)/shard_map/ppermute | solution.py:107
  176.8 6.9 %collective-permute-done.21.refs_3_ = bf16[512,384]{1,0:T(8,128)(2,1)S(1)} collective-permute-done((bf16[512,384]{1,0:T(8,128)(2,1)S(1)}, bf16[512,384]{1,0:T(8,128)(2,1)S(1)}, u32[]{:S(2)}, u32[]{:S(2)}) %collective-permute-start.21) | collective-permute-done | bytes 393248 | tf_op jit(solution)/shard_map/ppermute | solution.py:107
  188.1 8.0 %collective-permute-done.24.refs_5_ = bf16[384,512]{1,0:T(8,128)(2,1)S(1)} collective-permute-done((bf16[384,512]{1,0:T(8,128)(2,1)S(1)}, bf16[384,512]{1,0:T(8,128)(2,1)S(1)}, u32[]{:S(2)}, u32[]{:S(2)}) %collective-permute-start.24) | collective-permute-done | bytes 393248 | tf_op jit(solution)/shard_map/ppermute | solution.py:110
  197.7 4.5 %shard_map.191 = (f32[1024,512]{1,0:T(8,128)S(1)}, bf16[1536,512]{1,0:T(8,128)(2,1)S(1)}) custom-call(s32[2,1]{1,0:T(2,128)S(1)} %copy.48.lengths, bf16[512,1536]{1,0:T(8,128)(2,1)S(1)} %shard_map.189.refs_0_, bf16[512,1536]{1,0:T(8,128)(2,1)S(1)} %collective-permute-done.22.refs_1_, bf16[384,512]{1,0:T(8,128)(2,1)} %copy-done.35, ...), custom_call_target="tpu_custom_call" | custom-call | flops 20000000000 | bytes 1000 | tf_op jit(solution)/shard_map/pallas_call | solution.py:62
  203.2 10.5 %shard_map.192 = (bf16[512,1664]{1,0:T(8,128)(2,1)S(1)}, bf16[512,1664]{1,0:T(8,128)(2,1)S(1)}, f32[128,1536]{1,0:T(8,128)}, f32[128,128]{1,0:T(8,128)}) custom-call(s32[2,1]{1,0:T(2,128)S(1)} %copy.48.lengths, bf16[2048,384]{1,0:T(8,128)(2,1)S(1)} %shard_map.190.refs_0_, bf16[2048,384]{1,0:T(8,128)(2,1)S(1)} %collective-permute-done.27.refs_1_, ...), custom_call_target="tpu_custom_call" | custom-call | flops 1000 | bytes 1000 | tf_op jit(solution)/shard_map/pallas_call | solution.py:62
  217.2 6.6 %shard_map.193 = (bf16[512,512]{1,0:T(8,128)(2,1)S(1)}, bf16[512,1024]{1,0:T(8,128)(2,1)S(1)}, bf16[512,1664]{1,0:T(8,128)(2,1)S(1)}, bf16[1536,1024]{1,0:T(8,128)(2,1)S(1)}) custom-call(s32[2,1]{1,0:T(2,128)S(1)} %copy.48.lengths, bf16[512,1664]{1,0:T(8,128)(2,1)S(1)} %get-tuple-element.302.refs_0_.refs_2_.refs_3_.refs_4_, ...), custom_call_target="tpu_custom_call" | custom-call | flops 1000 | bytes 1000 | tf_op jit(solution)/shard_map/pallas_call | solution.py:62
  223.9 16.2 %shard_map.194 = (bf16[512,512]{1,0:T(8,128)(2,1)S(1)}, bf16[512,1024]{1,0:T(8,128)(2,1)S(1)}, bf16[512,1664]{1,0:T(8,128)(2,1)S(1)}) custom-call(s32[2,1]{1,0:T(2,128)S(1)} %copy.48.lengths, bf16[512,1664]{1,0:T(8,128)(2,1)S(1)} %get-tuple-element.301.refs_0_.refs_1_.refs_2_.refs_3_, f32[1024,512]{1,0:T(8,128)S(1)} %get-tuple-element.271.refs_1_, ...), custom_call_target="tpu_custom_call" | custom-call | flops 1000 | bytes 1000 | tf_op jit(solution)/shard_map/pallas_call | solution.py:62
  244.6 9.1 %collective-permute-done.29.refs_1_ = bf16[128,1664]{1,0:T(8,128)(2,1)S(1)} collective-permute-done((bf16[128,1664]{1,0:T(8,128)(2,1)S(1)}, bf16[128,1664]{1,0:T(8,128)(2,1)S(1)}, u32[]{:S(2)}, u32[]{:S(2)}) %collective-permute-start.29) | collective-permute-done | bytes 426016 | tf_op jit(solution)/shard_map/ppermute | solution.py:107
  253.7 8.8 %collective-permute-done.30.refs_2_ = bf16[128,1664]{1,0:T(8,128)(2,1)S(1)} collective-permute-done((bf16[128,1664]{1,0:T(8,128)(2,1)S(1)}, bf16[128,1664]{1,0:T(8,128)(2,1)S(1)}, u32[]{:S(2)}, u32[]{:S(2)}) %collective-permute-start.30) | collective-permute-done | bytes 426016 | tf_op jit(solution)/shard_map/ppermute | solution.py:107
  267.4 7.0 %shard_map.198 = (bf16[768,1024]{1,0:T(8,128)(2,1)S(1)}, bf16[768,512]{1,0:T(8,128)(2,1)S(1)}, bf16[768,1024]{1,0:T(8,128)(2,1)S(1)}, bf16[768,512]{1,0:T(8,128)(2,1)S(1)}) custom-call(s32[2,1]{1,0:T(2,128)S(1)} %copy.48.lengths, bf16[512,1536]{1,0:T(8,128)(2,1)S(1)} %shard_map.189.refs_0_, bf16[512,1536]{1,0:T(8,128)(2,1)S(1)} %collective-permute-done.22.refs_1_, ...), custom_call_target="tpu_custom_call" | custom-call | flops 20000000000 | bytes 1000 | tf_op jit(solution)/shard_map/pallas_call | solution.py:62
  277.4 8.2 %collective-permute-done.33.refs_2_ = bf16[128,1664]{1,0:T(8,128)(2,1)S(1)} collective-permute-done((bf16[128,1664]{1,0:T(8,128)(2,1)S(1)}, bf16[128,1664]{1,0:T(8,128)(2,1)S(1)}, u32[]{:S(2)}, u32[]{:S(2)}) %collective-permute-start.33) | collective-permute-done | bytes 426016 | tf_op jit(solution)/shard_map/ppermute | solution.py:107
  295.8 8.6 %shard_map.201 = (bf16[8,128,192]{2,1,0:T(8,128)(2,1)S(1)}, f32[2,512,128]{2,1,0:T(8,128)S(1)}, bf16[2,512,128]{2,1,0:T(8,128)(2,1)S(1)}) custom-call(s32[2,1]{1,0:T(2,128)S(1)} %copy.48.lengths, bf16[2,3,512,128]{3,2,1,0:T(8,128)(2,1)S(1)} %get-tuple-element.226.refs_0_, bf16[2,512,128]{2,1,0:T(8,128)(2,1)S(1)} %get-tuple-element.236.refs_1_, ...), custom_call_target="tpu_custom_call" | custom-call | flops 1000 | bytes 1000 | tf_op jit(solution)/shard_map/pallas_call | solution.py:62
  312.1 4.7 %shard_map.203.refs_2_ = bf16[1536,256]{1,0:T(8,128)(2,1)} custom-call(s32[2,1]{1,0:T(2,128)S(1)} %copy.48.lengths, bf16[512,1664]{1,0:T(8,128)(2,1)S(1)} %shard_map.199.refs_1_.refs_0_, bf16[512,1664]{1,0:T(8,128)(2,1)S(1)} %collective-permute-done.35.refs_2_.refs_1_, bf16[512,384]{1,0:T(8,128)(2,1)S(1)} %get-tuple-element.253.refs_0_.refs_2_, ...), custom_call_target="tpu_custom_call" | custom-call | flops 20000000000 | bytes 1000 | tf_op jit(solution)/shard_map/pallas_call | solution.py:62
  317.5 4.8 %collective-permute-done.38.refs_3_ = bf16[2,512,128]{2,1,0:T(8,128)(2,1)S(1)} collective-permute-done((bf16[2,512,128]{2,1,0:T(8,128)(2,1)S(1)}, bf16[2,512,128]{2,1,0:T(8,128)(2,1)S(1)}, u32[]{:S(2)}, u32[]{:S(2)}) %collective-permute-start.38) | collective-permute-done | bytes 262176 | tf_op jit(solution)/shard_map/ppermute | solution.py:116
  326.8 5.2 %collective-permute-done.41.refs_3_ = bf16[128,1536]{1,0:T(8,128)(2,1)S(1)} collective-permute-done((bf16[128,1536]{1,0:T(8,128)(2,1)S(1)}, bf16[128,1536]{1,0:T(8,128)(2,1)S(1)}, u32[]{:S(2)}, u32[]{:S(2)}) %collective-permute-start.41) | collective-permute-done | bytes 393248 | tf_op jit(solution)/shard_map/ppermute | solution.py:107
  343.4 11.8 %collective-permute-done.44.refs_3_ = bf16[384,512]{1,0:T(8,128)(2,1)S(1)} collective-permute-done((bf16[384,512]{1,0:T(8,128)(2,1)S(1)}, bf16[384,512]{1,0:T(8,128)(2,1)S(1)}, u32[]{:S(2)}, u32[]{:S(2)}) %collective-permute-start.44) | collective-permute-done | bytes 393248 | tf_op jit(solution)/shard_map/ppermute | solution.py:110
  360.4 5.3 %collective-permute-done.49.refs_1_ = bf16[768,640]{1,0:T(8,128)(2,1)S(1)} collective-permute-done((bf16[768,640]{1,0:T(8,128)(2,1)S(1)}, bf16[768,640]{1,0:T(8,128)(2,1)S(1)}, u32[]{:S(2)}, u32[]{:S(2)}) %collective-permute-start.49) | collective-permute-done | bytes 983072 | tf_op jit(solution)/shard_map/ppermute | solution.py:110
  366.5 15.0 %collective-permute-done.46.refs_1_ = bf16[128,1536]{1,0:T(8,128)(2,1)S(1)} collective-permute-done((bf16[128,1536]{1,0:T(8,128)(2,1)S(1)}, bf16[128,1536]{1,0:T(8,128)(2,1)S(1)}, u32[]{:S(2)}, u32[]{:S(2)}) %collective-permute-start.46) | collective-permute-done | bytes 393248 | tf_op jit(solution)/shard_map/ppermute | solution.py:107
  381.5 12.1 %collective-permute-done.48.refs_3_ = bf16[128,1536]{1,0:T(8,128)(2,1)S(1)} collective-permute-done((bf16[128,1536]{1,0:T(8,128)(2,1)S(1)}, bf16[128,1536]{1,0:T(8,128)(2,1)S(1)}, u32[]{:S(2)}, u32[]{:S(2)}) %collective-permute-start.48) | collective-permute-done | bytes 393248 | tf_op jit(solution)/shard_map/ppermute | solution.py:107
  401.3 23.7 %collective-permute-done.50.refs_1_ = bf16[384,640]{1,0:T(8,128)(2,1)S(1)} collective-permute-done((bf16[384,640]{1,0:T(8,128)(2,1)S(1)}, bf16[384,640]{1,0:T(8,128)(2,1)S(1)}, u32[]{:S(2)}, u32[]{:S(2)}) %collective-permute-start.50) | collective-permute-done | bytes 491552 | tf_op jit(solution)/shard_map/ppermute | solution.py:110
  (227 shorter events, 146.4 us)
Async XLA Ops:
  15.0 22.6 %collective-permute-start.2 = (bf16[128,1664]{1,0:T(8,128)(2,1)S(1)}, bf16[128,1664]{1,0:T(8,128)(2,1)S(1)}, u32[]{:S(2)}, u32[]{:S(2)}) collective-permute-start(bf16[128,1664]{1,0:T(8,128)(2,1)S(1)} %get-tuple-element.211.refs_0_), channel_id=1, source_target_pairs={{0,6},{1,7},{2,4},{3,5},{4,2},{5,3},{6,0},{7,1},{8,14},{9,15},{10,... | collective-permute-start | bytes 1277960 | tf_op jit(solution)/shard_map/ppermute | solution.py:107
  20.1 47.4 %all-to-all-start.1 = ((bf16[8,48,1536]{2,1,0:T(8,128)(2,1)}), bf16[8,48,1536]{2,1,0:T(8,128)(2,1)}, u32[]{:S(2)}, u32[]{:S(2)}) async-start(bf16[8,48,1536]{2,1,0:T(8,128)(2,1)} %shard_map.181), calls=%async_computation.1 | async-start | bytes 2359296 | tf_op jit(solution)/shard_map/all_to_all | solution.py:126
  38.3 29.2 %collective-permute-start.3 = (bf16[512,1664]{1,0:T(8,128)(2,1)S(1)}, bf16[512,1664]{1,0:T(8,128)(2,1)S(1)}, u32[]{:S(2)}, u32[]{:S(2)}) collective-permute-start(bf16[512,1664]{1,0:T(8,128)(2,1)S(1)} %shard_map.180.refs_0_.refs_2_), channel_id=1, source_target_pairs={{0,1},{1,0},{2,3},{3,2},{4,5},{5,4},{6,7},{7,6},{8,9},{9,8},{10,11... | collective-permute-start | bytes 5111816 | tf_op jit(solution)/shard_map/ppermute | solution.py:107
  41.1 25.0 %collective-permute-start.5 = (bf16[384,384]{1,0:T(8,128)(2,1)S(1)}, bf16[384,384]{1,0:T(8,128)(2,1)S(1)}, u32[]{:S(2)}, u32[]{:S(2)}) collective-permute-start(bf16[384,384]{1,0:T(8,128)(2,1)S(1)} %bitcast.45), channel_id=1, source_target_pairs={{0,16},{1,17},{2,18},{3,19},{4,20},{5,21},{6,22},{7,23},{8,24},{9,... | collective-permute-start | bytes 884744 | tf_op jit(solution)/shard_map/ppermute | solution.py:110
  77.6 38.4 %collective-permute-start.15 = (bf16[4,48,1664]{2,1,0:T(8,128)(2,1)S(1)}, bf16[4,48,1664]{2,1,0:T(8,128)(2,1)S(1)}, u32[]{:S(2)}, u32[]{:S(2)}) collective-permute-start(bf16[4,48,1664]{2,1,0:T(8,128)(2,1)S(1)} %shard_map.185.refs_0_), channel_id=1, source_target_pairs={{0,4},{1,5},{2,6},{3,7},{4,0},{5,1},{6,2},{7,3},{8,12},{9,13},{10,... | collective-permute-start | bytes 1916936 | tf_op jit(solution)/shard_map/ppermute | solution.py:107
  80.4 35.6 %collective-permute-start.16 = (bf16[4,48,1664]{2,1,0:T(8,128)(2,1)S(1)}, bf16[4,48,1664]{2,1,0:T(8,128)(2,1)S(1)}, u32[]{:S(2)}, u32[]{:S(2)}) collective-permute-start(bf16[4,48,1664]{2,1,0:T(8,128)(2,1)S(1)} %shard_map.185.refs_0_), channel_id=1, source_target_pairs={{0,2},{1,3},{2,0},{3,1},{4,6},{5,7},{6,4},{7,5},{8,10},{9,11},{10,... | collective-permute-start | bytes 1916936 | tf_op jit(solution)/shard_map/ppermute | solution.py:107
  82.0 35.8 %collective-permute-start.17 = (bf16[4,48,1664]{2,1,0:T(8,128)(2,1)S(1)}, bf16[4,48,1664]{2,1,0:T(8,128)(2,1)S(1)}, u32[]{:S(2)}, u32[]{:S(2)}) collective-permute-start(bf16[4,48,1664]{2,1,0:T(8,128)(2,1)S(1)} %shard_map.185.refs_0_), channel_id=1, source_target_pairs={{0,6},{1,7},{2,4},{3,5},{4,2},{5,3},{6,0},{7,1},{8,14},{9,15},{10,... | collective-permute-start | bytes 1916936 | tf_op jit(solution)/shard_map/ppermute | solution.py:107
  83.4 59.4 %collective-permute-start.10 = (bf16[384,1024]{1,0:T(8,128)(2,1)S(1)}, bf16[384,1024]{1,0:T(8,128)(2,1)S(1)}, u32[]{:S(2)}, u32[]{:S(2)}) collective-permute-start(bf16[384,1024]{1,0:T(8,128)(2,1)S(1)} %get-tuple-element.272.refs_2_), channel_id=1, source_target_pairs={{0,16},{1,17},{2,18},{3,19},{4,20},{5,21},{6,22},{7,23},{8,24},{9,... | collective-permute-start | bytes 2359304 | tf_op jit(solution)/shard_map/ppermute | solution.py:110
  90.1 22.5 %collective-permute-start.8 = (bf16[2,512,128]{2,1,0:T(8,128)(2,1)S(1)}, bf16[2,512,128]{2,1,0:T(8,128)(2,1)S(1)}, u32[]{:S(2)}, u32[]{:S(2)}) collective-permute-start(bf16[2,512,128]{2,1,0:T(8,128)(2,1)S(1)} %get-tuple-element.236.refs_1_), channel_id=1, source_target_pairs={{0,8},{1,9},{2,10},{3,11},{4,12},{5,13},{6,14},{7,15},{16,24},{17,... | collective-permute-start | bytes 786440 | tf_op jit(solution)/shard_map/ppermute | solution.py:116
  117.8 25.0 %collective-permute-start.13 = (bf16[128,1536]{1,0:T(8,128)(2,1)S(1)}, bf16[128,1536]{1,0:T(8,128)(2,1)S(1)}, u32[]{:S(2)}, u32[]{:S(2)}) collective-permute-start(bf16[128,1536]{1,0:T(8,128)(2,1)S(1)} %bitcast.29), channel_id=1, source_target_pairs={{0,6},{1,7},{2,4},{3,5},{4,2},{5,3},{6,0},{7,1},{8,14},{9,15},{10,... | collective-permute-start | bytes 1179656 | tf_op jit(solution)/shard_map/ppermute | solution.py:107
  143.7 52.4 %collective-permute-start.22 = (bf16[512,1536]{1,0:T(8,128)(2,1)S(1)}, bf16[512,1536]{1,0:T(8,128)(2,1)S(1)}, u32[]{:S(2)}, u32[]{:S(2)}) collective-permute-start(bf16[512,1536]{1,0:T(8,128)(2,1)S(1)} %shard_map.189.refs_0_), channel_id=1, source_target_pairs={{0,1},{1,0},{2,3},{3,2},{4,5},{5,4},{6,7},{7,6},{8,9},{9,8},{10,11... | collective-permute-start | bytes 4718600 | tf_op jit(solution)/shard_map/ppermute | solution.py:107
  151.1 25.1 %collective-permute-start.19 = (bf16[512,384]{1,0:T(8,128)(2,1)S(1)}, bf16[512,384]{1,0:T(8,128)(2,1)S(1)}, u32[]{:S(2)}, u32[]{:S(2)}) collective-permute-start(bf16[512,384]{1,0:T(8,128)(2,1)S(1)} %get-tuple-element.253.refs_0_.refs_2_), channel_id=1, source_target_pairs={{0,4},{1,5},{2,6},{3,7},{4,0},{5,1},{6,2},{7,3},{8,12},{9,13},{10,... | collective-permute-start | bytes 1179656 | tf_op jit(solution)/shard_map/ppermute | solution.py:107
  151.4 24.7 %collective-permute-start.20 = (bf16[512,384]{1,0:T(8,128)(2,1)S(1)}, bf16[512,384]{1,0:T(8,128)(2,1)S(1)}, u32[]{:S(2)}, u32[]{:S(2)}) collective-permute-start(bf16[512,384]{1,0:T(8,128)(2,1)S(1)} %get-tuple-element.253.refs_0_.refs_2_), channel_id=1, source_target_pairs={{0,2},{1,3},{2,0},{3,1},{4,6},{5,7},{6,4},{7,5},{8,10},{9,11},{10,... | collective-permute-start | bytes 1179656 | tf_op jit(solution)/shard_map/ppermute | solution.py:107
  151.5 32.1 %collective-permute-start.21 = (bf16[512,384]{1,0:T(8,128)(2,1)S(1)}, bf16[512,384]{1,0:T(8,128)(2,1)S(1)}, u32[]{:S(2)}, u32[]{:S(2)}) collective-permute-start(bf16[512,384]{1,0:T(8,128)(2,1)S(1)} %get-tuple-element.253.refs_0_.refs_2_), channel_id=1, source_target_pairs={{0,6},{1,7},{2,4},{3,5},{4,2},{5,3},{6,0},{7,1},{8,14},{9,15},{10,... | collective-permute-start | bytes 1179656 | tf_op jit(solution)/shard_map/ppermute | solution.py:107
  154.6 41.5 %collective-permute-start.25 = (bf16[384,1024]{1,0:T(8,128)(2,1)S(1)}, bf16[384,1024]{1,0:T(8,128)(2,1)S(1)}, u32[]{:S(2)}, u32[]{:S(2)}) collective-permute-start(bf16[384,1024]{1,0:T(8,128)(2,1)S(1)} %get-tuple-element.272.refs_2_), channel_id=1, source_target_pairs={{0,8},{1,9},{2,10},{3,11},{4,12},{5,13},{6,14},{7,15},{8,0},{9,1},... | collective-permute-start | bytes 2359304 | tf_op jit(solution)/shard_map/ppermute | solution.py:110
  176.1 26.1 %collective-permute-start.18 = (bf16[16,48,1664]{2,1,0:T(8,128)(2,1)S(1)}, bf16[16,48,1664]{2,1,0:T(8,128)(2,1)S(1)}, u32[]{:S(2)}, u32[]{:S(2)}) collective-permute-start(bf16[16,48,1664]{2,1,0:T(8,128)(2,1)S(1)} %shard_map.186.refs_0_), channel_id=1, source_target_pairs={{0,1},{1,0},{2,3},{3,2},{4,5},{5,4},{6,7},{7,6},{8,9},{9,8},{10,11... | collective-permute-start | bytes 7667720 | tf_op jit(solution)/shard_map/ppermute | solution.py:107
  241.1 21.4 %collective-permute-start.30 = (bf16[128,1664]{1,0:T(8,128)(2,1)S(1)}, bf16[128,1664]{1,0:T(8,128)(2,1)S(1)}, u32[]{:S(2)}, u32[]{:S(2)}) collective-permute-start(bf16[128,1664]{1,0:T(8,128)(2,1)S(1)} %get-tuple-element.288), channel_id=1, source_target_pairs={{0,2},{1,3},{2,0},{3,1},{4,6},{5,7},{6,4},{7,5},{8,10},{9,11},{10,... | collective-permute-start | bytes 1277960 | tf_op jit(solution)/shard_map/ppermute | solution.py:107
  241.2 21.3 %collective-permute-start.31 = (bf16[128,1664]{1,0:T(8,128)(2,1)S(1)}, bf16[128,1664]{1,0:T(8,128)(2,1)S(1)}, u32[]{:S(2)}, u32[]{:S(2)}) collective-permute-start(bf16[128,1664]{1,0:T(8,128)(2,1)S(1)} %get-tuple-element.289), channel_id=1, source_target_pairs={{0,6},{1,7},{2,4},{3,5},{4,2},{5,3},{6,0},{7,1},{8,14},{9,15},{10,... | collective-permute-start | bytes 1277960 | tf_op jit(solution)/shard_map/ppermute | solution.py:107
  265.6 20.0 %collective-permute-start.33 = (bf16[128,1664]{1,0:T(8,128)(2,1)S(1)}, bf16[128,1664]{1,0:T(8,128)(2,1)S(1)}, u32[]{:S(2)}, u32[]{:S(2)}) collective-permute-start(bf16[128,1664]{1,0:T(8,128)(2,1)S(1)} %get-tuple-element.312.refs_0_), channel_id=1, source_target_pairs={{0,2},{1,3},{2,0},{3,1},{4,6},{5,7},{6,4},{7,5},{8,10},{9,11},{10,... | collective-permute-start | bytes 1277960 | tf_op jit(solution)/shard_map/ppermute | solution.py:107
  265.9 19.7 %collective-permute-start.34 = (bf16[128,1664]{1,0:T(8,128)(2,1)S(1)}, bf16[128,1664]{1,0:T(8,128)(2,1)S(1)}, u32[]{:S(2)}, u32[]{:S(2)}) collective-permute-start(bf16[128,1664]{1,0:T(8,128)(2,1)S(1)} %get-tuple-element.312.refs_0_), channel_id=1, source_target_pairs={{0,6},{1,7},{2,4},{3,5},{4,2},{5,3},{6,0},{7,1},{8,14},{9,15},{10,... | collective-permute-start | bytes 1277960 | tf_op jit(solution)/shard_map/ppermute | solution.py:107
  286.8 20.4 %collective-permute-start.37 = (bf16[768,512]{1,0:T(8,128)(2,1)S(1)}, bf16[768,512]{1,0:T(8,128)(2,1)S(1)}, u32[]{:S(2)}, u32[]{:S(2)}) collective-permute-start(bf16[768,512]{1,0:T(8,128)(2,1)S(1)} %get-tuple-element.329), channel_id=1, source_target_pairs={{0,16},{1,17},{2,18},{3,19},{4,20},{5,21},{6,22},{7,23},{8,24},{9,... | collective-permute-start | bytes 2359304 | tf_op jit(solution)/shard_map/ppermute | solution.py:110
  287.4 55.1 %collective-permute-start.43 = (bf16[768,1024]{1,0:T(8,128)(2,1)S(1)}, bf16[768,1024]{1,0:T(8,128)(2,1)S(1)}, u32[]{:S(2)}, u32[]{:S(2)}) collective-permute-start(bf16[768,1024]{1,0:T(8,128)(2,1)S(1)} %get-tuple-element.356), channel_id=1, source_target_pairs={{0,16},{1,17},{2,18},{3,19},{4,20},{5,21},{6,22},{7,23},{8,24},{9,... | collective-permute-start | bytes 4718600 | tf_op jit(solution)/shard_map/ppermute | solution.py:110
  310.6 21.4 %collective-permute-start.41 = (bf16[128,1536]{1,0:T(8,128)(2,1)S(1)}, bf16[128,1536]{1,0:T(8,128)(2,1)S(1)}, u32[]{:S(2)}, u32[]{:S(2)}) collective-permute-start(bf16[128,1536]{1,0:T(8,128)(2,1)S(1)} %get-tuple-element.337), channel_id=1, source_target_pairs={{0,6},{1,7},{2,4},{3,5},{4,2},{5,3},{6,0},{7,1},{8,14},{9,15},{10,... | collective-permute-start | bytes 1179656 | tf_op jit(solution)/shard_map/ppermute | solution.py:107
  335.2 19.9 %collective-permute-start.42 = (bf16[512,1536]{1,0:T(8,128)(2,1)S(1)}, bf16[512,1536]{1,0:T(8,128)(2,1)S(1)}, u32[]{:S(2)}, u32[]{:S(2)}) collective-permute-start(bf16[512,1536]{1,0:T(8,128)(2,1)S(1)} %get-tuple-element.354), channel_id=1, source_target_pairs={{0,1},{1,0},{2,3},{3,2},{4,5},{5,4},{6,7},{7,6},{8,9},{9,8},{10,11... | collective-permute-start | bytes 4718600 | tf_op jit(solution)/shard_map/ppermute | solution.py:107
  335.3 19.8 %collective-permute-start.44 = (bf16[384,512]{1,0:T(8,128)(2,1)S(1)}, bf16[384,512]{1,0:T(8,128)(2,1)S(1)}, u32[]{:S(2)}, u32[]{:S(2)}) collective-permute-start(bf16[384,512]{1,0:T(8,128)(2,1)S(1)} %get-tuple-element.361), channel_id=1, source_target_pairs={{0,8},{1,9},{2,10},{3,11},{4,12},{5,13},{6,14},{7,15},{8,0},{9,1},... | collective-permute-start | bytes 1179656 | tf_op jit(solution)/shard_map/ppermute | solution.py:110
  341.9 23.9 %collective-permute-start.49 = (bf16[768,640]{1,0:T(8,128)(2,1)S(1)}, bf16[768,640]{1,0:T(8,128)(2,1)S(1)}, u32[]{:S(2)}, u32[]{:S(2)}) collective-permute-start(bf16[768,640]{1,0:T(8,128)(2,1)S(1)} %get-tuple-element.374), channel_id=1, source_target_pairs={{0,16},{1,17},{2,18},{3,19},{4,20},{5,21},{6,22},{7,23},{8,24},{9,... | collective-permute-start | bytes 2949128 | tf_op jit(solution)/shard_map/ppermute | solution.py:110
  355.2 40.3 %collective-permute-start.45 = (bf16[384,1024]{1,0:T(8,128)(2,1)S(1)}, bf16[384,1024]{1,0:T(8,128)(2,1)S(1)}, u32[]{:S(2)}, u32[]{:S(2)}) collective-permute-start(bf16[384,1024]{1,0:T(8,128)(2,1)S(1)} %get-tuple-element.363), channel_id=1, source_target_pairs={{0,8},{1,9},{2,10},{3,11},{4,12},{5,13},{6,14},{7,15},{8,0},{9,1},... | collective-permute-start | bytes 2359304 | tf_op jit(solution)/shard_map/ppermute | solution.py:110
  356.1 25.4 %collective-permute-start.46 = (bf16[128,1536]{1,0:T(8,128)(2,1)S(1)}, bf16[128,1536]{1,0:T(8,128)(2,1)S(1)}, u32[]{:S(2)}, u32[]{:S(2)}) collective-permute-start(bf16[128,1536]{1,0:T(8,128)(2,1)S(1)} %get-tuple-element.367), channel_id=1, source_target_pairs={{0,4},{1,5},{2,6},{3,7},{4,0},{5,1},{6,2},{7,3},{8,12},{9,13},{10,... | collective-permute-start | bytes 1179656 | tf_op jit(solution)/shard_map/ppermute | solution.py:107
  358.9 22.6 %collective-permute-start.47 = (bf16[128,1536]{1,0:T(8,128)(2,1)S(1)}, bf16[128,1536]{1,0:T(8,128)(2,1)S(1)}, u32[]{:S(2)}, u32[]{:S(2)}) collective-permute-start(bf16[128,1536]{1,0:T(8,128)(2,1)S(1)} %get-tuple-element.368), channel_id=1, source_target_pairs={{0,2},{1,3},{2,0},{3,1},{4,6},{5,7},{6,4},{7,5},{8,10},{9,11},{10,... | collective-permute-start | bytes 1179656 | tf_op jit(solution)/shard_map/ppermute | solution.py:107
  360.2 33.3 %collective-permute-start.48 = (bf16[128,1536]{1,0:T(8,128)(2,1)S(1)}, bf16[128,1536]{1,0:T(8,128)(2,1)S(1)}, u32[]{:S(2)}, u32[]{:S(2)}) collective-permute-start(bf16[128,1536]{1,0:T(8,128)(2,1)S(1)} %get-tuple-element.369), channel_id=1, source_target_pairs={{0,6},{1,7},{2,4},{3,5},{4,2},{5,3},{6,0},{7,1},{8,14},{9,15},{10,... | collective-permute-start | bytes 1179656 | tf_op jit(solution)/shard_map/ppermute | solution.py:107
  397.3 44.9 %all-to-all-start.2 = ((bf16[8,48,1536]{2,1,0:T(8,128)(2,1)}), bf16[8,48,1536]{2,1,0:T(8,128)(2,1)S(1)}, u32[]{:S(2)}, u32[]{:S(2)}) async-start(bf16[8,48,1536]{2,1,0:T(8,128)(2,1)} %bitcast.17), calls=%async_computation.2 | async-start | bytes 2359296 | tf_op jit(solution)/shard_map/all_to_all | solution.py:126
  400.8 24.2 %collective-permute-start.50 = (bf16[384,640]{1,0:T(8,128)(2,1)S(1)}, bf16[384,640]{1,0:T(8,128)(2,1)S(1)}, u32[]{:S(2)}, u32[]{:S(2)}) collective-permute-start(bf16[384,640]{1,0:T(8,128)(2,1)S(1)} %get-tuple-element.385), channel_id=1, source_target_pairs={{0,8},{1,9},{2,10},{3,11},{4,12},{5,13},{6,14},{7,15},{8,0},{9,1},... | collective-permute-start | bytes 1474568 | tf_op jit(solution)/shard_map/ppermute | solution.py:110
  (77 other events, 1004.9 us)

commit v5 on v4

--- a/solution.py
+++ b/solution.py
@@ -839,8 +839,8 @@
     cot_near = links.near(cot)
     dn_far = [links.outer(dn_group, 0, dg) for dg in range(1, ng)]
     gu_side = [links.outer(gu_group, dx, 0) for dx in range(1, nx)]
-    kv, kvs, dn_group, dn_far, gu_group, gu_side, cot, cot_near, wo_even = fence(
-        kv, kvs, dn_group, dn_far, gu_group, gu_side, cot, cot_near, wo_even
+    kv, kvs, dn_group, dn_far, gu_group, gu_side, cot, cot_near = fence(
+        kv, kvs, dn_group, dn_far, gu_group, gu_side, cot, cot_near
     )
     wo_odd = links.core(wo_even)
     kvs = [kv] + list(kvs)

time: 445 us -> 432 us (0.971)
  waiting for transfers between devices: 236 us -> 199 us
  starting transfers between devices: 79.7 us -> 107 us
    ppermute x17, waiting for transfers between devices: 89.6 us -> 68 us  [outer(): lax.ppermute(value, AXES, self._pairs(lambda x, g, t: (x ^ dx, g ^ dg, t)))]
    ppermute x39, starting transfers between devices: 38.1 us -> 57.8 us  [cube(): lax.ppermute(value, AXES, self._pairs(lambda x, g, t: (x, g, t ^ bits)))]
    ppermute x2, waiting for transfers between devices: 21.8 us -> 5.43 us  [climb(): return lax.ppermute(value, AXES, self._pairs(move))]
    all_to_all x3, starting transfers between devices: 13.2 us -> 20.6 us  [swap(): lax.all_to_all(value, AXES, split_axis=0, concat_axis=0, tiled=True, axis...]
  transfers between devices with their start and end apart: 61 -> 61, of which waited for: 28 -> 31; matrix products, arithmetic and copies ran while one was open for 0% -> 0% of each run, Pallas kernels for 21% -> 22%
where the time goes in v5:
time: 432 us
  waiting for transfers between devices  199 us (46%)
  Pallas kernels  110 us (25%)
  starting transfers between devices  107 us (25%)
  local copies, waits for them, and re-layouts  15.1 us (3%)
    ppermute x39, waiting for transfers between devices, cube(): lax.ppermute(value, AXES, self._pairs(lambda x, g, t: (x, g, t ^ bits)))  122 us
    pallas_call x38, Pallas kernels, __call__(): pl.pallas_call(run, out_shape=list(outs), in_specs=[pl.BlockSpec(memory_s...  110 us
    ppermute x17, waiting for transfers between devices, outer(): lax.ppermute(value, AXES, self._pairs(lambda x, g, t: (x ^ dx, g ^ dg, t)))  68 us
    ppermute x39, starting transfers between devices, cube(): lax.ppermute(value, AXES, self._pairs(lambda x, g, t: (x, g, t ^ bits)))  57.8 us
    ppermute x17, starting transfers between devices, outer(): lax.ppermute(value, AXES, self._pairs(lambda x, g, t: (x ^ dx, g ^ dg, t)))  26 us
    all_to_all x3, starting transfers between devices, swap(): lax.all_to_all(value, AXES, split_axis=0, concat_axis=0, tiled=True, axis...  20.6 us
    unnamed x98, local copies, waits for them, and re-layouts  14.5 us
  transfers between devices with their start and end apart: 61, of which 31 were waited for; matrix products, arithmetic and copies ran while one was open for 0% of the time, Pallas kernels for 22%

profile of v5, /device:TPU:0, one launch (start us, length us, event | category | flops | bytes accessed | tf_op | source)
XLA Modules:
  0.0 432.5 jit_solution(12247734578541991171)
XLA Ops:
  6.3 5.3 %all-to-all-start = ((bf16[8,48,384]{2,1,0:T(8,128)(2,1)}), bf16[8,48,384]{2,1,0:T(8,128)(2,1)S(1)}, u32[]{:S(2)}, u32[]{:S(2)}) async-start(bf16[8,48,384]{2,1,0:T(8,128)(2,1)} %get-tuple-element.214), calls=%async_computation | async-start | bytes 589824 | tf_op jit(solution)/shard_map/all_to_all | solution.py:126
  20.1 11.8 %all-to-all-start.1 = ((bf16[8,48,1536]{2,1,0:T(8,128)(2,1)}), bf16[8,48,1536]{2,1,0:T(8,128)(2,1)}, u32[]{:S(2)}, u32[]{:S(2)}) async-start(bf16[8,48,1536]{2,1,0:T(8,128)(2,1)} %shard_map.181), calls=%async_computation.1 | async-start | bytes 2359296 | tf_op jit(solution)/shard_map/all_to_all | solution.py:126
  41.6 11.6 %collective-permute-done.4.refs_3_ = bf16[384,384]{1,0:T(8,128)(2,1)S(1)} collective-permute-done((bf16[384,384]{1,0:T(8,128)(2,1)S(1)}, bf16[384,384]{1,0:T(8,128)(2,1)S(1)}, u32[]{:S(2)}, u32[]{:S(2)}) %collective-permute-start.4) | collective-permute-done | bytes 294944 | tf_op jit(solution)/shard_map/ppermute | solution.py:110
  58.1 7.3 %collective-permute-done.7.refs_1_ = bf16[1,48,1664]{2,1,0:T(8,128)(2,1)S(1)} collective-permute-done((bf16[1,48,1664]{2,1,0:T(8,128)(2,1)S(1)}, bf16[1,48,1664]{2,1,0:T(8,128)(2,1)S(1)}, u32[]{:S(2)}, u32[]{:S(2)}) %collective-permute-start.7) | collective-permute-done | bytes 159776 | tf_op jit(solution)/shard_map/ppermute | solution.py:110
  69.5 6.0 %shard_map.182 = (bf16[1024,1536]{1,0:T(8,128)(2,1)}, bf16[2,3,512,128]{3,2,1,0:T(8,128)(2,1)S(1)}, bf16[2,512,128]{2,1,0:T(8,128)(2,1)S(1)}, f32[8,1536]{1,0:T(8,128)}, bf16[1536,384]{1,0:T(8,128)(2,1)}) custom-call(s32[2,1]{1,0:T(2,128)S(1)} %copy.48.lengths, bf16[512,1664]{1,0:T(8,128)(2,1)S(1)} %shard_map.180.refs_0_.refs_2_, ...), custom_call_target="tpu_custom_call" | custom-call | flops 1000 | bytes 1000 | tf_op jit(solution)/shard_map/pallas_call | solution.py:62
  77.4 5.3 %collective-permute-start.13 = (bf16[128,1536]{1,0:T(8,128)(2,1)S(1)}, bf16[128,1536]{1,0:T(8,128)(2,1)S(1)}, u32[]{:S(2)}, u32[]{:S(2)}) collective-permute-start(bf16[128,1536]{1,0:T(8,128)(2,1)S(1)} %bitcast.27), channel_id=1, source_target_pairs={{0,6},{1,7},{2,4},{3,5},{4,2},{5,3},{6,0},{7,1},{8,14},{9,15},{10,... | collective-permute-start | bytes 1179656 | tf_op jit(solution)/shard_map/ppermute | solution.py:107
  83.8 13.3 %collective-permute-start.11 = (bf16[128,1536]{1,0:T(8,128)(2,1)S(1)}, bf16[128,1536]{1,0:T(8,128)(2,1)S(1)}, u32[]{:S(2)}, u32[]{:S(2)}) collective-permute-start(bf16[128,1536]{1,0:T(8,128)(2,1)S(1)} %bitcast.29), channel_id=1, source_target_pairs={{0,4},{1,5},{2,6},{3,7},{4,0},{5,1},{6,2},{7,3},{8,12},{9,13},{10,... | collective-permute-start | bytes 1179656 | tf_op jit(solution)/shard_map/ppermute | solution.py:107
  101.2 5.7 %collective-permute-done.11.refs_1_ = bf16[128,1536]{1,0:T(8,128)(2,1)S(1)} collective-permute-done((bf16[128,1536]{1,0:T(8,128)(2,1)S(1)}, bf16[128,1536]{1,0:T(8,128)(2,1)S(1)}, u32[]{:S(2)}, u32[]{:S(2)}) %collective-permute-start.11) | collective-permute-done | bytes 393248 | tf_op jit(solution)/shard_map/ppermute | solution.py:107
  108.3 7.8 %collective-permute-start.17 = (bf16[4,48,1664]{2,1,0:T(8,128)(2,1)S(1)}, bf16[4,48,1664]{2,1,0:T(8,128)(2,1)S(1)}, u32[]{:S(2)}, u32[]{:S(2)}) collective-permute-start(bf16[4,48,1664]{2,1,0:T(8,128)(2,1)S(1)} %shard_map.186.refs_0_), channel_id=1, source_target_pairs={{0,6},{1,7},{2,4},{3,5},{4,2},{5,3},{6,0},{7,1},{8,14},{9,15},{10,... | collective-permute-start | bytes 1916936 | tf_op jit(solution)/shard_map/ppermute | solution.py:107
  118.0 7.3 %shard_map.184 = (bf16[512,384]{1,0:T(8,128)(2,1)S(1)}, f32[2,3,64,512]{3,2,1,0:T(8,128)}, f32[2,3,512]{2,1,0:T(4,128)}) custom-call(s32[2,1]{1,0:T(2,128)S(1)} %copy.48.lengths, bf16[2,3,512,128]{3,2,1,0:T(8,128)(2,1)S(1)} %get-tuple-element.225.refs_0_, bf16[2,512,128]{2,1,0:T(8,128)(2,1)S(1)} %get-tuple-element.234.refs_1_, ...), custom_call_target="tpu_custom_call" | custom-call | flops 1000 | bytes 1000 | tf_op jit(solution)/shard_map/pallas_call | solution.py:62
  125.3 6.1 %collective-permute-done.17.refs_3_ = bf16[4,48,1664]{2,1,0:T(8,128)(2,1)S(1)} collective-permute-done((bf16[4,48,1664]{2,1,0:T(8,128)(2,1)S(1)}, bf16[4,48,1664]{2,1,0:T(8,128)(2,1)S(1)}, u32[]{:S(2)}, u32[]{:S(2)}) %collective-permute-start.17) | collective-permute-done | bytes 639008 | tf_op jit(solution)/shard_map/ppermute | solution.py:107
  132.4 11.2 %collective-permute-done.16.refs_2_ = bf16[4,48,1664]{2,1,0:T(8,128)(2,1)S(1)} collective-permute-done((bf16[4,48,1664]{2,1,0:T(8,128)(2,1)S(1)}, bf16[4,48,1664]{2,1,0:T(8,128)(2,1)S(1)}, u32[]{:S(2)}, u32[]{:S(2)}) %collective-permute-start.16) | collective-permute-done | bytes 639008 | tf_op jit(solution)/shard_map/ppermute | solution.py:107
  145.3 5.0 %collective-permute-start.25 = (bf16[384,1024]{1,0:T(8,128)(2,1)S(1)}, bf16[384,1024]{1,0:T(8,128)(2,1)S(1)}, u32[]{:S(2)}, u32[]{:S(2)}) collective-permute-start(bf16[384,1024]{1,0:T(8,128)(2,1)S(1)} %get-tuple-element.270.refs_2_), channel_id=1, source_target_pairs={{0,8},{1,9},{2,10},{3,11},{4,12},{5,13},{6,14},{7,15},{8,0},{9,1},... | collective-permute-start | bytes 2359304 | tf_op jit(solution)/shard_map/ppermute | solution.py:110
  152.6 11.5 %collective-permute-done.21.refs_3_ = bf16[512,384]{1,0:T(8,128)(2,1)S(1)} collective-permute-done((bf16[512,384]{1,0:T(8,128)(2,1)S(1)}, bf16[512,384]{1,0:T(8,128)(2,1)S(1)}, u32[]{:S(2)}, u32[]{:S(2)}) %collective-permute-start.21) | collective-permute-done | bytes 393248 | tf_op jit(solution)/shard_map/ppermute | solution.py:107
  166.6 11.7 %collective-permute-done.19.refs_1_ = bf16[512,384]{1,0:T(8,128)(2,1)S(1)} collective-permute-done((bf16[512,384]{1,0:T(8,128)(2,1)S(1)}, bf16[512,384]{1,0:T(8,128)(2,1)S(1)}, u32[]{:S(2)}, u32[]{:S(2)}) %collective-permute-start.19) | collective-permute-done | bytes 393248 | tf_op jit(solution)/shard_map/ppermute | solution.py:107
  178.3 5.8 %collective-permute-done.25.refs_3_ = bf16[384,1024]{1,0:T(8,128)(2,1)S(1)} collective-permute-done((bf16[384,1024]{1,0:T(8,128)(2,1)S(1)}, bf16[384,1024]{1,0:T(8,128)(2,1)S(1)}, u32[]{:S(2)}, u32[]{:S(2)}) %collective-permute-start.25) | collective-permute-done | bytes 786464 | tf_op jit(solution)/shard_map/ppermute | solution.py:110
  192.0 10.5 %shard_map.192 = (bf16[512,1664]{1,0:T(8,128)(2,1)S(1)}, bf16[512,1664]{1,0:T(8,128)(2,1)S(1)}, f32[128,1536]{1,0:T(8,128)}, f32[128,128]{1,0:T(8,128)}) custom-call(s32[2,1]{1,0:T(2,128)S(1)} %copy.48.lengths, bf16[2048,384]{1,0:T(8,128)(2,1)S(1)} %shard_map.190.refs_0_, bf16[2048,384]{1,0:T(8,128)(2,1)S(1)} %collective-permute-done.27.refs_1_, ...), custom_call_target="tpu_custom_call" | custom-call | flops 1000 | bytes 1000 | tf_op jit(solution)/shard_map/pallas_call | solution.py:62
  204.0 6.6 %shard_map.193 = (bf16[512,512]{1,0:T(8,128)(2,1)S(1)}, bf16[512,1024]{1,0:T(8,128)(2,1)S(1)}, bf16[512,1664]{1,0:T(8,128)(2,1)S(1)}, bf16[1536,1024]{1,0:T(8,128)(2,1)S(1)}) custom-call(s32[2,1]{1,0:T(2,128)S(1)} %copy.48.lengths, bf16[512,1664]{1,0:T(8,128)(2,1)S(1)} %get-tuple-element.300.refs_0_.refs_2_.refs_3_.refs_4_, ...), custom_call_target="tpu_custom_call" | custom-call | flops 1000 | bytes 1000 | tf_op jit(solution)/shard_map/pallas_call | solution.py:62
  210.8 16.2 %shard_map.194 = (bf16[512,512]{1,0:T(8,128)(2,1)S(1)}, bf16[512,1024]{1,0:T(8,128)(2,1)S(1)}, bf16[512,1664]{1,0:T(8,128)(2,1)S(1)}) custom-call(s32[2,1]{1,0:T(2,128)S(1)} %copy.48.lengths, bf16[512,1664]{1,0:T(8,128)(2,1)S(1)} %get-tuple-element.299.refs_0_.refs_1_.refs_2_.refs_3_, f32[1024,512]{1,0:T(8,128)S(1)} %get-tuple-element.269.refs_1_, ...), custom_call_target="tpu_custom_call" | custom-call | flops 1000 | bytes 1000 | tf_op jit(solution)/shard_map/pallas_call | solution.py:62
  231.5 9.1 %collective-permute-done.29.refs_1_ = bf16[128,1664]{1,0:T(8,128)(2,1)S(1)} collective-permute-done((bf16[128,1664]{1,0:T(8,128)(2,1)S(1)}, bf16[128,1664]{1,0:T(8,128)(2,1)S(1)}, u32[]{:S(2)}, u32[]{:S(2)}) %collective-permute-start.29) | collective-permute-done | bytes 426016 | tf_op jit(solution)/shard_map/ppermute | solution.py:107
  240.6 8.3 %collective-permute-done.30.refs_2_ = bf16[128,1664]{1,0:T(8,128)(2,1)S(1)} collective-permute-done((bf16[128,1664]{1,0:T(8,128)(2,1)S(1)}, bf16[128,1664]{1,0:T(8,128)(2,1)S(1)}, u32[]{:S(2)}, u32[]{:S(2)}) %collective-permute-start.30) | collective-permute-done | bytes 426016 | tf_op jit(solution)/shard_map/ppermute | solution.py:107
  255.5 7.0 %shard_map.198 = (bf16[768,1024]{1,0:T(8,128)(2,1)S(1)}, bf16[768,512]{1,0:T(8,128)(2,1)S(1)}, bf16[768,1024]{1,0:T(8,128)(2,1)S(1)}, bf16[768,512]{1,0:T(8,128)(2,1)S(1)}) custom-call(s32[2,1]{1,0:T(2,128)S(1)} %copy.48.lengths, bf16[512,1536]{1,0:T(8,128)(2,1)S(1)} %shard_map.189.refs_0_, bf16[512,1536]{1,0:T(8,128)(2,1)S(1)} %collective-permute-done.22.refs_1_, ...), custom_call_target="tpu_custom_call" | custom-call | flops 20000000000 | bytes 1000 | tf_op jit(solution)/shard_map/pallas_call | solution.py:62
  265.7 7.8 %collective-permute-done.33.refs_2_ = bf16[128,1664]{1,0:T(8,128)(2,1)S(1)} collective-permute-done((bf16[128,1664]{1,0:T(8,128)(2,1)S(1)}, bf16[128,1664]{1,0:T(8,128)(2,1)S(1)}, u32[]{:S(2)}, u32[]{:S(2)}) %collective-permute-start.33) | collective-permute-done | bytes 426016 | tf_op jit(solution)/shard_map/ppermute | solution.py:107
  283.8 8.6 %shard_map.201 = (bf16[8,128,192]{2,1,0:T(8,128)(2,1)S(1)}, f32[2,512,128]{2,1,0:T(8,128)S(1)}, bf16[2,512,128]{2,1,0:T(8,128)(2,1)S(1)}) custom-call(s32[2,1]{1,0:T(2,128)S(1)} %copy.48.lengths, bf16[2,3,512,128]{3,2,1,0:T(8,128)(2,1)S(1)} %get-tuple-element.225.refs_0_, bf16[2,512,128]{2,1,0:T(8,128)(2,1)S(1)} %get-tuple-element.234.refs_1_, ...), custom_call_target="tpu_custom_call" | custom-call | flops 1000 | bytes 1000 | tf_op jit(solution)/shard_map/pallas_call | solution.py:62
  300.0 4.7 %shard_map.203.refs_2_ = bf16[1536,256]{1,0:T(8,128)(2,1)} custom-call(s32[2,1]{1,0:T(2,128)S(1)} %copy.48.lengths, bf16[512,1664]{1,0:T(8,128)(2,1)S(1)} %shard_map.199.refs_1_.refs_0_, bf16[512,1664]{1,0:T(8,128)(2,1)S(1)} %collective-permute-done.35.refs_2_.refs_1_, bf16[512,384]{1,0:T(8,128)(2,1)S(1)} %get-tuple-element.251.refs_0_.refs_2_, ...), custom_call_target="tpu_custom_call" | custom-call | flops 20000000000 | bytes 1000 | tf_op jit(solution)/shard_map/pallas_call | solution.py:62
  305.4 4.8 %collective-permute-done.38.refs_3_ = bf16[2,512,128]{2,1,0:T(8,128)(2,1)S(1)} collective-permute-done((bf16[2,512,128]{2,1,0:T(8,128)(2,1)S(1)}, bf16[2,512,128]{2,1,0:T(8,128)(2,1)S(1)}, u32[]{:S(2)}, u32[]{:S(2)}) %collective-permute-start.38) | collective-permute-done | bytes 262176 | tf_op jit(solution)/shard_map/ppermute | solution.py:116
  314.8 5.2 %collective-permute-done.41.refs_3_ = bf16[128,1536]{1,0:T(8,128)(2,1)S(1)} collective-permute-done((bf16[128,1536]{1,0:T(8,128)(2,1)S(1)}, bf16[128,1536]{1,0:T(8,128)(2,1)S(1)}, u32[]{:S(2)}, u32[]{:S(2)}) %collective-permute-start.41) | collective-permute-done | bytes 393248 | tf_op jit(solution)/shard_map/ppermute | solution.py:107
  332.2 10.9 %collective-permute-done.44.refs_3_ = bf16[384,512]{1,0:T(8,128)(2,1)S(1)} collective-permute-done((bf16[384,512]{1,0:T(8,128)(2,1)S(1)}, bf16[384,512]{1,0:T(8,128)(2,1)S(1)}, u32[]{:S(2)}, u32[]{:S(2)}) %collective-permute-start.44) | collective-permute-done | bytes 393248 | tf_op jit(solution)/shard_map/ppermute | solution.py:110
  348.2 5.4 %collective-permute-done.49.refs_1_ = bf16[768,640]{1,0:T(8,128)(2,1)S(1)} collective-permute-done((bf16[768,640]{1,0:T(8,128)(2,1)S(1)}, bf16[768,640]{1,0:T(8,128)(2,1)S(1)}, u32[]{:S(2)}, u32[]{:S(2)}) %collective-permute-start.49) | collective-permute-done | bytes 983072 | tf_op jit(solution)/shard_map/ppermute | solution.py:110
  354.4 15.0 %collective-permute-done.46.refs_1_ = bf16[128,1536]{1,0:T(8,128)(2,1)S(1)} collective-permute-done((bf16[128,1536]{1,0:T(8,128)(2,1)S(1)}, bf16[128,1536]{1,0:T(8,128)(2,1)S(1)}, u32[]{:S(2)}, u32[]{:S(2)}) %collective-permute-start.46) | collective-permute-done | bytes 393248 | tf_op jit(solution)/shard_map/ppermute | solution.py:107
  369.4 12.0 %collective-permute-done.48.refs_3_ = bf16[128,1536]{1,0:T(8,128)(2,1)S(1)} collective-permute-done((bf16[128,1536]{1,0:T(8,128)(2,1)S(1)}, bf16[128,1536]{1,0:T(8,128)(2,1)S(1)}, u32[]{:S(2)}, u32[]{:S(2)}) %collective-permute-start.48) | collective-permute-done | bytes 393248 | tf_op jit(solution)/shard_map/ppermute | solution.py:107
  389.2 23.7 %collective-permute-done.50.refs_1_ = bf16[384,640]{1,0:T(8,128)(2,1)S(1)} collective-permute-done((bf16[384,640]{1,0:T(8,128)(2,1)S(1)}, bf16[384,640]{1,0:T(8,128)(2,1)S(1)}, u32[]{:S(2)}, u32[]{:S(2)}) %collective-permute-start.50) | collective-permute-done | bytes 491552 | tf_op jit(solution)/shard_map/ppermute | solution.py:110
  (227 shorter events, 142.5 us)
Async XLA Ops:
  11.5 21.0 %collective-permute-start.2 = (bf16[128,1664]{1,0:T(8,128)(2,1)S(1)}, bf16[128,1664]{1,0:T(8,128)(2,1)S(1)}, u32[]{:S(2)}, u32[]{:S(2)}) collective-permute-start(bf16[128,1664]{1,0:T(8,128)(2,1)S(1)} %get-tuple-element.210.refs_0_), channel_id=1, source_target_pairs={{0,6},{1,7},{2,4},{3,5},{4,2},{5,3},{6,0},{7,1},{8,14},{9,15},{10,... | collective-permute-start | bytes 1277960 | tf_op jit(solution)/shard_map/ppermute | solution.py:107
  14.5 21.8 %collective-permute-start.1 = (bf16[128,1664]{1,0:T(8,128)(2,1)S(1)}, bf16[128,1664]{1,0:T(8,128)(2,1)S(1)}, u32[]{:S(2)}, u32[]{:S(2)}) collective-permute-start(bf16[128,1664]{1,0:T(8,128)(2,1)S(1)} %get-tuple-element.210.refs_0_), channel_id=1, source_target_pairs={{0,2},{1,3},{2,0},{3,1},{4,6},{5,7},{6,4},{7,5},{8,10},{9,11},{10,... | collective-permute-start | bytes 1277960 | tf_op jit(solution)/shard_map/ppermute | solution.py:107
  15.0 21.7 %collective-permute-start = (bf16[128,1664]{1,0:T(8,128)(2,1)S(1)}, bf16[128,1664]{1,0:T(8,128)(2,1)S(1)}, u32[]{:S(2)}, u32[]{:S(2)}) collective-permute-start(bf16[128,1664]{1,0:T(8,128)(2,1)S(1)} %get-tuple-element.210.refs_0_), channel_id=1, source_target_pairs={{0,4},{1,5},{2,6},{3,7},{4,0},{5,1},{6,2},{7,3},{8,12},{9,13},{10,... | collective-permute-start | bytes 1277960 | tf_op jit(solution)/shard_map/ppermute | solution.py:107
  20.1 47.4 %all-to-all-start.1 = ((bf16[8,48,1536]{2,1,0:T(8,128)(2,1)}), bf16[8,48,1536]{2,1,0:T(8,128)(2,1)}, u32[]{:S(2)}, u32[]{:S(2)}) async-start(bf16[8,48,1536]{2,1,0:T(8,128)(2,1)} %shard_map.181), calls=%async_computation.1 | async-start | bytes 2359296 | tf_op jit(solution)/shard_map/all_to_all | solution.py:126
  37.4 30.1 %collective-permute-start.3 = (bf16[512,1664]{1,0:T(8,128)(2,1)S(1)}, bf16[512,1664]{1,0:T(8,128)(2,1)S(1)}, u32[]{:S(2)}, u32[]{:S(2)}) collective-permute-start(bf16[512,1664]{1,0:T(8,128)(2,1)S(1)} %shard_map.180.refs_0_.refs_2_), channel_id=1, source_target_pairs={{0,1},{1,0},{2,3},{3,2},{4,5},{5,4},{6,7},{7,6},{8,9},{9,8},{10,11... | collective-permute-start | bytes 5111816 | tf_op jit(solution)/shard_map/ppermute | solution.py:107
  40.1 25.9 %collective-permute-start.5 = (bf16[384,384]{1,0:T(8,128)(2,1)S(1)}, bf16[384,384]{1,0:T(8,128)(2,1)S(1)}, u32[]{:S(2)}, u32[]{:S(2)}) collective-permute-start(bf16[384,384]{1,0:T(8,128)(2,1)S(1)} %bitcast.45), channel_id=1, source_target_pairs={{0,16},{1,17},{2,18},{3,19},{4,20},{5,21},{6,22},{7,23},{8,24},{9,... | collective-permute-start | bytes 884744 | tf_op jit(solution)/shard_map/ppermute | solution.py:110
  68.9 37.9 %collective-permute-start.10 = (bf16[384,1024]{1,0:T(8,128)(2,1)S(1)}, bf16[384,1024]{1,0:T(8,128)(2,1)S(1)}, u32[]{:S(2)}, u32[]{:S(2)}) collective-permute-start(bf16[384,1024]{1,0:T(8,128)(2,1)S(1)} %get-tuple-element.270.refs_2_), channel_id=1, source_target_pairs={{0,16},{1,17},{2,18},{3,19},{4,20},{5,21},{6,22},{7,23},{8,24},{9,... | collective-permute-start | bytes 2359304 | tf_op jit(solution)/shard_map/ppermute | solution.py:110
  77.3 20.4 %collective-permute-start.9 = (bf16[384,512]{1,0:T(8,128)(2,1)S(1)}, bf16[384,512]{1,0:T(8,128)(2,1)S(1)}, u32[]{:S(2)}, u32[]{:S(2)}) collective-permute-start(bf16[384,512]{1,0:T(8,128)(2,1)S(1)} %get-tuple-element.260.refs_2_), channel_id=1, source_target_pairs={{0,8},{1,9},{2,10},{3,11},{4,12},{5,13},{6,14},{7,15},{8,0},{9,1},... | collective-permute-start | bytes 1179656 | tf_op jit(solution)/shard_map/ppermute | solution.py:110
  77.4 22.2 %collective-permute-start.13 = (bf16[128,1536]{1,0:T(8,128)(2,1)S(1)}, bf16[128,1536]{1,0:T(8,128)(2,1)S(1)}, u32[]{:S(2)}, u32[]{:S(2)}) collective-permute-start(bf16[128,1536]{1,0:T(8,128)(2,1)S(1)} %bitcast.27), channel_id=1, source_target_pairs={{0,6},{1,7},{2,4},{3,5},{4,2},{5,3},{6,0},{7,1},{8,14},{9,15},{10,... | collective-permute-start | bytes 1179656 | tf_op jit(solution)/shard_map/ppermute | solution.py:107
  83.8 23.0 %collective-permute-start.11 = (bf16[128,1536]{1,0:T(8,128)(2,1)S(1)}, bf16[128,1536]{1,0:T(8,128)(2,1)S(1)}, u32[]{:S(2)}, u32[]{:S(2)}) collective-permute-start(bf16[128,1536]{1,0:T(8,128)(2,1)S(1)} %bitcast.29), channel_id=1, source_target_pairs={{0,4},{1,5},{2,6},{3,7},{4,0},{5,1},{6,2},{7,3},{8,12},{9,13},{10,... | collective-permute-start | bytes 1179656 | tf_op jit(solution)/shard_map/ppermute | solution.py:107
  107.7 76.4 %collective-permute-start.22 = (bf16[512,1536]{1,0:T(8,128)(2,1)S(1)}, bf16[512,1536]{1,0:T(8,128)(2,1)S(1)}, u32[]{:S(2)}, u32[]{:S(2)}) collective-permute-start(bf16[512,1536]{1,0:T(8,128)(2,1)S(1)} %shard_map.189.refs_0_), channel_id=1, source_target_pairs={{0,1},{1,0},{2,3},{3,2},{4,5},{5,4},{6,7},{7,6},{8,9},{9,8},{10,11... | collective-permute-start | bytes 4718600 | tf_op jit(solution)/shard_map/ppermute | solution.py:107
  108.3 23.1 %collective-permute-start.17 = (bf16[4,48,1664]{2,1,0:T(8,128)(2,1)S(1)}, bf16[4,48,1664]{2,1,0:T(8,128)(2,1)S(1)}, u32[]{:S(2)}, u32[]{:S(2)}) collective-permute-start(bf16[4,48,1664]{2,1,0:T(8,128)(2,1)S(1)} %shard_map.186.refs_0_), channel_id=1, source_target_pairs={{0,6},{1,7},{2,4},{3,5},{4,2},{5,3},{6,0},{7,1},{8,14},{9,15},{10,... | collective-permute-start | bytes 1916936 | tf_op jit(solution)/shard_map/ppermute | solution.py:107
  116.1 27.4 %collective-permute-start.16 = (bf16[4,48,1664]{2,1,0:T(8,128)(2,1)S(1)}, bf16[4,48,1664]{2,1,0:T(8,128)(2,1)S(1)}, u32[]{:S(2)}, u32[]{:S(2)}) collective-permute-start(bf16[4,48,1664]{2,1,0:T(8,128)(2,1)S(1)} %shard_map.186.refs_0_), channel_id=1, source_target_pairs={{0,2},{1,3},{2,0},{3,1},{4,6},{5,7},{6,4},{7,5},{8,10},{9,11},{10,... | collective-permute-start | bytes 1916936 | tf_op jit(solution)/shard_map/ppermute | solution.py:107
  117.1 28.3 %collective-permute-start.15 = (bf16[4,48,1664]{2,1,0:T(8,128)(2,1)S(1)}, bf16[4,48,1664]{2,1,0:T(8,128)(2,1)S(1)}, u32[]{:S(2)}, u32[]{:S(2)}) collective-permute-start(bf16[4,48,1664]{2,1,0:T(8,128)(2,1)S(1)} %shard_map.186.refs_0_), channel_id=1, source_target_pairs={{0,4},{1,5},{2,6},{3,7},{4,0},{5,1},{6,2},{7,3},{8,12},{9,13},{10,... | collective-permute-start | bytes 1916936 | tf_op jit(solution)/shard_map/ppermute | solution.py:107
  117.1 34.0 %collective-permute-start.23 = (bf16[384,512]{1,0:T(8,128)(2,1)S(1)}, bf16[384,512]{1,0:T(8,128)(2,1)S(1)}, u32[]{:S(2)}, u32[]{:S(2)}) collective-permute-start(bf16[384,512]{1,0:T(8,128)(2,1)S(1)} %get-tuple-element.260.refs_2_), channel_id=1, source_target_pairs={{0,16},{1,17},{2,18},{3,19},{4,20},{5,21},{6,22},{7,23},{8,24},{9,... | collective-permute-start | bytes 1179656 | tf_op jit(solution)/shard_map/ppermute | solution.py:110
  131.4 19.7 %collective-permute-start.24 = (bf16[384,512]{1,0:T(8,128)(2,1)S(1)}, bf16[384,512]{1,0:T(8,128)(2,1)S(1)}, u32[]{:S(2)}, u32[]{:S(2)}) collective-permute-start(bf16[384,512]{1,0:T(8,128)(2,1)S(1)} %collective-permute-done.9.refs_3_), channel_id=1, source_target_pairs={{0,16},{1,17},{2,18},{3,19},{4,20},{5,21},{6,22},{7,23},{8,24},{9,... | collective-permute-start | bytes 1179656 | tf_op jit(solution)/shard_map/ppermute | solution.py:110
  143.5 20.6 %collective-permute-start.21 = (bf16[512,384]{1,0:T(8,128)(2,1)S(1)}, bf16[512,384]{1,0:T(8,128)(2,1)S(1)}, u32[]{:S(2)}, u32[]{:S(2)}) collective-permute-start(bf16[512,384]{1,0:T(8,128)(2,1)S(1)} %get-tuple-element.251.refs_0_.refs_2_), channel_id=1, source_target_pairs={{0,6},{1,7},{2,4},{3,5},{4,2},{5,3},{6,0},{7,1},{8,14},{9,15},{10,... | collective-permute-start | bytes 1179656 | tf_op jit(solution)/shard_map/ppermute | solution.py:107
  145.3 38.8 %collective-permute-start.25 = (bf16[384,1024]{1,0:T(8,128)(2,1)S(1)}, bf16[384,1024]{1,0:T(8,128)(2,1)S(1)}, u32[]{:S(2)}, u32[]{:S(2)}) collective-permute-start(bf16[384,1024]{1,0:T(8,128)(2,1)S(1)} %get-tuple-element.270.refs_2_), channel_id=1, source_target_pairs={{0,8},{1,9},{2,10},{3,11},{4,12},{5,13},{6,14},{7,15},{8,0},{9,1},... | collective-permute-start | bytes 2359304 | tf_op jit(solution)/shard_map/ppermute | solution.py:110
  151.1 40.0 %collective-permute-start.18 = (bf16[16,48,1664]{2,1,0:T(8,128)(2,1)S(1)}, bf16[16,48,1664]{2,1,0:T(8,128)(2,1)S(1)}, u32[]{:S(2)}, u32[]{:S(2)}) collective-permute-start(bf16[16,48,1664]{2,1,0:T(8,128)(2,1)S(1)} %shard_map.187.refs_0_), channel_id=1, source_target_pairs={{0,1},{1,0},{2,3},{3,2},{4,5},{5,4},{6,7},{7,6},{8,9},{9,8},{10,11... | collective-permute-start | bytes 7667720 | tf_op jit(solution)/shard_map/ppermute | solution.py:107
  230.0 20.7 %collective-permute-start.31 = (bf16[128,1664]{1,0:T(8,128)(2,1)S(1)}, bf16[128,1664]{1,0:T(8,128)(2,1)S(1)}, u32[]{:S(2)}, u32[]{:S(2)}) collective-permute-start(bf16[128,1664]{1,0:T(8,128)(2,1)S(1)} %get-tuple-element.287), channel_id=1, source_target_pairs={{0,6},{1,7},{2,4},{3,5},{4,2},{5,3},{6,0},{7,1},{8,14},{9,15},{10,... | collective-permute-start | bytes 1277960 | tf_op jit(solution)/shard_map/ppermute | solution.py:107
  274.8 20.4 %collective-permute-start.37 = (bf16[768,512]{1,0:T(8,128)(2,1)S(1)}, bf16[768,512]{1,0:T(8,128)(2,1)S(1)}, u32[]{:S(2)}, u32[]{:S(2)}) collective-permute-start(bf16[768,512]{1,0:T(8,128)(2,1)S(1)} %get-tuple-element.327), channel_id=1, source_target_pairs={{0,16},{1,17},{2,18},{3,19},{4,20},{5,21},{6,22},{7,23},{8,24},{9,... | collective-permute-start | bytes 2359304 | tf_op jit(solution)/shard_map/ppermute | solution.py:110
  276.3 55.0 %collective-permute-start.43 = (bf16[768,1024]{1,0:T(8,128)(2,1)S(1)}, bf16[768,1024]{1,0:T(8,128)(2,1)S(1)}, u32[]{:S(2)}, u32[]{:S(2)}) collective-permute-start(bf16[768,1024]{1,0:T(8,128)(2,1)S(1)} %get-tuple-element.354), channel_id=1, source_target_pairs={{0,16},{1,17},{2,18},{3,19},{4,20},{5,21},{6,22},{7,23},{8,24},{9,... | collective-permute-start | bytes 4718600 | tf_op jit(solution)/shard_map/ppermute | solution.py:110
  298.5 21.5 %collective-permute-start.41 = (bf16[128,1536]{1,0:T(8,128)(2,1)S(1)}, bf16[128,1536]{1,0:T(8,128)(2,1)S(1)}, u32[]{:S(2)}, u32[]{:S(2)}) collective-permute-start(bf16[128,1536]{1,0:T(8,128)(2,1)S(1)} %get-tuple-element.335), channel_id=1, source_target_pairs={{0,6},{1,7},{2,4},{3,5},{4,2},{5,3},{6,0},{7,1},{8,14},{9,15},{10,... | collective-permute-start | bytes 1179656 | tf_op jit(solution)/shard_map/ppermute | solution.py:107
  323.2 19.8 %collective-permute-start.42 = (bf16[512,1536]{1,0:T(8,128)(2,1)S(1)}, bf16[512,1536]{1,0:T(8,128)(2,1)S(1)}, u32[]{:S(2)}, u32[]{:S(2)}) collective-permute-start(bf16[512,1536]{1,0:T(8,128)(2,1)S(1)} %get-tuple-element.352), channel_id=1, source_target_pairs={{0,1},{1,0},{2,3},{3,2},{4,5},{5,4},{6,7},{7,6},{8,9},{9,8},{10,11... | collective-permute-start | bytes 4718600 | tf_op jit(solution)/shard_map/ppermute | solution.py:107
  323.3 19.8 %collective-permute-start.44 = (bf16[384,512]{1,0:T(8,128)(2,1)S(1)}, bf16[384,512]{1,0:T(8,128)(2,1)S(1)}, u32[]{:S(2)}, u32[]{:S(2)}) collective-permute-start(bf16[384,512]{1,0:T(8,128)(2,1)S(1)} %get-tuple-element.359), channel_id=1, source_target_pairs={{0,8},{1,9},{2,10},{3,11},{4,12},{5,13},{6,14},{7,15},{8,0},{9,1},... | collective-permute-start | bytes 1179656 | tf_op jit(solution)/shard_map/ppermute | solution.py:110
  329.7 23.9 %collective-permute-start.49 = (bf16[768,640]{1,0:T(8,128)(2,1)S(1)}, bf16[768,640]{1,0:T(8,128)(2,1)S(1)}, u32[]{:S(2)}, u32[]{:S(2)}) collective-permute-start(bf16[768,640]{1,0:T(8,128)(2,1)S(1)} %get-tuple-element.372), channel_id=1, source_target_pairs={{0,16},{1,17},{2,18},{3,19},{4,20},{5,21},{6,22},{7,23},{8,24},{9,... | collective-permute-start | bytes 2949128 | tf_op jit(solution)/shard_map/ppermute | solution.py:110
  343.1 40.3 %collective-permute-start.45 = (bf16[384,1024]{1,0:T(8,128)(2,1)S(1)}, bf16[384,1024]{1,0:T(8,128)(2,1)S(1)}, u32[]{:S(2)}, u32[]{:S(2)}) collective-permute-start(bf16[384,1024]{1,0:T(8,128)(2,1)S(1)} %get-tuple-element.361), channel_id=1, source_target_pairs={{0,8},{1,9},{2,10},{3,11},{4,12},{5,13},{6,14},{7,15},{8,0},{9,1},... | collective-permute-start | bytes 2359304 | tf_op jit(solution)/shard_map/ppermute | solution.py:110
  344.0 25.4 %collective-permute-start.46 = (bf16[128,1536]{1,0:T(8,128)(2,1)S(1)}, bf16[128,1536]{1,0:T(8,128)(2,1)S(1)}, u32[]{:S(2)}, u32[]{:S(2)}) collective-permute-start(bf16[128,1536]{1,0:T(8,128)(2,1)S(1)} %get-tuple-element.365), channel_id=1, source_target_pairs={{0,4},{1,5},{2,6},{3,7},{4,0},{5,1},{6,2},{7,3},{8,12},{9,13},{10,... | collective-permute-start | bytes 1179656 | tf_op jit(solution)/shard_map/ppermute | solution.py:107
  346.7 22.8 %collective-permute-start.47 = (bf16[128,1536]{1,0:T(8,128)(2,1)S(1)}, bf16[128,1536]{1,0:T(8,128)(2,1)S(1)}, u32[]{:S(2)}, u32[]{:S(2)}) collective-permute-start(bf16[128,1536]{1,0:T(8,128)(2,1)S(1)} %get-tuple-element.366), channel_id=1, source_target_pairs={{0,2},{1,3},{2,0},{3,1},{4,6},{5,7},{6,4},{7,5},{8,10},{9,11},{10,... | collective-permute-start | bytes 1179656 | tf_op jit(solution)/shard_map/ppermute | solution.py:107
  348.1 33.3 %collective-permute-start.48 = (bf16[128,1536]{1,0:T(8,128)(2,1)S(1)}, bf16[128,1536]{1,0:T(8,128)(2,1)S(1)}, u32[]{:S(2)}, u32[]{:S(2)}) collective-permute-start(bf16[128,1536]{1,0:T(8,128)(2,1)S(1)} %get-tuple-element.367), channel_id=1, source_target_pairs={{0,6},{1,7},{2,4},{3,5},{4,2},{5,3},{6,0},{7,1},{8,14},{9,15},{10,... | collective-permute-start | bytes 1179656 | tf_op jit(solution)/shard_map/ppermute | solution.py:107
  385.1 45.0 %all-to-all-start.2 = ((bf16[8,48,1536]{2,1,0:T(8,128)(2,1)}), bf16[8,48,1536]{2,1,0:T(8,128)(2,1)S(1)}, u32[]{:S(2)}, u32[]{:S(2)}) async-start(bf16[8,48,1536]{2,1,0:T(8,128)(2,1)} %bitcast.17), calls=%async_computation.2 | async-start | bytes 2359296 | tf_op jit(solution)/shard_map/all_to_all | solution.py:126
  388.7 24.2 %collective-permute-start.50 = (bf16[384,640]{1,0:T(8,128)(2,1)S(1)}, bf16[384,640]{1,0:T(8,128)(2,1)S(1)}, u32[]{:S(2)}, u32[]{:S(2)}) collective-permute-start(bf16[384,640]{1,0:T(8,128)(2,1)S(1)} %get-tuple-element.383), channel_id=1, source_target_pairs={{0,8},{1,9},{2,10},{3,11},{4,12},{5,13},{6,14},{7,15},{8,0},{9,1},... | collective-permute-start | bytes 1474568 | tf_op jit(solution)/shard_map/ppermute | solution.py:110
  (77 other events, 1051.0 us)
